TPU v7x, 256 devices: a whole 4x4x8 slice. The times are simulated.
256 devices in a mesh: pipe: 64 (over z_lo, x, y), tp: 4 (over z_hi, core).
Axes of the slice: x: 4, y: 4, z: 8 (z_hi: 2, z_lo: 4; z = z_hi * 4 + z_lo), core: 2. Of those that a mesh axis runs over, the one named last changes fastest.
Arguments:
- hidden_stash: bfloat16 [64, 512, 8192], P('pipe', None, 'tp'), may hold values from -6 to 6
- key_stash: bfloat16 [64, 512, 512], P('pipe', None, 'tp'), may hold values from -6 to 6
- value_stash: bfloat16 [64, 512, 512], P('pipe', None, 'tp'), may hold values from -4 to 4
- top_grads: bfloat16 [512, 8192], P(None, 'tp'), may hold values from -1400 to 1400
- response_lengths: int32 [4], replicated, may hold values from 1 to 64, 192 in all
Outputs:
- kv_grads: float32 [64, 512, 1024], P('pipe', None, 'tp')
Inputs may be any that keep to these rules, and one draw needn't show every extreme that they name: `response_lengths`: one response has exactly 64 live tokens; the lengths sum to 192.
All inputs are finite; a program needn't handle non-finite values.
Results may differ from a plain program's by a relative error of at most 0.012.
The roundings to bfloat16 on the way count: a program that leaves them out, or rounds other values in their place, can miss the bound.
Values may be sent and summed in bfloat16 or wider, within the bound.
No kernel may reach another device: no remote copies, remote signals or barrier semaphores. Data moves between devices by JAX's collectives and lax.ppermute only.
A program may use at most 64 MiB of HBM per device.

v0:
```python
import math

import jax
import jax.numpy as jnp
from jax import lax
from jax.sharding import PartitionSpec as P

HD = 128
PROMPT = 256
NRESP = 4
RLEN = 64


clip_rms = 0.5


def shifted(array, axis, by):
    peers = lax.axis_size(axis)
    pairs = [(i, i + by) for i in range(peers) if 0 <= i + by < peers]
    return lax.ppermute(array, axis, pairs)


def live_rows(response_lengths, total_rows):
    positions = jnp.arange(total_rows, dtype=jnp.int32)
    response_slot = jnp.clip((positions - PROMPT) // RLEN, 0, NRESP - 1)
    offset_in = positions - PROMPT - response_slot * RLEN
    return (positions < PROMPT) | (offset_in < response_lengths[response_slot])


def visible_pairs(query_rows, live_flags):
    positions = jnp.arange(live_flags.shape[0], dtype=jnp.int32)
    query_col = query_rows[:, None]
    key_row = positions[None, :]
    causal_ok = key_row <= query_col
    in_prompt = key_row < PROMPT
    prompt_part = in_prompt & ((query_col >= PROMPT) | causal_ok)
    same_slot = (query_col - PROMPT) // RLEN == (key_row - PROMPT) // RLEN
    reply_part = ~in_prompt & (query_col >= PROMPT) & same_slot & causal_ok
    return live_flags[None, :] & (prompt_part | reply_part)


def piece_backward(query_bf, key_bf, value_bf, grad_bf, visible_mask):
    head_dim = key_bf.shape[-1]
    score_scale = 1.0 / math.sqrt(head_dim)
    scores = (
        jnp.einsum("qgnd,kgd->gnqk", query_bf, key_bf, preferred_element_type=jnp.float32)
        * score_scale
    )
    scores = jnp.where(visible_mask[None, None], scores, -jnp.inf)
    row_max = jnp.max(scores, axis=-1, keepdims=True)
    weights = jnp.exp(scores - row_max)
    probability = weights / jnp.sum(weights, axis=-1, keepdims=True)
    probability_bf = probability.astype(jnp.bfloat16)
    attended = jnp.einsum(
        "gnqk,kgd->qgnd", probability_bf, value_bf, preferred_element_type=jnp.float32
    )
    row_delta = jnp.sum(grad_bf.astype(jnp.float32) * attended, axis=-1)
    dprobs = jnp.einsum("qgnd,kgd->gnqk", grad_bf, value_bf, preferred_element_type=jnp.float32)
    dscores_bf = (probability * (dprobs - jnp.transpose(row_delta, (1, 2, 0))[..., None])).astype(
        jnp.bfloat16
    )
    query_grad = (
        jnp.einsum("gnqk,kgd->qgnd", dscores_bf, key_bf, preferred_element_type=jnp.float32)
        * score_scale
    )
    key_grad = (
        jnp.einsum("gnqk,qgnd->kgd", dscores_bf, query_bf, preferred_element_type=jnp.float32)
        * score_scale
    )
    value_grad = jnp.einsum(
        "gnqk,qgnd->kgd", probability_bf, grad_bf, preferred_element_type=jnp.float32
    )
    return (query_grad, key_grad, value_grad)


def on_device(hidden_stash, key_stash, value_stash, top_grads, response_lengths):
    section_count = lax.axis_size("pipe")
    section_index = lax.axis_index("pipe")
    total_rows = hidden_stash.shape[1]
    local_width = hidden_stash.shape[2]
    kv_width = key_stash.shape[2]
    local_groups = kv_width // HD
    group_size = local_width // kv_width
    piece_rows = 64
    piece_count = total_rows // piece_rows
    live_flags = live_rows(response_lengths, total_rows)
    start_grad = jnp.where(live_flags[:, None], top_grads, jnp.zeros_like(top_grads))
    stash_local = hidden_stash[0]
    key_local = key_stash[0].reshape(total_rows, local_groups, HD)
    value_local = value_stash[0].reshape(total_rows, local_groups, HD)

    def compute_piece(first_row, grad_in, key_acc, value_acc):
        query_rows = first_row + jnp.arange(piece_rows, dtype=jnp.int32)
        visible_mask = visible_pairs(query_rows, live_flags)
        query_piece = lax.dynamic_slice_in_dim(stash_local, first_row, piece_rows, 0)
        query_piece = query_piece.reshape(piece_rows, local_groups, group_size, HD)
        grad_piece = grad_in.reshape(piece_rows, local_groups, group_size, HD)
        query_grad, key_grad, value_grad = piece_backward(
            query_piece, key_local, value_local, grad_piece, visible_mask
        )
        outgoing = (
            grad_in.astype(jnp.float32) + query_grad.reshape(piece_rows, local_width)
        ).astype(jnp.bfloat16)
        return (outgoing, key_acc + key_grad, value_acc + value_grad)

    def pass_through(first_row, grad_in, key_acc, value_acc):
        return (grad_in, key_acc, value_acc)

    def tick_step(tick_index, loop_state):
        incoming, key_acc, value_acc = loop_state
        item_index = tick_index - (section_count - 1 - section_index)
        active = (item_index >= 0) & (item_index < piece_count)
        order_index = jnp.clip(item_index, 0, piece_count - 1)
        first_row = (order_index + PROMPT // piece_rows) % piece_count * piece_rows
        from_top = lax.dynamic_slice_in_dim(start_grad, first_row, piece_rows, 0)
        grad_in = jnp.where(section_index == section_count - 1, from_top, incoming)
        outgoing, key_acc, value_acc = lax.cond(
            active, compute_piece, pass_through, first_row, grad_in, key_acc, value_acc
        )
        incoming = shifted(outgoing, "pipe", -1)
        return (incoming, key_acc, value_acc)

    initial = (
        jnp.zeros((piece_rows, local_width), jnp.bfloat16),
        jnp.zeros((total_rows, local_groups, HD), jnp.float32),
        jnp.zeros((total_rows, local_groups, HD), jnp.float32),
    )
    final_state = lax.fori_loop(0, piece_count + section_count - 1, tick_step, initial)
    key_total = final_state[1]
    value_total = final_state[2]
    paired = jnp.stack([key_total, value_total], axis=2).reshape(1, total_rows, 2 * kv_width)
    square_sum = lax.psum(jnp.sum(paired * paired), ("pipe", "tp"))
    entries = section_count * lax.axis_size("tp") * total_rows * 2 * kv_width
    clip_limit = clip_rms * math.sqrt(entries)
    factor = clip_limit / jnp.maximum(jnp.sqrt(square_sum), clip_limit)
    return paired * factor


def solution(mesh):
    placed = (
        P("pipe", None, "tp"),
        P("pipe", None, "tp"),
        P("pipe", None, "tp"),
        P(None, "tp"),
        P(),
    )
    return jax.shard_map(
        on_device, mesh=mesh, in_specs=placed, out_specs=P("pipe", None, "tp"), check_vma=False
    )
```

profile of v0, /device:TPU:1, one launch (start us, length us, event | category | flops | bytes accessed | tf_op | source)
XLA Modules:
  0.0 1560.9 jit_solution(2984994049444820776)
XLA Ops:
  7.4 1417.4 %while.20 = (s32[]{:T(128)}, bf16[64,2048]{1,0:T(8,128)(2,1)S(1)}, f32[512,1,128]{0,2,1:T(8,128)S(1)}, f32[512,1,128]{2,0,1:T(8,128)S(1)}, s32[]{:T(128)}, /*ind...) while((s32[]{:T(128)}, bf16[64,2048]{1,0:T(8,128)(2,1)S(1)}, ...), condition=%wide.region_6.7_spmd.clone, body=%wide.region_0.6_spmd.clone.sunk | while | flops 813697728 | bytes 30035968 | solution.py:128
  151.1 9.3 collective-permute-done
  165.4 10.7 collective-permute-done
  181.1 11.4 collective-permute-done
  197.5 10.6 collective-permute-done
  327.4 9.4 collective-permute-done
  341.8 10.8 collective-permute-done
  357.5 11.5 collective-permute-done
  373.9 10.5 collective-permute-done
  389.4 9.2 collective-permute-done
  467.2 16.4 %collective-permute-done = bf16[64,2048]{1,0:T(8,128)(2,1)S(1)} collective-permute-done((bf16[64,2048]{1,0:T(8,128)(2,1)S(1)}, bf16[64,2048]{1,0:T(8,128)(2,1)S(1)}, u32[]{:S(2)}, u32[]{:S(2)}) %collective-permute-start) | collective-permute-done | bytes 262176 | tf_op jit(solution)/shard_map/while/body/eval_jaxpr/ppermute | solution.py:20
  488.6 15.6 %collective-permute-done = bf16[64,2048]{1,0:T(8,128)(2,1)S(1)} collective-permute-done((bf16[64,2048]{1,0:T(8,128)(2,1)S(1)}, bf16[64,2048]{1,0:T(8,128)(2,1)S(1)}, u32[]{:S(2)}, u32[]{:S(2)}) %collective-permute-start) | collective-permute-done | bytes 262176 | tf_op jit(solution)/shard_map/while/body/eval_jaxpr/ppermute | solution.py:20
  509.2 10.1 collective-permute-done
  524.3 9.1 collective-permute-done
  538.3 10.8 collective-permute-done
  554.1 10.3 collective-permute-done
  569.4 9.1 collective-permute-done
  583.5 10.5 collective-permute-done
  599.0 10.3 collective-permute-done
  627.9 9.3 collective-permute-done
  642.2 10.5 collective-permute-done
  657.7 11.1 collective-permute-done
  673.8 13.0 collective-permute-done
  691.8 12.7 collective-permute-done
  709.5 12.1 collective-permute-done
  726.5 11.4 collective-permute-done
  742.9 9.0 collective-permute-done
  756.9 10.3 collective-permute-done
  772.2 10.9 collective-permute-done
  788.0 9.0 collective-permute-done
  802.1 10.0 collective-permute-done
  817.1 11.2 collective-permute-done
  833.2 9.1 collective-permute-done
  847.3 9.0 collective-permute-done
  861.3 9.5 collective-permute-done
  875.7 10.5 collective-permute-done
  891.3 11.7 collective-permute-done
  907.9 307.0 %collective-permute-done = bf16[64,2048]{1,0:T(8,128)(2,1)S(1)} collective-permute-done((bf16[64,2048]{1,0:T(8,128)(2,1)S(1)}, bf16[64,2048]{1,0:T(8,128)(2,1)S(1)}, u32[]{:S(2)}, u32[]{:S(2)}) %collective-permute-start) | collective-permute-done | bytes 262176 | tf_op jit(solution)/shard_map/while/body/eval_jaxpr/ppermute | solution.py:20
  1228.5 21.7 %collective-permute-done = bf16[64,2048]{1,0:T(8,128)(2,1)S(1)} collective-permute-done((bf16[64,2048]{1,0:T(8,128)(2,1)S(1)}, bf16[64,2048]{1,0:T(8,128)(2,1)S(1)}, u32[]{:S(2)}, u32[]{:S(2)}) %collective-permute-start) | collective-permute-done | bytes 262176 | tf_op jit(solution)/shard_map/while/body/eval_jaxpr/ppermute | solution.py:20
  1253.8 8.6 conditional.3
  1263.8 23.2 %collective-permute-done = bf16[64,2048]{1,0:T(8,128)(2,1)S(1)} collective-permute-done((bf16[64,2048]{1,0:T(8,128)(2,1)S(1)}, bf16[64,2048]{1,0:T(8,128)(2,1)S(1)}, u32[]{:S(2)}, u32[]{:S(2)}) %collective-permute-start) | collective-permute-done | bytes 262176 | tf_op jit(solution)/shard_map/while/body/eval_jaxpr/ppermute | solution.py:20
  1300.6 9.7 collective-permute-done
  1323.9 10.8 collective-permute-done
  1348.3 9.3 collective-permute-done
  1371.2 9.8 collective-permute-done
  1394.6 10.8 collective-permute-done
  1409.0 8.6 conditional.3
  1425.7 132.8 %psum.7 = f32[]{:T(128)} all-reduce(f32[]{:T(128)} %multiply_reduce_fusion), channel_id=1, replica_groups=mesh['pipe'=64,'tp'=4] {'pipe','tp'}, use_global_device_ids=true, to_apply=%region_8.9 | all-reduce | flops 1 | bytes 8 | tf_op jit(solution)/shard_map/psum | solution.py:132
  (912 shorter events, 684.3 us)
Async XLA Ops:
  22.6 9.9 collective-permute-start
  47.1 9.6 collective-permute-start
  149.8 10.6 collective-permute-start
  164.1 12.0 collective-permute-start
  179.8 12.7 collective-permute-start
  196.2 11.9 collective-permute-start
  326.1 10.7 collective-permute-start
  340.5 12.1 collective-permute-start
  356.2 12.8 collective-permute-start
  372.6 11.8 collective-permute-start
  388.1 10.5 collective-permute-start
  452.5 9.7 collective-permute-start
  465.9 17.7 %collective-permute-start = (bf16[64,2048]{1,0:T(8,128)(2,1)S(1)}, bf16[64,2048]{1,0:T(8,128)(2,1)S(1)}, u32[]{:S(2)}, u32[]{:S(2)}) collective-permute-start(bf16[64,2048]{1,0:T(8,128)(2,1)S(1)} %get-tuple-element.591), channel_id=1, source_target_pairs={{4,0},{8,4},{12,8},{16,12},{20,16},{24,20},{28,24},{32,28},{36,32}... | collective-permute-start | bytes 786440 | tf_op jit(solution)/shard_map/while/body/eval_jaxpr/ppermute | solution.py:20
  487.3 16.9 %collective-permute-start = (bf16[64,2048]{1,0:T(8,128)(2,1)S(1)}, bf16[64,2048]{1,0:T(8,128)(2,1)S(1)}, u32[]{:S(2)}, u32[]{:S(2)}) collective-permute-start(bf16[64,2048]{1,0:T(8,128)(2,1)S(1)} %get-tuple-element.591), channel_id=1, source_target_pairs={{4,0},{8,4},{12,8},{16,12},{20,16},{24,20},{28,24},{32,28},{36,32}... | collective-permute-start | bytes 786440 | tf_op jit(solution)/shard_map/while/body/eval_jaxpr/ppermute | solution.py:20
  507.9 11.4 collective-permute-start
  523.0 10.4 collective-permute-start
  537.0 12.1 collective-permute-start
  552.8 11.6 collective-permute-start
  568.1 10.4 collective-permute-start
  582.2 11.8 collective-permute-start
  597.7 11.6 collective-permute-start
  613.0 9.9 collective-permute-start
  626.6 10.6 collective-permute-start
  640.9 11.9 collective-permute-start
  656.4 12.4 collective-permute-start
  672.5 14.3 collective-permute-start
  690.5 14.0 collective-permute-start
  708.2 13.4 collective-permute-start
  725.2 12.7 collective-permute-start
  741.6 10.3 collective-permute-start
  755.6 11.6 collective-permute-start
  770.9 12.2 collective-permute-start
  786.7 10.3 collective-permute-start
  800.8 11.3 collective-permute-start
  815.7 12.5 collective-permute-start
  831.9 10.4 collective-permute-start
  846.0 10.3 collective-permute-start
  860.0 10.8 collective-permute-start
  874.4 11.8 collective-permute-start
  889.9 13.0 collective-permute-start
  906.6 308.3 %collective-permute-start = (bf16[64,2048]{1,0:T(8,128)(2,1)S(1)}, bf16[64,2048]{1,0:T(8,128)(2,1)S(1)}, u32[]{:S(2)}, u32[]{:S(2)}) collective-permute-start(bf16[64,2048]{1,0:T(8,128)(2,1)S(1)} %get-tuple-element.591), channel_id=1, source_target_pairs={{4,0},{8,4},{12,8},{16,12},{20,16},{24,20},{28,24},{32,28},{36,32}... | collective-permute-start | bytes 786440 | tf_op jit(solution)/shard_map/while/body/eval_jaxpr/ppermute | solution.py:20
  1227.2 23.0 %collective-permute-start = (bf16[64,2048]{1,0:T(8,128)(2,1)S(1)}, bf16[64,2048]{1,0:T(8,128)(2,1)S(1)}, u32[]{:S(2)}, u32[]{:S(2)}) collective-permute-start(bf16[64,2048]{1,0:T(8,128)(2,1)S(1)} %get-tuple-element.591), channel_id=1, source_target_pairs={{4,0},{8,4},{12,8},{16,12},{20,16},{24,20},{28,24},{32,28},{36,32}... | collective-permute-start | bytes 786440 | tf_op jit(solution)/shard_map/while/body/eval_jaxpr/ppermute | solution.py:20
  1262.5 24.5 %collective-permute-start = (bf16[64,2048]{1,0:T(8,128)(2,1)S(1)}, bf16[64,2048]{1,0:T(8,128)(2,1)S(1)}, u32[]{:S(2)}, u32[]{:S(2)}) collective-permute-start(bf16[64,2048]{1,0:T(8,128)(2,1)S(1)} %get-tuple-element.591), channel_id=1, source_target_pairs={{4,0},{8,4},{12,8},{16,12},{20,16},{24,20},{28,24},{32,28},{36,32}... | collective-permute-start | bytes 786440 | tf_op jit(solution)/shard_map/while/body/eval_jaxpr/ppermute | solution.py:20
  1299.3 11.0 collective-permute-start
  1322.6 12.1 collective-permute-start
  1347.0 10.6 collective-permute-start
  1369.9 11.1 collective-permute-start
  1393.3 12.1 collective-permute-start
  (57 other events, 255.8 us)
where the time goes:
time: 1570 us; the launch traced here: 1560 us
  waiting for transfers between devices  995 us (63%)
  other arithmetic  282 us (18%)
  blocking collectives  133 us (8%)
  starting transfers between devices  91.7 us (6%)
  matrix products  37.2 us (2%)
    ppermute x71, waiting for transfers between devices, shifted(): return lax.ppermute(array, axis, pairs)  995 us
    gather x72, other arithmetic, live_rows(): return (positions < PROMPT) | (offset_in < response_lengths[response_slot])  184 us
    psum x1, blocking collectives, on_device(): square_sum = lax.psum(jnp.sum(paired * paired), ('pipe', 'tp'))  133 us
    ppermute x71, starting transfers between devices, shifted(): return lax.ppermute(array, axis, pairs)  91.7 us
    select_n x71, other arithmetic, tick_step(): grad_in = jnp.where(section_index == section_count - 1, from_top, incoming)  72.6 us
  transfers between devices with their start and end apart: 71, of which 71 were waited for; matrix products, arithmetic and copies ran while one was open for 0% of the time, Pallas kernels for 0%

commit v1 on v0

v1 whole, which is shorter than its diff:
```python
import math

import jax
import jax.numpy as jnp
from jax import lax
from jax.experimental import pallas as pl
from jax.experimental.pallas import tpu as pltpu
from jax.sharding import Mesh, PartitionSpec as P

HD = 128
PROMPT = 256
NRESP = 4
RLEN = 64
RESP = 192
LIVE = PROMPT + RESP
STAGES = 4
SIDE = 4
PLANE = SIDE * SIDE

clip_rms = 0.5
SCALE = 1.0 / math.sqrt(HD)
EXP2_SCALE = SCALE * math.log2(math.e)
f32 = jnp.float32
bf16 = jnp.bfloat16


def dot(a, b):
    return lax.dot_general(a, b, (((1,), (0,)), ((), ())), preferred_element_type=f32)


def dot_nt(a, b):
    return lax.dot_general(a, b, (((1,), (1,)), ((), ())), preferred_element_type=f32)


def params():
    return pltpu.CompilerParams(vmem_limit_bytes=48 << 20)


def shape(dims, dtype=f32):
    return jax.ShapeDtypeStruct(dims, dtype)


def starts(lens):
    first = lens[0]
    second = first + lens[1]
    return first, second, second + lens[2]


def start_of(row, lens):
    one, two, three = starts(lens)
    return jnp.where(
        row >= three, three, jnp.where(row >= two, two, jnp.where(row >= one, one, 0))
    )


def prompt_bias(query_dim):
    q = lax.broadcasted_iota(jnp.int32, (PROMPT, PROMPT), query_dim)
    k = lax.broadcasted_iota(jnp.int32, (PROMPT, PROMPT), 1 - query_dim)
    return jnp.where(k <= q, 0.0, -jnp.inf).astype(f32)


def response_bias(lens, query_dim):
    q = lax.broadcasted_iota(jnp.int32, (RESP, RESP), query_dim)
    k = lax.broadcasted_iota(jnp.int32, (RESP, RESP), 1 - query_dim)
    return jnp.where((k <= q) & (k >= start_of(q, lens)), 0.0, -jnp.inf).astype(f32)


def chosen_rows(lens, row_dim):
    dims = (RESP, NRESP * RLEN) if row_dim == 0 else (NRESP * RLEN, RESP)
    row = lax.broadcasted_iota(jnp.int32, dims, row_dim)
    col = lax.broadcasted_iota(jnp.int32, dims, 1 - row_dim)
    one, two, three = starts(lens)
    slot = (
        (row >= one).astype(jnp.int32)
        + (row >= two).astype(jnp.int32)
        + (row >= three).astype(jnp.int32)
    )
    return jnp.where(col == slot * RLEN + row - start_of(row, lens), 1.0, 0.0).astype(bf16)


def pack_kernel(lens, place, x_ref, top_ref, key_ref, value_ref, xp_out, xr_out, tp_out, tr_out, k_out, v_out):
    chosen = chosen_rows(lens, 0)
    for h in range(x_ref.shape[1] // HD):
        cols = slice(h * HD, (h + 1) * HD)
        xp_out[h] = x_ref[:PROMPT, cols]
        xr_out[h] = dot(chosen, x_ref[PROMPT:, cols]).astype(bf16)
    tp_out[...] = top_ref[:PROMPT]
    tr_out[...] = dot(chosen, top_ref[PROMPT:]).astype(bf16)
    for ref, out in ((key_ref, k_out), (value_ref, v_out)):
        out[:PROMPT] = ref[:PROMPT]
        out[PROMPT:] = dot(chosen, ref[PROMPT:]).astype(bf16)


def pack(lens, place, x, top, key, value):
    rows, width = x.shape
    heads = width // HD
    whole = lambda *dims: pl.BlockSpec(dims, lambda i, l, p: (0,) * len(dims))
    return pl.pallas_call(
        pack_kernel,
        name="pack",
        grid_spec=pltpu.PrefetchScalarGridSpec(
            num_scalar_prefetch=2,
            grid=(1,),
            in_specs=[
                whole(rows, width),
                pl.BlockSpec((rows, HD), lambda i, l, p: (0, p[0])),
                whole(rows, HD),
                whole(rows, HD),
            ],
            out_specs=[
                whole(heads, PROMPT, HD),
                whole(heads, RESP, HD),
                whole(PROMPT, HD),
                whole(RESP, HD),
                whole(LIVE, HD),
                whole(LIVE, HD),
            ],
        ),
        out_shape=[
            shape((heads, PROMPT, HD), bf16),
            shape((heads, RESP, HD), bf16),
            shape((PROMPT, HD), bf16),
            shape((RESP, HD), bf16),
            shape((LIVE, HD), bf16),
            shape((LIVE, HD), bf16),
        ],
        compiler_params=params(),
    )(lens, place, x, top, key, value)


def prompt_prob_kernel(lens, ks, vs, q_ref, k_ref, v_ref, prob_ref, att_ref, bias):
    @pl.when(pl.program_id(0) == 0)
    def _():
        bias[...] = prompt_bias(0)

    s = dot_nt(q_ref[0], k_ref[0]) + bias[...]
    m = jnp.max(s, -1, keepdims=True)
    w = jnp.exp2((s - m) * EXP2_SCALE)
    p = w * (1.0 / jnp.sum(w, -1, keepdims=True))
    prob_ref[0] = p
    att_ref[0] = dot(p.astype(bf16), v_ref[0])


def prompt_prob(lens, ks, vs, q, k, v):
    n = q.shape[0]
    block = lambda *dims: pl.BlockSpec((1,) + dims, lambda l, a, b, c: (l, 0, 0))
    return pl.pallas_call(
        prompt_prob_kernel,
        name="prompt_prob",
        grid_spec=pltpu.PrefetchScalarGridSpec(
            num_scalar_prefetch=3,
            grid=(n,),
            in_specs=[
                block(PROMPT, HD),
                pl.BlockSpec((1, PROMPT, HD), lambda l, a, b, c: (b[l], 0, 0)),
                pl.BlockSpec((1, PROMPT, HD), lambda l, a, b, c: (c[l], 0, 0)),
            ],
            out_specs=[block(PROMPT, PROMPT), block(PROMPT, HD)],
            scratch_shapes=[pltpu.VMEM((PROMPT, PROMPT), f32)],
        ),
        out_shape=[shape((n, PROMPT, PROMPT)), shape((n, PROMPT, HD))],
        compiler_params=params(),
    )(lens, ks, vs, q, k, v)


def response_prob_kernel(lens, ks, vs, q_ref, k_ref, v_ref, first_ref, own_ref, att_ref, bias):
    @pl.when(pl.program_id(0) == 0)
    def _():
        bias[...] = response_bias(lens, 0)

    q = q_ref[0]
    k = k_ref[0]
    v = v_ref[0]
    s1 = dot_nt(q, k[:PROMPT])
    s2 = dot_nt(q, k[PROMPT:]) + bias[...]
    m = jnp.maximum(jnp.max(s1, -1, keepdims=True), jnp.max(s2, -1, keepdims=True))
    w1 = jnp.exp2((s1 - m) * EXP2_SCALE)
    w2 = jnp.exp2((s2 - m) * EXP2_SCALE)
    r = 1.0 / (jnp.sum(w1, -1, keepdims=True) + jnp.sum(w2, -1, keepdims=True))
    p1 = w1 * r
    p2 = w2 * r
    first_ref[0] = p1
    own_ref[0] = p2
    att_ref[0] = dot(p1.astype(bf16), v[:PROMPT]) + dot(p2.astype(bf16), v[PROMPT:])


def response_prob(lens, ks, vs, q, k, v):
    n = q.shape[0]
    block = lambda *dims: pl.BlockSpec((1,) + dims, lambda l, a, b, c: (l, 0, 0))
    return pl.pallas_call(
        response_prob_kernel,
        name="response_prob",
        grid_spec=pltpu.PrefetchScalarGridSpec(
            num_scalar_prefetch=3,
            grid=(n,),
            in_specs=[
                block(RESP, HD),
                pl.BlockSpec((1, LIVE, HD), lambda l, a, b, c: (b[l], 0, 0)),
                pl.BlockSpec((1, LIVE, HD), lambda l, a, b, c: (c[l], 0, 0)),
            ],
            out_specs=[block(RESP, PROMPT), block(RESP, RESP), block(RESP, HD)],
            scratch_shapes=[pltpu.VMEM((RESP, RESP), f32)],
        ),
        out_shape=[shape((n, RESP, PROMPT)), shape((n, RESP, RESP)), shape((n, RESP, HD))],
        compiler_params=params(),
    )(lens, ks, vs, q, k, v)


def prompt_chain_kernel(ks, vs, g_ref, prob_ref, att_ref, k_ref, v_ref, stash_ref, out_ref):
    @pl.when(pl.program_id(0) == 0)
    def _():
        out_ref[...] = g_ref[...]

    d = out_ref[...]
    stash_ref[0] = d
    wide = d.astype(f32)
    delta = jnp.sum(wide * att_ref[0], -1, keepdims=True)
    ds = (prob_ref[0] * (dot_nt(d, v_ref[0]) - delta)).astype(bf16)
    out_ref[...] = (wide + dot(ds, k_ref[0]) * SCALE).astype(bf16)


def response_chain_kernel(ks, vs, g_ref, first_ref, own_ref, att_ref, k_ref, v_ref, stash_ref, out_ref):
    @pl.when(pl.program_id(0) == 0)
    def _():
        out_ref[...] = g_ref[...]

    d = out_ref[...]
    stash_ref[0] = d
    wide = d.astype(f32)
    k = k_ref[0]
    v = v_ref[0]
    delta = jnp.sum(wide * att_ref[0], -1, keepdims=True)
    ds1 = (first_ref[0] * (dot_nt(d, v[:PROMPT]) - delta)).astype(bf16)
    ds2 = (own_ref[0] * (dot_nt(d, v[PROMPT:]) - delta)).astype(bf16)
    step = dot(ds1, k[:PROMPT]) + dot(ds2, k[PROMPT:])
    out_ref[...] = (wide + step * SCALE).astype(bf16)


def chain(kernel, name, ks, vs, g, probs, k, v):
    n = probs[0].shape[0]
    rows = g.shape[0]
    keys = probs[0].shape[2] if len(probs) == 2 else LIVE
    block = lambda *dims: pl.BlockSpec((1,) + dims, lambda i, a, b: (n - 1 - i, 0, 0))
    whole = pl.BlockSpec((rows, HD), lambda i, a, b: (0, 0))
    return pl.pallas_call(
        kernel,
        name=name,
        grid_spec=pltpu.PrefetchScalarGridSpec(
            num_scalar_prefetch=2,
            grid=(n,),
            in_specs=[whole]
            + [block(*p.shape[1:]) for p in probs]
            + [
                pl.BlockSpec((1, keys, HD), lambda i, a, b: (a[n - 1 - i], 0, 0)),
                pl.BlockSpec((1, keys, HD), lambda i, a, b: (b[n - 1 - i], 0, 0)),
            ],
            out_specs=[block(rows, HD), whole],
        ),
        out_shape=[shape((n, rows, HD), bf16), shape((rows, HD), bf16)],
        compiler_params=params(),
    )(ks, vs, g, *probs, k, v)


def kv_grad_kernel(lens, qp_ref, qr_ref, gp_ref, gr_ref, k_ref, v_ref, out_ref, sum_ref, bias_p, bias_r, acc):
    h = pl.program_id(0)

    @pl.when(h == 0)
    def _():
        bias_p[...] = prompt_bias(1)
        bias_r[...] = response_bias(lens, 1)
        acc[...] = jnp.zeros_like(acc)

    qp, qr, gp, gr = qp_ref[0], qr_ref[0], gp_ref[0], gr_ref[0]
    k1, k2 = k_ref[:PROMPT], k_ref[PROMPT:]
    v1, v2 = v_ref[:PROMPT], v_ref[PROMPT:]
    s = dot_nt(k1, qp) + bias_p[...]
    dp = dot_nt(v1, gp)
    w = jnp.exp2((s - jnp.max(s, 0, keepdims=True)) * EXP2_SCALE)
    p = w * (1.0 / jnp.sum(w, 0, keepdims=True))
    pb = p.astype(bf16)
    delta = jnp.sum(pb.astype(f32) * dp, 0, keepdims=True)
    ds = (p * (dp - delta)).astype(bf16)
    s1 = dot_nt(k1, qr)
    s2 = dot_nt(k2, qr) + bias_r[...]
    dp1 = dot_nt(v1, gr)
    dp2 = dot_nt(v2, gr)
    m = jnp.maximum(jnp.max(s1, 0, keepdims=True), jnp.max(s2, 0, keepdims=True))
    w1 = jnp.exp2((s1 - m) * EXP2_SCALE)
    w2 = jnp.exp2((s2 - m) * EXP2_SCALE)
    r = 1.0 / (jnp.sum(w1, 0, keepdims=True) + jnp.sum(w2, 0, keepdims=True))
    p1 = w1 * r
    p2 = w2 * r
    pb1 = p1.astype(bf16)
    pb2 = p2.astype(bf16)
    delta = jnp.sum(pb1.astype(f32) * dp1, 0, keepdims=True) + jnp.sum(
        pb2.astype(f32) * dp2, 0, keepdims=True
    )
    ds1 = (p1 * (dp1 - delta)).astype(bf16)
    ds2 = (p2 * (dp2 - delta)).astype(bf16)
    acc[:PROMPT, :HD] += (dot(ds, qp) + dot(ds1, qr)) * SCALE
    acc[PROMPT:, :HD] += dot(ds2, qr) * SCALE
    acc[:PROMPT, HD:] += dot(pb, gp) + dot(pb1, gr)
    acc[PROMPT:, HD:] += dot(pb2, gr)

    @pl.when(h == pl.num_programs(0) - 1)
    def _():
        total = acc[...]
        squares = jnp.sum(total * total, 0, keepdims=True)
        sum_ref[...] = squares[:, :HD] + squares[:, HD:]
        out_ref[:PROMPT] = total[:PROMPT]
        spread = chosen_rows(lens, 1)
        left = total[PROMPT:]
        placed = jnp.zeros((NRESP * RLEN, 2 * HD), f32)
        for _ in range(3):
            term = left.astype(bf16)
            placed = placed + dot(spread, term)
            left = left - term.astype(f32)
        out_ref[PROMPT:] = placed


def kv_grad(lens, qp, qr, gp, gr, k, v):
    n = qp.shape[0]
    rows = PROMPT + NRESP * RLEN
    block = lambda *dims: pl.BlockSpec((1,) + dims, lambda i, a: (i, 0, 0))
    whole = lambda *dims: pl.BlockSpec(dims, lambda i, a: (0, 0))
    return pl.pallas_call(
        kv_grad_kernel,
        name="kv_grad",
        grid_spec=pltpu.PrefetchScalarGridSpec(
            num_scalar_prefetch=1,
            grid=(n,),
            in_specs=[
                block(PROMPT, HD),
                block(RESP, HD),
                block(PROMPT, HD),
                block(RESP, HD),
                whole(LIVE, HD),
                whole(LIVE, HD),
            ],
            out_specs=[whole(rows, 2 * HD), whole(1, HD)],
            scratch_shapes=[
                pltpu.VMEM((PROMPT, PROMPT), f32),
                pltpu.VMEM((RESP, RESP), f32),
                pltpu.VMEM((LIVE, 2 * HD), f32),
            ],
        ),
        out_shape=[shape((rows, 2 * HD)), shape((1, HD))],
        compiler_params=params(),
    )(lens, qp, qr, gp, gr, k, v)


def ring(step, size=SIDE):
    return [(i, (i + step) % size) for i in range(size)]


def gathered(block, axis):
    low = lax.ppermute(block, axis, ring(1))
    high = lax.ppermute(block, axis, ring(-1))
    half = block.shape[0] // 2
    far = jnp.concatenate(
        [
            lax.ppermute(low[:half], axis, ring(1)),
            lax.ppermute(high[half:], axis, ring(-1)),
        ]
    )
    return jnp.stack([block, low, high, far])


def slot_of(distance):
    distance = distance % SIDE
    return jnp.where(distance == 0, 0, jnp.where(distance == SIDE - 1, 1, distance + 1))


def on_device(hidden_stash, key_stash, value_stash, top_grads, lens):
    stage = lax.axis_index("zl")
    my_x = lax.axis_index("x")
    my_y = lax.axis_index("y")
    place = (my_x * SIDE + my_y).reshape(1).astype(jnp.int32)
    qp, qr, tp, tr, k, v = pack(
        lens, place, hidden_stash[0], top_grads, key_stash[0], value_stash[0]
    )
    layers = jnp.arange(PLANE, dtype=jnp.int32)
    slot_x = slot_of(layers // SIDE - my_x)
    slot_y = slot_of(layers % SIDE - my_y)
    ks = (slot_x * SIDE + slot_y).astype(jnp.int32)
    vs = (slot_y * SIDE + slot_x).astype(jnp.int32)
    all_k = gathered(gathered(k, "y"), "x").reshape(PLANE, LIVE, HD)
    all_v = gathered(gathered(v, "x"), "y").reshape(PLANE, LIVE, HD)
    plane = ("x", "y")
    my_qp = lax.all_to_all(qp, plane, 0, 0, tiled=True)
    my_qr = lax.all_to_all(qr, plane, 0, 0, tiled=True)
    prob_p = prompt_prob(lens, ks, vs, my_qp, all_k, all_v)
    prob_r = response_prob(lens, ks, vs, my_qr, all_k, all_v)
    gp, gr = tp, tr
    stash_p = jnp.zeros((PLANE, PROMPT, HD), bf16)
    stash_r = jnp.zeros((PLANE, RESP, HD), bf16)
    for now in range(STAGES - 1, -1, -1):
        mine = stage == now

        def run_p(g, stash):
            return tuple(chain(prompt_chain_kernel, "prompt_chain", ks, vs, g, prob_p, all_k, all_v))

        def run_r(g, stash):
            return tuple(chain(response_chain_kernel, "response_chain", ks, vs, g, prob_r, all_k, all_v))

        def idle(g, stash):
            return (stash, g)

        stash_p, gp = lax.cond(mine, run_p, idle, gp, stash_p)
        stash_r, gr = lax.cond(mine, run_r, idle, gr, stash_r)
        if now:
            gp = lax.ppermute(gp, "zl", [(now, now - 1)])
            gr = lax.ppermute(gr, "zl", [(now, now - 1)])
    own_gp = lax.all_to_all(stash_p, plane, 0, 0, tiled=True)
    own_gr = lax.all_to_all(stash_r, plane, 0, 0, tiled=True)
    raw, squares = kv_grad(lens, qp, qr, own_gp, own_gr, k, v)
    for axes, size in ((plane, PLANE), (("zl", "tp"), STAGES * lax.axis_size("tp"))):
        spread = jnp.broadcast_to(squares, (size, HD))
        squares = jnp.sum(lax.all_to_all(spread, axes, 0, 0, tiled=True), 0, keepdims=True)
    square_sum = jnp.sum(squares)
    entries = STAGES * PLANE * lax.axis_size("tp") * raw.shape[0] * raw.shape[1]
    clip_limit = clip_rms * math.sqrt(entries)
    factor = clip_limit / jnp.maximum(jnp.sqrt(square_sum), clip_limit)
    return (raw * factor)[None]


def solution(mesh):
    parts = mesh.devices.reshape(STAGES, SIDE, SIDE, -1)
    finer = Mesh(parts, ("zl", "x", "y", "tp"))
    pipe = ("zl", "x", "y")
    placed = (
        P(pipe, None, "tp"),
        P(pipe, None, "tp"),
        P(pipe, None, "tp"),
        P(None, "tp"),
        P(),
    )
    return jax.shard_map(
        on_device, mesh=finer, in_specs=placed, out_specs=P(pipe, None, "tp"), check_vma=False
    )
```

time: 1570 us -> 255 us (0.16)
  waiting for transfers between devices: 995 us -> 67 us
  other arithmetic: 282 us -> 7.64 us
  blocking collectives: 133 us -> 48.4 us
  Pallas kernels: 0 us -> 71.6 us
  starting transfers between devices: 91.7 us -> 47.3 us
  matrix products: 37.2 us -> 0 us
    ppermute x71 -> x22, waiting for transfers between devices: 995 us -> 67 us  [the longest x3 51.2 us: on_device(): gr = lax.ppermute(gr, 'zl', [(now, now - 1)])]
    gather x72 -> x0, other arithmetic: 184 us -> none  [live_rows(): return (positions < PROMPT) | (offset_in < response_lengths[response_slot])]
    psum x1 -> x0, blocking collectives: 133 us -> none  [on_device(): square_sum = lax.psum(jnp.sum(paired * paired), ('pipe', 'tp'))]
    select_n x88 -> x0, other arithmetic: 75.9 us -> none  [the longest x71 72.6 us: tick_step(): grad_in = jnp.where(section_index == section_count - 1, from_top, incoming)]
    pallas_call x0 -> x6, Pallas kernels: none -> 71.6 us  [the longest x2 26.9 us: chain(): pl.pallas_call(kernel, name=name, grid_spec=pltpu.PrefetchScalarGridSpec(...]
    ppermute x71 -> x22, starting transfers between devices: 91.7 us -> 32.8 us  [the longest x4 9.77 us: gathered(): high = lax.ppermute(block, axis, ring(-1))]
    all_to_all x0 -> x3, blocking collectives: none -> 48.4 us  [the longest x2 30.2 us: on_device(): lax.all_to_all(spread, axes, 0, 0, tiled=True)]
    dot_general x48 -> x0, matrix products: 37.2 us -> none  [the longest x8 11.2 us: piece_backward(): jnp.einsum('gnqk,kgd->qgnd', probability_bf, value_bf, preferred_element_...]
  transfers between devices with their start and end apart: 71 -> 25, of which waited for: 71 -> 4; matrix products, arithmetic and copies ran while one was open for 0% -> 5% of each run, Pallas kernels for 0% -> 20%
where the time goes in v1:
time: 255 us; the launch traced here: 253 us
  Pallas kernels  71.6 us (28%)
  waiting for transfers between devices  67 us (26%)
  blocking collectives  48.4 us (19%)
  starting transfers between devices  47.3 us (19%)
  local copies, waits for them, and re-layouts  9.63 us (4%)
  other arithmetic  7.64 us (3%)
    ppermute x3, waiting for transfers between devices, on_device(): gr = lax.ppermute(gr, 'zl', [(now, now - 1)])  51.2 us
    all_to_all x2, blocking collectives, on_device(): lax.all_to_all(spread, axes, 0, 0, tiled=True)  30.2 us
    pallas_call x2, Pallas kernels, chain(): pl.pallas_call(kernel, name=name, grid_spec=pltpu.PrefetchScalarGridSpec(...  26.9 us
    all_to_all x1, blocking collectives, on_device(): own_gp = lax.all_to_all(stash_p, plane, 0, 0, tiled=True)  18.2 us
    pallas_call x1, Pallas kernels, kv_grad(): pl.pallas_call(kv_grad_kernel, name='kv_grad', grid_spec=pltpu.PrefetchSc...  16.8 us
    pallas_call x1, Pallas kernels, prompt_prob(): pl.pallas_call(prompt_prob_kernel, name='prompt_prob', grid_spec=pltpu.Pr...  13.7 us
    pallas_call x1, Pallas kernels, response_prob(): pl.pallas_call(response_prob_kernel, name='response_prob', grid_spec=pltp...  10.9 us
    ppermute x4, starting transfers between devices, gathered(): high = lax.ppermute(block, axis, ring(-1))  9.77 us
  transfers between devices with their start and end apart: 25, of which 4 were waited for; matrix products, arithmetic and copies ran while one was open for 5% of the time, Pallas kernels for 20%

profile of v1, /device:TPU:1, one launch (start us, length us, event | category | flops | bytes accessed | tf_op | source)
XLA Modules:
  0.0 252.7 jit_solution(15156216635765797170)
XLA Ops:
  0.0 1.6 copy-done
  1.6 0.9 copy-done.1
  2.5 0.9 copy-done.2
  4.1 3.4 %pack.1 = (bf16[16,256,128]{2,1,0:T(8,128)(2,1)}, bf16[16,192,128]{2,1,0:T(8,128)(2,1)}, bf16[256,128]{1,0:T(8,128)(2,1)S(1)}, bf16[192,128]{1,0:T(8,128)(2,1)},...) custom-call(s32[4]{0:T(128)S(1)} %copy-done.3, s32[1]{0:T(128)} %bitcast.place, ...), custom_call_target="tpu_custom_call" | custom-call | tf_op jit(solution)/shard_map/pack/pallas_call | solution.py:98
  7.5 2.0 collective-permute-start.8
  9.5 1.3 collective-permute-start.9
  10.8 1.5 collective-permute-start
  12.3 1.4 collective-permute-start.1
  13.8 2.7 %collective-permute-start.11 = (bf16[224,128]{1,0:T(8,128)(2,1)S(1)}, bf16[224,128]{1,0:T(8,128)(2,1)S(1)}, u32[]{:S(2)}, u32[]{:S(2)}) collective-permute-start(bf16[224,128]{1,0:T(8,128)(2,1)S(1)} %slice.37), channel_id=1, source_target_pairs={{0,48},{16,0},{32,16},{48,32},{1,49},{17,1},{33,17},{49,33},{2,50}... | collective-permute-start | bytes 172040 | tf_op jit(solution)/shard_map/ppermute | solution.py:363
  16.6 4.1 %all-to-all-start.2 = ((bf16[16,192,128]{2,1,0:T(8,128)(2,1)}), bf16[16,192,128]{2,1,0:T(8,128)(2,1)S(1)}, u32[]{:S(2)}, u32[]{:S(2)}) async-start(bf16[16,192,128]{2,1,0:T(8,128)(2,1)} %get-tuple-element.253.qr_ref), calls=%async_computation.2 | async-start | bytes 1572864 | tf_op jit(solution)/shard_map/all_to_all | solution.py:391
  20.6 1.4 collective-permute-start.2
  22.1 1.4 collective-permute-start.3
  23.5 0.9 fusion.4
  24.5 2.5 collective-permute-start.13
  27.1 0.8 fusion.5
  27.9 3.0 %collective-permute-start.4 = (bf16[4,448,128]{2,1,0:T(8,128)(2,1)}, bf16[4,448,128]{2,1,0:T(8,128)(2,1)}, u32[]{:S(2)}, u32[]{:S(2)}) collective-permute-start(bf16[4,448,128]{2,1,0:T(8,128)(2,1)} %get-tuple-element.280), channel_id=1, source_target_pairs={{0,16},{16,32},{32,48},{48,0},{1,17},{17,33},{33,49},{49,1},{2,18}... | collective-permute-start | bytes 1376264 | tf_op jit(solution)/shard_map/ppermute | solution.py:357
  30.9 4.5 %collective-permute-start.5 = (bf16[4,448,128]{2,1,0:T(8,128)(2,1)}, bf16[4,448,128]{2,1,0:T(8,128)(2,1)}, u32[]{:S(2)}, u32[]{:S(2)}) collective-permute-start(bf16[4,448,128]{2,1,0:T(8,128)(2,1)} %get-tuple-element.280), channel_id=1, source_target_pairs={{0,48},{16,0},{32,16},{48,32},{1,49},{17,1},{33,17},{49,33},{2,50}... | collective-permute-start | bytes 1376264 | tf_op jit(solution)/shard_map/ppermute | solution.py:358
  35.5 5.1 %all-to-all-start = ((bf16[16,256,128]{2,1,0:T(8,128)(2,1)}), bf16[16,256,128]{2,1,0:T(8,128)(2,1)S(1)}, u32[]{:S(2)}, u32[]{:S(2)}) async-start(bf16[16,256,128]{2,1,0:T(8,128)(2,1)} %get-tuple-element.252.qp_ref), calls=%async_computation | async-start | bytes 2097152 | tf_op jit(solution)/shard_map/all_to_all | solution.py:390
  40.6 3.2 %collective-permute-done.12 = bf16[4,448,128]{2,1,0:T(8,128)(2,1)S(1)} collective-permute-done((bf16[4,448,128]{2,1,0:T(8,128)(2,1)}, bf16[4,448,128]{2,1,0:T(8,128)(2,1)S(1)}, u32[]{:S(2)}, u32[]{:S(2)}) %collective-permute-start.12) | collective-permute-done | bytes 458784 | tf_op jit(solution)/shard_map/ppermute | solution.py:357
  43.8 0.7 slice.38
  44.5 1.7 slice.39
  46.1 2.7 %collective-permute-start.15 = (bf16[2,448,128]{2,1,0:T(8,128)(2,1)}, bf16[2,448,128]{2,1,0:T(8,128)(2,1)}, u32[]{:S(2)}, u32[]{:S(2)}) collective-permute-start(bf16[2,448,128]{2,1,0:T(8,128)(2,1)} %slice.39), channel_id=1, source_target_pairs={{0,12},{4,0},{8,4},{12,8},{1,13},{5,1},{9,5},{13,9},{2,14},{6,2},{... | collective-permute-start | bytes 688136 | tf_op jit(solution)/shard_map/ppermute | solution.py:363
  48.8 1.0 slice.34
  50.3 1.0 slice.35
  51.2 2.4 collective-permute-start.7
  53.6 8.8 %collective-permute-done.14 = bf16[2,448,128]{2,1,0:T(8,128)(2,1)} collective-permute-done((bf16[2,448,128]{2,1,0:T(8,128)(2,1)}, bf16[2,448,128]{2,1,0:T(8,128)(2,1)}, u32[]{:S(2)}, u32[]{:S(2)}) %collective-permute-start.14) | collective-permute-done | bytes 229408 | tf_op jit(solution)/shard_map/ppermute | solution.py:362
  62.4 1.1 maximum_bitcast_fusion.1
  63.6 1.2 pad_maximum_fusion.1
  64.9 2.1 pad_maximum_fusion
  67.0 10.9 %response_prob.1 = (f32[16,192,256]{2,1,0:T(8,128)}, f32[16,192,192]{2,1,0:T(8,128)}, f32[16,192,128]{2,1,0:T(8,128)}) custom-call(s32[4]{0:T(128)S(1)} %copy-done.4, s32[16]{0:T(128)S(1)} %get-tuple-element.282.ks, s32[16]{0:T(128)S(1)} %get-tuple-element.281.vs, bf16[16,192,128]{2,1,0:T(8,128)(2,1)S(1)} %all-to-all-done.2.q_ref, ...), custom_call_target="tpu_custom_call" | custom-call | tf_op jit(solution)/shard_map/response_prob/pallas_call | solution.py:190
  77.8 1.1 conditional.12
  77.9 1.1 broadcast_in_dim.13
  80.3 1.3 collective-permute-start.21
  81.6 51.2 %collective-permute-done.21 = bf16[192,128]{1,0:T(8,128)(2,1)S(1)} collective-permute-done((bf16[192,128]{1,0:T(8,128)(2,1)S(1)}, bf16[192,128]{1,0:T(8,128)(2,1)S(1)}, u32[]{:S(2)}, u32[]{:S(2)}) %collective-permute-start.21) | collective-permute-done | bytes 49184 | tf_op jit(solution)/shard_map/ppermute | solution.py:413
  132.8 14.3 %conditional.15 = (bf16[16,192,128]{2,1,0:T(8,128)(2,1)}) conditional(s32[]{:T(128)} %convert_element_type.16, bf16[16,192,128]{2,1,0:T(8,128)(2,1)} %get-tuple-element.273, (s32[16]{0:T(128)S(1)}, s32[16]{0:T(128)S(1)}, bf16[192,128]{1,0:T(8,128)(2,1)S(1)}, f32[16,192,256]{2,1,0:T(8,128)}, f32[16,192,192]{2,1,0:T(8,128)}, ...), branch_computations={%region_14.15_spmd, %region_15.16_spmd} | conditional | bytes 8 | solution.py:410
  132.8 14.3 %response_chain.7 = (bf16[16,192,128]{2,1,0:T(8,128)(2,1)}, bf16[192,128]{1,0:T(8,128)(2,1)}) custom-call(s32[16]{0:T(128)S(1)} %get-tuple-element.218.ks, s32[16]{0:T(128)S(1)} %get-tuple-element.219.vs, bf16[192,128]{1,0:T(8,128)(2,1)S(1)} %get-tuple-element.220.g_ref, f32[16,192,256]{2,1,0:T(8,128)} %get-tuple-element.221.first_ref, ...), custom_call_target="tpu_custom_call" | custom-call | tf_op jit(solution)/shard_map/cond/branch_1_fun/response_chain/pallas_call | solution.py:245
  147.1 5.3 %all-to-all-start.3 = ((bf16[16,192,128]{2,1,0:T(8,128)(2,1)}), bf16[16,192,128]{2,1,0:T(8,128)(2,1)S(1)}, u32[]{:S(2)}, u32[]{:S(2)}) async-start(bf16[16,192,128]{2,1,0:T(8,128)(2,1)} %get-tuple-element.314), calls=%async_computation.3 | async-start | bytes 1572864 | tf_op jit(solution)/shard_map/all_to_all | solution.py:415
  152.4 13.7 %prompt_prob.1 = (f32[16,256,256]{2,1,0:T(8,128)}, f32[16,256,128]{2,1,0:T(8,128)}) custom-call(s32[4]{0:T(128)S(1)} %copy-done.4, s32[16]{0:T(128)S(1)} %get-tuple-element.282.ks, s32[16]{0:T(128)S(1)} %get-tuple-element.281.vs, bf16[16,256,128]{2,1,0:T(8,128)(2,1)S(1)} %all-to-all-done.q_ref, bf16[16,448,128]{2,1,0:T(8,128)(2,1)} %bitcast.54, ...), custom_call_target="tpu_custom_call" | custom-call | tf_op jit(solution)/shard_map/prompt_prob/pallas_call | solution.py:147
  166.3 0.7 collective-permute-start.16
  167.7 1.3 collective-permute-start.18
  169.0 3.7 %collective-permute-done.18 = bf16[256,128]{1,0:T(8,128)(2,1)S(1)} collective-permute-done((bf16[256,128]{1,0:T(8,128)(2,1)S(1)}, bf16[256,128]{1,0:T(8,128)(2,1)S(1)}, u32[]{:S(2)}, u32[]{:S(2)}) %collective-permute-start.18) | collective-permute-done | bytes 65568 | tf_op jit(solution)/shard_map/ppermute | solution.py:412
  172.7 12.7 %conditional.11 = (bf16[16,256,128]{2,1,0:T(8,128)(2,1)S(1)}) conditional(s32[]{:T(128)} %convert_element_type.16, bf16[16,256,128]{2,1,0:T(8,128)(2,1)S(1)} %get-tuple-element.263, (s32[16]{0:T(128)S(1)}, s32[16]{0:T(128)S(1)}, bf16[256,128]{1,0:T(8,128)(2,1)S(1)}, f32[16,256,256]{2,1,0:T(8,128)}, f32[16,256,128]{2,1,0:T(8,128)}, ...), branch_computations={%region_6.7_spmd, %region_7.8_spmd} | conditional | bytes 8 | solution.py:409
  172.7 12.7 %prompt_chain.7 = (bf16[16,256,128]{2,1,0:T(8,128)(2,1)S(1)}, bf16[256,128]{1,0:T(8,128)(2,1)}) custom-call(s32[16]{0:T(128)S(1)} %get-tuple-element.184.ks, s32[16]{0:T(128)S(1)} %get-tuple-element.185.vs, bf16[256,128]{1,0:T(8,128)(2,1)S(1)} %get-tuple-element.186.g_ref, f32[16,256,256]{2,1,0:T(8,128)} %get-tuple-element.187.prob_ref, ...), custom_call_target="tpu_custom_call" | custom-call | tf_op jit(solution)/shard_map/cond/branch_1_fun/prompt_chain/pallas_call | solution.py:245
  185.4 18.2 %all_to_all.32.gp_ref = bf16[16,256,128]{2,1,0:T(8,128)(2,1)S(1)} all-to-all(bf16[16,256,128]{2,1,0:T(8,128)(2,1)S(1)} %get-tuple-element.310), channel_id=1, replica_groups=mesh['zl'=4,'x'=4,'y'=4,'tp'=4] {'x','y'}, dimensions={0} | all-to-all | bytes 2097152 | tf_op jit(solution)/shard_map/all_to_all | solution.py:414
  203.6 16.8 %kv_grad.1 = (f32[512,256]{1,0:T(8,128)S(1)}, f32[1,128]{1,0:T(1,128)S(1)}) custom-call(s32[4]{0:T(128)S(1)} %copy-done.4, bf16[16,256,128]{2,1,0:T(8,128)(2,1)} %get-tuple-element.252.qp_ref, bf16[16,192,128]{2,1,0:T(8,128)(2,1)} %get-tuple-element.253.qr_ref, bf16[16,256,128]{2,1,0:T(8,128)(2,1)S(1)} %all_to_all.32.gp_ref, ...), custom_call_target="tpu_custom_call" | custom-call | tf_op jit(solution)/shard_map/kv_grad/pallas_call | solution.py:326
  220.4 9.7 %all_to_all.33 = f32[16,1,128]{2,1,0:T(1,128)S(1)} all-to-all(f32[16,1,128]{2,1,0:T(1,128)S(1)} %broadcast_in_dim.26), channel_id=1, replica_groups=mesh['zl'=4,'x'=4,'y'=4,'tp'=4] {'x','y'}, dimensions={0} | all-to-all | bytes 16384 | tf_op jit(solution)/shard_map/all_to_all | solution.py:419
  230.1 20.5 %all_to_all.34 = f32[16,1,128]{2,1,0:T(1,128)S(1)} all-to-all(f32[16,1,128]{2,1,0:T(1,128)S(1)} %broadcast_in_dim.27), channel_id=1, replica_groups=mesh['zl'=4,'x'=4,'y'=4,'tp'=4] {'zl','tp'}, dimensions={0} | all-to-all | bytes 16384 | tf_op jit(solution)/shard_map/all_to_all | solution.py:419
  251.9 0.8 multiply_bitcast_fusion
  (61 shorter events, 4.6 us)
Async XLA Ops:
  0.0 1.6 copy-start
  1.6 0.9 copy-start.1
  2.5 0.9 copy-start.2
  3.4 0.7 copy-start.3
  7.5 6.2 %collective-permute-start.8 = (bf16[448,128]{1,0:T(8,128)(2,1)S(1)}, bf16[448,128]{1,0:T(8,128)(2,1)S(1)}, u32[]{:S(2)}, u32[]{:S(2)}) collective-permute-start(bf16[448,128]{1,0:T(8,128)(2,1)S(1)} %get-tuple-element.256.v_ref), channel_id=1, source_target_pairs={{0,16},{16,32},{32,48},{48,0},{1,17},{17,33},{33,49},{49,1},{2,18}... | collective-permute-start | bytes 344072 | tf_op jit(solution)/shard_map/ppermute | solution.py:357
  9.5 4.3 %collective-permute-start.9 = (bf16[448,128]{1,0:T(8,128)(2,1)S(1)}, bf16[448,128]{1,0:T(8,128)(2,1)S(1)}, u32[]{:S(2)}, u32[]{:S(2)}) collective-permute-start(bf16[448,128]{1,0:T(8,128)(2,1)S(1)} %get-tuple-element.256.v_ref), channel_id=1, source_target_pairs={{0,48},{16,0},{32,16},{48,32},{1,49},{17,1},{33,17},{49,33},{2,50}... | collective-permute-start | bytes 344072 | tf_op jit(solution)/shard_map/ppermute | solution.py:358
  10.8 9.9 %collective-permute-start = (bf16[448,128]{1,0:T(8,128)(2,1)S(1)}, bf16[448,128]{1,0:T(8,128)(2,1)S(1)}, u32[]{:S(2)}, u32[]{:S(2)}) collective-permute-start(bf16[448,128]{1,0:T(8,128)(2,1)S(1)} %get-tuple-element.255.k_ref), channel_id=1, source_target_pairs={{0,4},{4,8},{8,12},{12,0},{1,5},{5,9},{9,13},{13,1},{2,6},{6,10},{... | collective-permute-start | bytes 344072 | tf_op jit(solution)/shard_map/ppermute | solution.py:357
  12.3 9.8 %collective-permute-start.1 = (bf16[448,128]{1,0:T(8,128)(2,1)S(1)}, bf16[448,128]{1,0:T(8,128)(2,1)S(1)}, u32[]{:S(2)}, u32[]{:S(2)}) collective-permute-start(bf16[448,128]{1,0:T(8,128)(2,1)S(1)} %get-tuple-element.255.k_ref), channel_id=1, source_target_pairs={{0,12},{4,0},{8,4},{12,8},{1,13},{5,1},{9,5},{13,9},{2,14},{6,2},{... | collective-permute-start | bytes 344072 | tf_op jit(solution)/shard_map/ppermute | solution.py:358
  13.7 9.8 %collective-permute-start.10 = (bf16[224,128]{1,0:T(8,128)(2,1)S(1)}, bf16[224,128]{1,0:T(8,128)(2,1)S(1)}, u32[]{:S(2)}, u32[]{:S(2)}) collective-permute-start(bf16[224,128]{1,0:T(8,128)(2,1)S(1)} %slice.36), channel_id=1, source_target_pairs={{0,16},{16,32},{32,48},{48,0},{1,17},{17,33},{33,49},{49,1},{2,18}... | collective-permute-start | bytes 172040 | tf_op jit(solution)/shard_map/ppermute | solution.py:362
  13.8 9.7 %collective-permute-start.11 = (bf16[224,128]{1,0:T(8,128)(2,1)S(1)}, bf16[224,128]{1,0:T(8,128)(2,1)S(1)}, u32[]{:S(2)}, u32[]{:S(2)}) collective-permute-start(bf16[224,128]{1,0:T(8,128)(2,1)S(1)} %slice.37), channel_id=1, source_target_pairs={{0,48},{16,0},{32,16},{48,32},{1,49},{17,1},{33,17},{49,33},{2,50}... | collective-permute-start | bytes 172040 | tf_op jit(solution)/shard_map/ppermute | solution.py:363
  16.6 18.9 %all-to-all-start.2 = ((bf16[16,192,128]{2,1,0:T(8,128)(2,1)}), bf16[16,192,128]{2,1,0:T(8,128)(2,1)S(1)}, u32[]{:S(2)}, u32[]{:S(2)}) async-start(bf16[16,192,128]{2,1,0:T(8,128)(2,1)} %get-tuple-element.253.qr_ref), calls=%async_computation.2 | async-start | bytes 1572864 | tf_op jit(solution)/shard_map/all_to_all | solution.py:391
  20.6 6.4 %collective-permute-start.2 = (bf16[224,128]{1,0:T(8,128)(2,1)S(1)}, bf16[224,128]{1,0:T(8,128)(2,1)S(1)}, u32[]{:S(2)}, u32[]{:S(2)}) collective-permute-start(bf16[224,128]{1,0:T(8,128)(2,1)S(1)} %slice.32), channel_id=1, source_target_pairs={{0,4},{4,8},{8,12},{12,0},{1,5},{5,9},{9,13},{13,1},{2,6},{6,10},{... | collective-permute-start | bytes 172040 | tf_op jit(solution)/shard_map/ppermute | solution.py:362
  22.1 5.0 %collective-permute-start.3 = (bf16[224,128]{1,0:T(8,128)(2,1)S(1)}, bf16[224,128]{1,0:T(8,128)(2,1)S(1)}, u32[]{:S(2)}, u32[]{:S(2)}) collective-permute-start(bf16[224,128]{1,0:T(8,128)(2,1)S(1)} %slice.33), channel_id=1, source_target_pairs={{0,12},{4,0},{8,4},{12,8},{1,13},{5,1},{9,5},{13,9},{2,14},{6,2},{... | collective-permute-start | bytes 172040 | tf_op jit(solution)/shard_map/ppermute | solution.py:363
  24.4 19.4 %collective-permute-start.12 = (bf16[4,448,128]{2,1,0:T(8,128)(2,1)}, bf16[4,448,128]{2,1,0:T(8,128)(2,1)S(1)}, u32[]{:S(2)}, u32[]{:S(2)}) collective-permute-start(bf16[4,448,128]{2,1,0:T(8,128)(2,1)} %get-tuple-element.278), channel_id=1, source_target_pairs={{0,4},{4,8},{8,12},{12,0},{1,5},{5,9},{9,13},{13,1},{2,6},{6,10},{... | collective-permute-start | bytes 1376264 | tf_op jit(solution)/shard_map/ppermute | solution.py:357
  24.5 19.9 %collective-permute-start.13 = (bf16[4,448,128]{2,1,0:T(8,128)(2,1)}, bf16[4,448,128]{2,1,0:T(8,128)(2,1)}, u32[]{:S(2)}, u32[]{:S(2)}) collective-permute-start(bf16[4,448,128]{2,1,0:T(8,128)(2,1)} %get-tuple-element.278), channel_id=1, source_target_pairs={{0,12},{4,0},{8,4},{12,8},{1,13},{5,1},{9,5},{13,9},{2,14},{6,2},{... | collective-permute-start | bytes 1376264 | tf_op jit(solution)/shard_map/ppermute | solution.py:358
  27.9 20.9 %collective-permute-start.4 = (bf16[4,448,128]{2,1,0:T(8,128)(2,1)}, bf16[4,448,128]{2,1,0:T(8,128)(2,1)}, u32[]{:S(2)}, u32[]{:S(2)}) collective-permute-start(bf16[4,448,128]{2,1,0:T(8,128)(2,1)} %get-tuple-element.280), channel_id=1, source_target_pairs={{0,16},{16,32},{32,48},{48,0},{1,17},{17,33},{33,49},{49,1},{2,18}... | collective-permute-start | bytes 1376264 | tf_op jit(solution)/shard_map/ppermute | solution.py:357
  30.9 19.3 %collective-permute-start.5 = (bf16[4,448,128]{2,1,0:T(8,128)(2,1)}, bf16[4,448,128]{2,1,0:T(8,128)(2,1)}, u32[]{:S(2)}, u32[]{:S(2)}) collective-permute-start(bf16[4,448,128]{2,1,0:T(8,128)(2,1)} %get-tuple-element.280), channel_id=1, source_target_pairs={{0,48},{16,0},{32,16},{48,32},{1,49},{17,1},{33,17},{49,33},{2,50}... | collective-permute-start | bytes 1376264 | tf_op jit(solution)/shard_map/ppermute | solution.py:358
  35.5 111.6 %all-to-all-start = ((bf16[16,256,128]{2,1,0:T(8,128)(2,1)}), bf16[16,256,128]{2,1,0:T(8,128)(2,1)S(1)}, u32[]{:S(2)}, u32[]{:S(2)}) async-start(bf16[16,256,128]{2,1,0:T(8,128)(2,1)} %get-tuple-element.252.qp_ref), calls=%async_computation | async-start | bytes 2097152 | tf_op jit(solution)/shard_map/all_to_all | solution.py:390
  44.5 17.9 %collective-permute-start.14 = (bf16[2,448,128]{2,1,0:T(8,128)(2,1)}, bf16[2,448,128]{2,1,0:T(8,128)(2,1)}, u32[]{:S(2)}, u32[]{:S(2)}) collective-permute-start(bf16[2,448,128]{2,1,0:T(8,128)(2,1)} %slice.38), channel_id=1, source_target_pairs={{0,4},{4,8},{8,12},{12,0},{1,5},{5,9},{9,13},{13,1},{2,6},{6,10},{... | collective-permute-start | bytes 688136 | tf_op jit(solution)/shard_map/ppermute | solution.py:362
  46.1 16.3 %collective-permute-start.15 = (bf16[2,448,128]{2,1,0:T(8,128)(2,1)}, bf16[2,448,128]{2,1,0:T(8,128)(2,1)}, u32[]{:S(2)}, u32[]{:S(2)}) collective-permute-start(bf16[2,448,128]{2,1,0:T(8,128)(2,1)} %slice.39), channel_id=1, source_target_pairs={{0,12},{4,0},{8,4},{12,8},{1,13},{5,1},{9,5},{13,9},{2,14},{6,2},{... | collective-permute-start | bytes 688136 | tf_op jit(solution)/shard_map/ppermute | solution.py:363
  49.8 13.7 %collective-permute-start.6 = (bf16[2,448,128]{2,1,0:T(8,128)(2,1)S(1)}, bf16[2,448,128]{2,1,0:T(8,128)(2,1)S(1)}, u32[]{:S(2)}, u32[]{:S(2)}) collective-permute-start(bf16[2,448,128]{2,1,0:T(8,128)(2,1)S(1)} %slice.34), channel_id=1, source_target_pairs={{0,16},{16,32},{32,48},{48,0},{1,17},{17,33},{33,49},{49,1},{2,18}... | collective-permute-start | bytes 688136 | tf_op jit(solution)/shard_map/ppermute | solution.py:362
  51.2 12.3 %collective-permute-start.7 = (bf16[2,448,128]{2,1,0:T(8,128)(2,1)S(1)}, bf16[2,448,128]{2,1,0:T(8,128)(2,1)S(1)}, u32[]{:S(2)}, u32[]{:S(2)}) collective-permute-start(bf16[2,448,128]{2,1,0:T(8,128)(2,1)S(1)} %slice.35), channel_id=1, source_target_pairs={{0,48},{16,0},{32,16},{48,32},{1,49},{17,1},{33,17},{49,33},{2,50}... | collective-permute-start | bytes 688136 | tf_op jit(solution)/shard_map/ppermute | solution.py:363
  64.8 13.0 %copy-start.5 = (bf16[4,4,448,128]{3,2,1,0:T(8,128)(2,1)}, bf16[4,4,448,128]{3,2,1,0:T(8,128)(2,1)S(1)}, u32[]{:S(2)}) copy-start(bf16[4,4,448,128]{3,2,1,0:T(8,128)(2,1)S(1)} %pad_maximum_fusion.1) | copy-start | bytes 5505028
  64.9 2.1 copy-start.4
  66.9 10.9 %copy-start.6 = (bf16[4,4,448,128]{3,2,1,0:T(8,128)(2,1)}, bf16[4,4,448,128]{3,2,1,0:T(8,128)(2,1)S(1)}, u32[]{:S(2)}) copy-start(bf16[4,4,448,128]{3,2,1,0:T(8,128)(2,1)S(1)} %pad_maximum_fusion) | copy-start | bytes 5505028
  66.9 10.9 %copy-start.7 = (bf16[192,128]{1,0:T(8,128)(2,1)S(1)}, bf16[192,128]{1,0:T(8,128)(2,1)}, u32[]{:S(2)}) copy-start(bf16[192,128]{1,0:T(8,128)(2,1)} %get-tuple-element.265) | copy-start | bytes 147460
  78.9 0.7 collective-permute-start.19
  79.6 0.7 collective-permute-start.20
  80.3 52.5 %collective-permute-start.21 = (bf16[192,128]{1,0:T(8,128)(2,1)S(1)}, bf16[192,128]{1,0:T(8,128)(2,1)S(1)}, u32[]{:S(2)}, u32[]{:S(2)}) collective-permute-start(bf16[192,128]{1,0:T(8,128)(2,1)S(1)} %get-tuple-element.274), channel_id=1, source_target_pairs={{64,0},{65,1},{66,2},{67,3},{68,4},{69,5},{70,6},{71,7},{72,8},{73... | collective-permute-start | bytes 147464 | tf_op jit(solution)/shard_map/ppermute | solution.py:413
  147.1 38.3 %all-to-all-start.3 = ((bf16[16,192,128]{2,1,0:T(8,128)(2,1)}), bf16[16,192,128]{2,1,0:T(8,128)(2,1)S(1)}, u32[]{:S(2)}, u32[]{:S(2)}) async-start(bf16[16,192,128]{2,1,0:T(8,128)(2,1)} %get-tuple-element.314), calls=%async_computation.3 | async-start | bytes 1572864 | tf_op jit(solution)/shard_map/all_to_all | solution.py:415
  166.3 0.7 collective-permute-start.16
  167.0 0.7 collective-permute-start.17
  167.7 5.0 %collective-permute-start.18 = (bf16[256,128]{1,0:T(8,128)(2,1)S(1)}, bf16[256,128]{1,0:T(8,128)(2,1)S(1)}, u32[]{:S(2)}, u32[]{:S(2)}) collective-permute-start(bf16[256,128]{1,0:T(8,128)(2,1)S(1)} %get-tuple-element.264), channel_id=1, source_target_pairs={{64,0},{65,1},{66,2},{67,3},{68,4},{69,5},{70,6},{71,7},{72,8},{73... | collective-permute-start | bytes 196616 | tf_op jit(solution)/shard_map/ppermute | solution.py:412

commit v2 on v1

v2 whole, which is shorter than its diff:
```python
import functools
import math

import jax
import jax.numpy as jnp
from jax import lax
from jax.experimental import pallas as pl
from jax.experimental.pallas import tpu as pltpu
from jax.sharding import Mesh, PartitionSpec as P

HD = 128
PROMPT = 256
NRESP = 4
RLEN = 64
RESP = 192
LIVE = PROMPT + RESP
STAGES = 4
SIDE = 4
PLANE = SIDE * SIDE

clip_rms = 0.5
SCALE = 1.0 / math.sqrt(HD)
EXP2_SCALE = SCALE * math.log2(math.e)
f32 = jnp.float32
bf16 = jnp.bfloat16


def dot(a, b):
    return lax.dot_general(a, b, (((1,), (0,)), ((), ())), preferred_element_type=f32)


def dot_nt(a, b):
    return lax.dot_general(a, b, (((1,), (1,)), ((), ())), preferred_element_type=f32)


def params():
    return pltpu.CompilerParams(vmem_limit_bytes=60 << 20)


def shape(dims, dtype=f32):
    return jax.ShapeDtypeStruct(dims, dtype)


def starts(lens):
    first = lens[0]
    second = first + lens[1]
    return first, second, second + lens[2]


def start_of(row, lens):
    one, two, three = starts(lens)
    return jnp.where(
        row >= three, three, jnp.where(row >= two, two, jnp.where(row >= one, one, 0))
    )


def prompt_bias(query_dim):
    q = lax.broadcasted_iota(jnp.int32, (PROMPT, PROMPT), query_dim)
    k = lax.broadcasted_iota(jnp.int32, (PROMPT, PROMPT), 1 - query_dim)
    return jnp.where(k <= q, 0.0, -jnp.inf).astype(f32)


def response_bias(lens, query_dim):
    q = lax.broadcasted_iota(jnp.int32, (RESP, RESP), query_dim)
    k = lax.broadcasted_iota(jnp.int32, (RESP, RESP), 1 - query_dim)
    return jnp.where((k <= q) & (k >= start_of(q, lens)), 0.0, -jnp.inf).astype(f32)


def chosen_rows(lens, row_dim):
    dims = (RESP, NRESP * RLEN) if row_dim == 0 else (NRESP * RLEN, RESP)
    row = lax.broadcasted_iota(jnp.int32, dims, row_dim)
    col = lax.broadcasted_iota(jnp.int32, dims, 1 - row_dim)
    one, two, three = starts(lens)
    slot = (
        (row >= one).astype(jnp.int32)
        + (row >= two).astype(jnp.int32)
        + (row >= three).astype(jnp.int32)
    )
    return jnp.where(col == slot * RLEN + row - start_of(row, lens), 1.0, 0.0).astype(bf16)


def pack_kernel(lens, place, x_ref, top_ref, key_ref, value_ref, xp_out, xr_out, tp_out, tr_out, k_out, v_out):
    chosen = chosen_rows(lens, 0)
    for h in range(x_ref.shape[1] // HD):
        cols = slice(h * HD, (h + 1) * HD)
        xp_out[h] = x_ref[:PROMPT, cols]
        xr_out[h] = dot(chosen, x_ref[PROMPT:, cols]).astype(bf16)

    @pl.when(pl.program_id(0) == 0)
    def _():
        tp_out[...] = top_ref[:PROMPT]
        tr_out[...] = dot(chosen, top_ref[PROMPT:]).astype(bf16)
        for ref, out in ((key_ref, k_out), (value_ref, v_out)):
            out[:PROMPT] = ref[:PROMPT]
            out[PROMPT:] = dot(chosen, ref[PROMPT:]).astype(bf16)


def pack(lens, place, x, top, key, value):
    rows, width = x.shape
    heads = width // HD
    steps = 4
    some = heads // steps
    whole = lambda *dims: pl.BlockSpec(dims, lambda i, l, p: (0,) * len(dims))
    return pl.pallas_call(
        pack_kernel,
        name="pack",
        grid_spec=pltpu.PrefetchScalarGridSpec(
            num_scalar_prefetch=2,
            grid=(steps,),
            in_specs=[
                pl.BlockSpec((rows, some * HD), lambda i, l, p: (0, i)),
                pl.BlockSpec((rows, HD), lambda i, l, p: (0, p[0])),
                whole(rows, HD),
                whole(rows, HD),
            ],
            out_specs=[
                pl.BlockSpec((some, PROMPT, HD), lambda i, l, p: (i, 0, 0)),
                pl.BlockSpec((some, RESP, HD), lambda i, l, p: (i, 0, 0)),
                whole(PROMPT, HD),
                whole(RESP, HD),
                whole(LIVE, HD),
                whole(LIVE, HD),
            ],
        ),
        out_shape=[
            shape((heads, PROMPT, HD), bf16),
            shape((heads, RESP, HD), bf16),
            shape((PROMPT, HD), bf16),
            shape((RESP, HD), bf16),
            shape((LIVE, HD), bf16),
            shape((LIVE, HD), bf16),
        ],
        compiler_params=params(),
    )(lens, place, x, top, key, value)


def softmax(scores, dim):
    top = functools.reduce(jnp.maximum, [jnp.max(x, dim, keepdims=True) for x in scores])
    weights = [jnp.exp2((x - top) * EXP2_SCALE) for x in scores]
    total = functools.reduce(jnp.add, [jnp.sum(w, dim, keepdims=True) for w in weights])
    share = 1.0 / total
    return [w * share for w in weights]


AT_ONCE = 4
PROMPT_ROW = PROMPT + HD
RESP_ROW = 2 * PROMPT + HD


def prob_kernel(prompt, lens, ks, vs, q_ref, *refs):
    k_refs, v_refs = refs[:AT_ONCE], refs[AT_ONCE : 2 * AT_ONCE]
    out, bias = refs[2 * AT_ONCE :]

    @pl.when(pl.program_id(0) == 0)
    def _():
        bias[...] = prompt_bias(0) if prompt else response_bias(lens, 0)

    for u in range(AT_ONCE):
        q, k, v = q_ref[u], k_refs[u][0], v_refs[u][0]
        if prompt:
            (p,) = softmax([dot_nt(q, k) + bias[...]], -1)
            out[u, :, :PROMPT] = p
            out[u, :, PROMPT:] = dot(p.astype(bf16), v)
        else:
            p1, p2 = softmax([dot_nt(q, k[:PROMPT]), dot_nt(q, k[PROMPT:]) + bias[...]], -1)
            out[u, :, :PROMPT] = p1
            out[u, :, PROMPT:LIVE] = p2
            out[u, :, 2 * PROMPT :] = dot(p1.astype(bf16), v[:PROMPT]) + dot(
                p2.astype(bf16), v[PROMPT:]
            )


def prob(prompt, lens, ks, vs, q, k, v):
    n, rows, _ = q.shape
    keys, width = (PROMPT, PROMPT_ROW) if prompt else (LIVE, RESP_ROW)
    slot = lambda which, u: pl.BlockSpec(
        (1, keys, HD), lambda i, *tables: (tables[which][i * AT_ONCE + u], 0, 0)
    )
    block = lambda w: pl.BlockSpec((AT_ONCE, rows, w), lambda i, *tables: (i, 0, 0))
    return pl.pallas_call(
        functools.partial(prob_kernel, prompt),
        name="prompt_prob" if prompt else "response_prob",
        grid_spec=pltpu.PrefetchScalarGridSpec(
            num_scalar_prefetch=3,
            grid=(n // AT_ONCE,),
            in_specs=[block(HD)]
            + [slot(1, u) for u in range(AT_ONCE)]
            + [slot(2, u) for u in range(AT_ONCE)],
            out_specs=block(width),
            scratch_shapes=[pltpu.VMEM((rows, rows), f32)],
        ),
        out_shape=shape((n, rows, width)),
        compiler_params=params(),
    )(lens, ks, vs, q, *([k] * AT_ONCE), *([v] * AT_ONCE))


AHEAD = 3


def chain_kernel(prompt, n, active, ks, vs, g_in, stash_in, prob_hbm, k_hbm, v_hbm, g_out, stash, probs, keys, values, grads, last, sems, out_sems, g_sem):
    count = keys.shape[1]

    def loads(i):
        layer = n - 1 - i
        return (
            pltpu.make_async_copy(prob_hbm.at[layer], probs.at[layer], sems.at[layer, 0]),
            pltpu.make_async_copy(k_hbm.at[ks[layer], :count], keys.at[layer], sems.at[layer, 1]),
            pltpu.make_async_copy(v_hbm.at[vs[layer], :count], values.at[layer], sems.at[layer, 2]),
        )

    def save(layer):
        return pltpu.make_async_copy(grads.at[layer], stash.at[layer], out_sems.at[layer])

    def step(i, final):
        layer = n - 1 - i
        if not final:

            @pl.when(i + AHEAD < n)
            def _():
                for copy in loads(i + AHEAD):
                    copy.start()

        for copy in loads(i):
            copy.wait()
        save(layer).start()
        d = grads[layer]
        wide = d.astype(f32)
        k, v = keys[layer], values[layer]
        if prompt:
            delta = jnp.sum(wide * probs[layer, :, PROMPT:], -1, keepdims=True)
            ds = (probs[layer, :, :PROMPT] * (dot_nt(d, v) - delta)).astype(bf16)
            change = dot(ds, k)
        else:
            delta = jnp.sum(wide * probs[layer, :, 2 * PROMPT :], -1, keepdims=True)
            ds1 = (probs[layer, :, :PROMPT] * (dot_nt(d, v[:PROMPT]) - delta)).astype(bf16)
            ds2 = (probs[layer, :, PROMPT:LIVE] * (dot_nt(d, v[PROMPT:]) - delta)).astype(bf16)
            change = dot(ds1, k[:PROMPT]) + dot(ds2, k[PROMPT:])
        g = (wide + change * SCALE).astype(bf16)
        if final:
            last[...] = g
        else:
            grads[layer - 1] = g

    @pl.when(active[0] == 1)
    def _():
        first = pltpu.make_async_copy(g_in, grads.at[n - 1], g_sem)
        first.start()
        for i in range(AHEAD):
            for copy in loads(i):
                copy.start()
        first.wait()

        def body(i, carry):
            step(i, False)
            return carry

        lax.fori_loop(0, n - 1, body, 0)
        step(n - 1, True)
        done = pltpu.make_async_copy(last, g_out, g_sem)
        done.start()

        def finish(layer, carry):
            save(layer).wait()
            return carry

        lax.fori_loop(0, n, finish, 0)
        done.wait()


def chain(prompt, active, ks, vs, g, stash, probs, k, v):
    n, rows, width = probs.shape
    count = PROMPT if prompt else LIVE
    table = pl.BlockSpec(memory_space=pltpu.SMEM)
    hbm = pl.BlockSpec(memory_space=pl.ANY)
    return pl.pallas_call(
        functools.partial(chain_kernel, prompt, n),
        name="prompt_chain" if prompt else "response_chain",
        in_specs=[table] * 3 + [hbm] * 5,
        out_specs=[hbm] * 2,
        scratch_shapes=[
            pltpu.VMEM((n, rows, width), f32),
            pltpu.VMEM((n, count, HD), bf16),
            pltpu.VMEM((n, count, HD), bf16),
            pltpu.VMEM((n, rows, HD), bf16),
            pltpu.VMEM((rows, HD), bf16),
            pltpu.SemaphoreType.DMA((n, 3)),
            pltpu.SemaphoreType.DMA((n,)),
            pltpu.SemaphoreType.DMA,
        ],
        out_shape=[shape((rows, HD), bf16), shape((n, rows, HD), bf16)],
        input_output_aliases={3: 0, 4: 1},
        compiler_params=params(),
    )(active, ks, vs, g, stash, probs, k, v)


HEADS_AT_ONCE = 2


def prompt_grad_kernel(q_ref, g_ref, k_ref, v_ref, out_ref, bias):
    @pl.when(pl.program_id(0) == 0)
    def _():
        bias[...] = prompt_bias(1)
        out_ref[...] = jnp.zeros_like(out_ref)

    k, v = k_ref[...], v_ref[...]
    dk, dv = 0.0, 0.0
    for u in range(HEADS_AT_ONCE):
        q, g = q_ref[u], g_ref[u]
        (p,) = softmax([dot_nt(k, q) + bias[...]], 0)
        dp = dot_nt(v, g)
        pb = p.astype(bf16)
        delta = jnp.sum(pb.astype(f32) * dp, 0, keepdims=True)
        ds = (p * (dp - delta)).astype(bf16)
        dk = dk + dot(ds, q)
        dv = dv + dot(pb, g)
    out_ref[:, :HD] += dk * SCALE
    out_ref[:, HD:] += dv


def prompt_grad(q, g, k, v):
    n = q.shape[0]
    block = pl.BlockSpec((HEADS_AT_ONCE, PROMPT, HD), lambda i: (i, 0, 0))
    whole = lambda w: pl.BlockSpec((PROMPT, w), lambda i: (0, 0))
    return pl.pallas_call(
        prompt_grad_kernel,
        name="prompt_grad",
        grid=(n // HEADS_AT_ONCE,),
        in_specs=[block, block, whole(HD), whole(HD)],
        out_specs=whole(2 * HD),
        scratch_shapes=[pltpu.VMEM((PROMPT, PROMPT), f32)],
        out_shape=shape((PROMPT, 2 * HD)),
        compiler_params=params(),
    )(q, g, k, v)


def response_grad_kernel(lens, q_ref, g_ref, k_ref, v_ref, part_ref, out_ref, sum_ref, bias, acc):
    i = pl.program_id(0)

    @pl.when(i == 0)
    def _():
        bias[...] = response_bias(lens, 1)
        acc[:PROMPT] = part_ref[...]
        acc[PROMPT:] = jnp.zeros((RESP, 2 * HD), f32)

    k1, k2 = k_ref[:PROMPT], k_ref[PROMPT:]
    v1, v2 = v_ref[:PROMPT], v_ref[PROMPT:]
    dk1, dk2, dv1, dv2 = 0.0, 0.0, 0.0, 0.0
    for u in range(HEADS_AT_ONCE):
        q, g = q_ref[u], g_ref[u]
        p1, p2 = softmax([dot_nt(k1, q), dot_nt(k2, q) + bias[...]], 0)
        dp1, dp2 = dot_nt(v1, g), dot_nt(v2, g)
        pb1, pb2 = p1.astype(bf16), p2.astype(bf16)
        delta = jnp.sum(pb1.astype(f32) * dp1, 0, keepdims=True) + jnp.sum(
            pb2.astype(f32) * dp2, 0, keepdims=True
        )
        ds1 = (p1 * (dp1 - delta)).astype(bf16)
        ds2 = (p2 * (dp2 - delta)).astype(bf16)
        dk1, dk2 = dk1 + dot(ds1, q), dk2 + dot(ds2, q)
        dv1, dv2 = dv1 + dot(pb1, g), dv2 + dot(pb2, g)
    acc[:PROMPT, :HD] += dk1 * SCALE
    acc[PROMPT:, :HD] += dk2 * SCALE
    acc[:PROMPT, HD:] += dv1
    acc[PROMPT:, HD:] += dv2

    @pl.when(i == pl.num_programs(0) - 1)
    def _():
        total = acc[...]
        squares = jnp.sum(total * total, 0, keepdims=True)
        sum_ref[...] = squares[:, :HD] + squares[:, HD:]
        out_ref[:PROMPT] = total[:PROMPT]
        spread = chosen_rows(lens, 1)
        left = total[PROMPT:]
        placed = jnp.zeros((NRESP * RLEN, 2 * HD), f32)
        for _ in range(3):
            term = left.astype(bf16)
            placed = placed + dot(spread, term)
            left = left - term.astype(f32)
        out_ref[PROMPT:] = placed


def response_grad(lens, q, g, k, v, part):
    n = q.shape[0]
    rows = PROMPT + NRESP * RLEN
    block = pl.BlockSpec((HEADS_AT_ONCE, RESP, HD), lambda i, a: (i, 0, 0))
    whole = lambda *dims: pl.BlockSpec(dims, lambda i, a: (0, 0))
    return pl.pallas_call(
        response_grad_kernel,
        name="response_grad",
        grid_spec=pltpu.PrefetchScalarGridSpec(
            num_scalar_prefetch=1,
            grid=(n // HEADS_AT_ONCE,),
            in_specs=[
                block,
                block,
                whole(LIVE, HD),
                whole(LIVE, HD),
                whole(PROMPT, 2 * HD),
            ],
            out_specs=[whole(rows, 2 * HD), whole(1, HD)],
            scratch_shapes=[pltpu.VMEM((RESP, RESP), f32), pltpu.VMEM((LIVE, 2 * HD), f32)],
        ),
        out_shape=[shape((rows, 2 * HD)), shape((1, HD))],
        compiler_params=params(),
    )(lens, q, g, k, v, part)


def ring(step, size=SIDE):
    return [(i, (i + step) % size) for i in range(size)]


def gathered(block, axis):
    low = lax.ppermute(block, axis, ring(1))
    high = lax.ppermute(block, axis, ring(-1))
    half = block.shape[0] // 2
    far = jnp.concatenate(
        [
            lax.ppermute(low[:half], axis, ring(1)),
            lax.ppermute(high[half:], axis, ring(-1)),
        ]
    )
    return jnp.stack([block, low, high, far])


def slot_of(distance):
    distance = distance % SIDE
    return jnp.where(distance == 0, 0, jnp.where(distance == SIDE - 1, 1, distance + 1))


def summed(x, axis):
    size = lax.axis_size(axis)
    parts = [lax.ppermute(x, axis, ring(step, size)) for step in range(1, size)]
    return functools.reduce(jnp.add, parts, x)


def on_device(hidden_stash, key_stash, value_stash, top_grads, lens):
    stage = lax.axis_index("zl")
    my_x = lax.axis_index("x")
    my_y = lax.axis_index("y")
    place = (my_x * SIDE + my_y).reshape(1).astype(jnp.int32)
    qp, qr, gp, gr, k, v = pack(
        lens, place, hidden_stash[0], top_grads, key_stash[0], value_stash[0]
    )
    layers = jnp.arange(PLANE, dtype=jnp.int32)
    slot_x = slot_of(layers // SIDE - my_x)
    slot_y = slot_of(layers % SIDE - my_y)
    ks = (slot_x * SIDE + slot_y).astype(jnp.int32)
    vs = (slot_y * SIDE + slot_x).astype(jnp.int32)
    plane = ("x", "y")
    swap = lambda a: lax.all_to_all(a, plane, 0, 0, tiled=True)
    all_k = gathered(gathered(k, "y"), "x").reshape(PLANE, LIVE, HD)
    all_v = gathered(gathered(v, "x"), "y").reshape(PLANE, LIVE, HD)
    my_qp = swap(qp)
    my_qr = swap(lax.optimization_barrier((qr, my_qp))[0])
    prob_p = prob(True, lens, ks, vs, my_qp, all_k, all_v)
    stash_p, stash_r = my_qp, my_qr
    prob_r = None
    for now in range(STAGES - 1, -1, -1):
        active = (stage == now).astype(jnp.int32).reshape(1)
        gp, stash_p = chain(True, active, ks, vs, gp, stash_p, prob_p, all_k, all_v)
        if prob_r is None:
            my_qr, gp = lax.optimization_barrier((my_qr, gp))
            prob_r = prob(False, lens, ks, vs, my_qr, all_k, all_v)
            stash_r = my_qr
        if now:
            gp = lax.ppermute(gp, "zl", [(now, now - 1)])
        gr, stash_r = chain(False, active, ks, vs, gr, stash_r, prob_r, all_k, all_v)
        gp, gr = lax.optimization_barrier((gp, gr))
        if now:
            gr = lax.ppermute(gr, "zl", [(now, now - 1)])
    part = prompt_grad(qp, swap(stash_p), k, v)
    raw, squares = response_grad(lens, qr, swap(stash_r), k, v, part)
    for axis in ("y", "x", "tp", "zl"):
        squares = summed(squares, axis)
    square_sum = jnp.sum(squares)
    entries = STAGES * PLANE * lax.axis_size("tp") * raw.shape[0] * raw.shape[1]
    clip_limit = clip_rms * math.sqrt(entries)
    factor = clip_limit / jnp.maximum(jnp.sqrt(square_sum), clip_limit)
    return (raw * factor)[None]


def solution(mesh):
    parts = mesh.devices.reshape(STAGES, SIDE, SIDE, -1)
    finer = Mesh(parts, ("zl", "x", "y", "tp"))
    pipe = ("zl", "x", "y")
    placed = (
        P(pipe, None, "tp"),
        P(pipe, None, "tp"),
        P(pipe, None, "tp"),
        P(None, "tp"),
        P(),
    )
    return jax.shard_map(
        on_device, mesh=finer, in_specs=placed, out_specs=P(pipe, None, "tp"), check_vma=False
    )
```

time: 255 us -> 235 us (0.922)
  blocking collectives: 48.4 us -> 0 us
  starting transfers between devices: 47.3 us -> 76 us
    all_to_all x3 -> x0, blocking collectives: 48.4 us -> none  [the longest x2 30.2 us: on_device(): lax.all_to_all(spread, axes, 0, 0, tiled=True)]
    ppermute x3, waiting for transfers between devices: 51.2 us -> 16.8 us  [on_device(): gr = lax.ppermute(gr, 'zl', [(now, now - 1)])]
    ppermute x0 -> x12, starting transfers between devices: none -> 26.9 us  [summed(): parts = [lax.ppermute(x, axis, ring(step, size)) for step in range(1, size)]]
    ppermute x3, waiting for transfers between devices: 3.72 us -> 20.7 us  [on_device(): gp = lax.ppermute(gp, 'zl', [(now, now - 1)])]
    ppermute x0 -> x12, waiting for transfers between devices: none -> 10.5 us  [summed(): parts = [lax.ppermute(x, axis, ring(step, size)) for step in range(1, size)]]
    all_to_all x3 -> x4, starting transfers between devices: 14.5 us -> 20.7 us  [on_device(): swap = lambda a: lax.all_to_all(a, plane, 0, 0, tiled=True)]
    ppermute x4, waiting for transfers between devices: 8.84 us -> 13.2 us  [gathered(): lax.ppermute(low[:half], axis, ring(1))]
    ppermute x4, starting transfers between devices: 9.77 us -> 6.24 us  [gathered(): high = lax.ppermute(block, axis, ring(-1))]
  transfers between devices with their start and end apart: 25 -> 38, of which waited for: 4 -> 15; matrix products, arithmetic and copies ran while one was open for 5% -> 4% of each run, Pallas kernels for 20% -> 18%
where the time goes in v2:
time: 235 us; the launch traced here: 233 us
  starting transfers between devices  76 us (32%)
  Pallas kernels  70.8 us (30%)
  waiting for transfers between devices  67.3 us (29%)
  other arithmetic  9.84 us (4%)
  local copies, waits for them, and re-layouts  8.31 us (4%)
    ppermute x12, starting transfers between devices, summed(): parts = [lax.ppermute(x, axis, ring(step, size)) for step in range(1, size)]  26.9 us
    pallas_call x8, Pallas kernels, chain(): pl.pallas_call(functools.partial(chain_kernel, prompt, n), name='prompt_c...  26.2 us
    all_to_all x4, starting transfers between devices, on_device(): swap = lambda a: lax.all_to_all(a, plane, 0, 0, tiled=True)  20.7 us
    ppermute x3, waiting for transfers between devices, on_device(): gp = lax.ppermute(gp, 'zl', [(now, now - 1)])  20.7 us
    pallas_call x2, Pallas kernels, prob(): pl.pallas_call(functools.partial(prob_kernel, prompt), name='prompt_prob'...  18.8 us
    ppermute x3, waiting for transfers between devices, on_device(): gr = lax.ppermute(gr, 'zl', [(now, now - 1)])  16.8 us
    ppermute x4, waiting for transfers between devices, gathered(): lax.ppermute(low[:half], axis, ring(1))  13.2 us
    pallas_call x1, Pallas kernels, response_grad(): pl.pallas_call(response_grad_kernel, name='response_grad', grid_spec=pltp...  11.8 us
  transfers between devices with their start and end apart: 38, of which 15 were waited for; matrix products, arithmetic and copies ran while one was open for 4% of the time, Pallas kernels for 18%

profile of v2, /device:TPU:1, one launch (start us, length us, event | category | flops | bytes accessed | tf_op | source)
XLA Modules:
  0.0 233.4 jit_solution(5995573437227099302)
XLA Ops:
  0.0 5.4 %pack.1 = (bf16[16,256,128]{2,1,0:T(8,128)(2,1)}, bf16[16,192,128]{2,1,0:T(8,128)(2,1)}, bf16[256,128]{1,0:T(8,128)(2,1)}, bf16[192,128]{1,0:T(8,128)(2,1)}, bf1...) custom-call(s32[4]{0:T(128)} %lens.7, s32[1]{0:T(128)} %bitcast.place, bf16[512,2048]{1,0:T(8,128)(2,1)} %bitcast.66, ...), custom_call_target="tpu_custom_call" | custom-call | tf_op jit(solution)/shard_map/pack/pallas_call | solution.py:104
  5.5 2.1 collective-permute-start.8
  7.6 1.4 collective-permute-start.9
  8.9 1.4 collective-permute-start
  10.3 1.4 collective-permute-start.1
  11.8 4.4 %all-to-all-start = ((bf16[16,256,128]{2,1,0:T(8,128)(2,1)}), bf16[16,256,128]{2,1,0:T(8,128)(2,1)S(1)}, u32[]{:S(2)}, u32[]{:S(2)}) async-start(bf16[16,256,128]{2,1,0:T(8,128)(2,1)} %get-tuple-element.37.q_ref), calls=%async_computation | async-start | bytes 2097152 | tf_op jit(solution)/shard_map/all_to_all | solution.py:449
  16.2 1.4 collective-permute-start.10
  17.7 1.4 collective-permute-start.11
  19.1 1.4 collective-permute-start.2
  20.5 1.4 collective-permute-start.3
  21.9 7.3 %collective-permute-done.10 = bf16[224,128]{1,0:T(8,128)(2,1)S(1)} collective-permute-done((bf16[224,128]{1,0:T(8,128)(2,1)S(1)}, bf16[224,128]{1,0:T(8,128)(2,1)S(1)}, u32[]{:S(2)}, u32[]{:S(2)}) %collective-permute-start.10) | collective-permute-done | bytes 57376 | tf_op jit(solution)/shard_map/ppermute | solution.py:417
  29.4 1.2 collective-permute-start.12
  30.6 1.5 collective-permute-start.13
  33.7 1.9 collective-permute-start.5
  35.7 4.3 %collective-permute-done.12 = bf16[4,448,128]{2,1,0:T(8,128)(2,1)S(1)} collective-permute-done((bf16[4,448,128]{2,1,0:T(8,128)(2,1)S(1)}, bf16[4,448,128]{2,1,0:T(8,128)(2,1)S(1)}, u32[]{:S(2)}, u32[]{:S(2)}) %collective-permute-start.12) | collective-permute-done | bytes 458784 | tf_op jit(solution)/shard_map/ppermute | solution.py:412
  41.4 2.7 %collective-permute-start.15 = (bf16[2,448,128]{2,1,0:T(8,128)(2,1)}, bf16[2,448,128]{2,1,0:T(8,128)(2,1)}, u32[]{:S(2)}, u32[]{:S(2)}) collective-permute-start(bf16[2,448,128]{2,1,0:T(8,128)(2,1)} %slice.39), channel_id=1, source_target_pairs={{0,12},{4,0},{8,4},{12,8},{1,13},{5,1},{9,5},{13,9},{2,14},{6,2},{... | collective-permute-start | bytes 688136 | tf_op jit(solution)/shard_map/ppermute | solution.py:418
  44.1 3.6 %all-to-all-start.1 = ((bf16[16,192,128]{2,1,0:T(8,128)(2,1)}), bf16[16,192,128]{2,1,0:T(8,128)(2,1)S(1)}, u32[]{:S(2)}, u32[]{:S(2)}) async-start(bf16[16,192,128]{2,1,0:T(8,128)(2,1)} %get-tuple-element.38.q_ref), calls=%async_computation.1 | async-start | bytes 1572864 | tf_op jit(solution)/shard_map/all_to_all | solution.py:449
  48.8 1.5 collective-permute-start.6
  51.3 1.5 collective-permute-start.7
  54.4 5.8 %collective-permute-done.6 = bf16[2,448,128]{2,1,0:T(8,128)(2,1)S(1)} collective-permute-done((bf16[2,448,128]{2,1,0:T(8,128)(2,1)S(1)}, bf16[2,448,128]{2,1,0:T(8,128)(2,1)S(1)}, u32[]{:S(2)}, u32[]{:S(2)}) %collective-permute-start.6) | collective-permute-done | bytes 229408 | tf_op jit(solution)/shard_map/ppermute | solution.py:417
  60.3 1.5 pad_maximum_fusion.1
  61.8 2.6 %pad_maximum_fusion = bf16[4,4,448,128]{3,2,1,0:T(8,128)(2,1)} fusion(bf16[1,4,448,128]{3,2,1,0:T(8,128)(2,1)S(1)} %maximum_bitcast_fusion, bf16[1,4,448,128]{3,2,1,0:T(8,128)(2,1)} %bitcast.14, bf16[1,4,448,128]{3,2,1,0:T(8,128)(2,1)} %bitcast.13, bf16[1,4,448,128]{3,2,1,0:T(8,128)(2,1)S(1)} %get-tuple-element.69), kind=kLoop, calls=%fused_computation | loop fusion | flops 2752512 | bytes 3670016 | tf_op jit(solution)/shard_map/stack | solution.py:421
  64.4 8.2 %prompt_prob.1.prob_hbm = f32[16,256,384]{2,1,0:T(8,128)} custom-call(s32[4]{0:T(128)} %lens.7, s32[16]{0:T(128)} %get-tuple-element.72.ks, s32[16]{0:T(128)} %get-tuple-element.71.vs, bf16[16,256,128]{2,1,0:T(8,128)(2,1)} %copy-done, bf16[16,448,128]{2,1,0:T(8,128)(2,1)} %bitcast.50, bf16[16,448,128]{2,1,0:T(8,128)(2,1)} %bitcast.51, ...), custom_call_target="tpu_custom_call" | custom-call | tf_op jit(solution)/shard_map/prompt_prob/pallas_call | solution.py:180
  72.6 1.3 prompt_chain.4
  74.8 10.6 %response_prob.1.prob_hbm = f32[16,192,640]{2,1,0:T(8,128)} custom-call(s32[4]{0:T(128)} %lens.7, s32[16]{0:T(128)} %get-tuple-element.72.ks, s32[16]{0:T(128)} %get-tuple-element.71.vs, bf16[16,192,128]{2,1,0:T(8,128)(2,1)} %copy-done.1, bf16[16,448,128]{2,1,0:T(8,128)(2,1)} %bitcast.55, bf16[16,448,128]{2,1,0:T(8,128)(2,1)} %bitcast.56, ...), custom_call_target="tpu_custom_call" | custom-call | tf_op jit(solution)/shard_map/response_prob/pallas_call | solution.py:180
  85.3 1.3 response_chain.4
  87.2 1.4 prompt_chain.5
  90.6 1.3 response_chain.5
  92.5 1.4 prompt_chain.6
  93.9 1.3 collective-permute-start.19
  96.5 1.3 response_chain.6
  97.8 20.7 %collective-permute-done.19.g_in = bf16[256,128]{1,0:T(8,128)(2,1)S(1)} collective-permute-done((bf16[256,128]{1,0:T(8,128)(2,1)}, bf16[256,128]{1,0:T(8,128)(2,1)S(1)}, u32[]{:S(2)}, u32[]{:S(2)}) %collective-permute-start.19) | collective-permute-done | bytes 65568 | tf_op jit(solution)/shard_map/ppermute | solution.py:465
  119.1 8.9 %prompt_chain.7 = (bf16[256,128]{1,0:T(8,128)(2,1)}, bf16[16,256,128]{2,1,0:T(8,128)(2,1)}) custom-call(s32[1]{0:T(128)} %bitcast.4.active, s32[16]{0:T(128)} %get-tuple-element.72.ks, s32[16]{0:T(128)} %get-tuple-element.71.vs, bf16[256,128]{1,0:T(8,128)(2,1)} %copy-done.8, ...), custom_call_target="tpu_custom_call", output_to_operand_aliasing={{0}: (3, {}), {1}: (4, {})} | custom-call | tf_op jit(solution)/shard_map/prompt_chain/pallas_call | solution.py:275
  128.0 6.0 %all-to-all-start.3 = ((bf16[16,256,128]{2,1,0:T(8,128)(2,1)}), bf16[16,256,128]{2,1,0:T(8,128)(2,1)S(1)}, u32[]{:S(2)}, u32[]{:S(2)}) async-start(bf16[16,256,128]{2,1,0:T(8,128)(2,1)} %get-tuple-element.64), calls=%async_computation.3 | async-start | bytes 2097152 | tf_op jit(solution)/shard_map/all_to_all | solution.py:449
  134.0 1.3 collective-permute-start.21
  135.3 16.8 %collective-permute-done.21.g_in = bf16[192,128]{1,0:T(8,128)(2,1)S(1)} collective-permute-done((bf16[192,128]{1,0:T(8,128)(2,1)S(1)}, bf16[192,128]{1,0:T(8,128)(2,1)S(1)}, u32[]{:S(2)}, u32[]{:S(2)}) %collective-permute-start.21) | collective-permute-done | bytes 49184 | tf_op jit(solution)/shard_map/ppermute | solution.py:469
  152.7 9.5 %response_chain.7 = (bf16[192,128]{1,0:T(8,128)(2,1)}, bf16[16,192,128]{2,1,0:T(8,128)(2,1)}) custom-call(s32[1]{0:T(128)} %bitcast.4.active, s32[16]{0:T(128)} %get-tuple-element.72.ks, s32[16]{0:T(128)} %get-tuple-element.71.vs, bf16[192,128]{1,0:T(8,128)(2,1)} %copy-done.14, ...), custom_call_target="tpu_custom_call", output_to_operand_aliasing={{0}: (3, {}), {1}: (4, {})} | custom-call | tf_op jit(solution)/shard_map/response_chain/pallas_call | solution.py:275
  162.3 6.7 %all-to-all-start.2 = ((bf16[16,192,128]{2,1,0:T(8,128)(2,1)}), bf16[16,192,128]{2,1,0:T(8,128)(2,1)S(1)}, u32[]{:S(2)}, u32[]{:S(2)}) async-start(bf16[16,192,128]{2,1,0:T(8,128)(2,1)} %get-tuple-element.61), calls=%async_computation.2 | async-start | bytes 1572864 | tf_op jit(solution)/shard_map/all_to_all | solution.py:449
  169.0 8.6 %prompt_grad.1.part_ref = f32[256,256]{1,0:T(8,128)} custom-call(bf16[16,256,128]{2,1,0:T(8,128)(2,1)} %get-tuple-element.37.q_ref, bf16[16,256,128]{2,1,0:T(8,128)(2,1)} %copy-done.2, bf16[448,128]{1,0:T(8,128)(2,1)} %get-tuple-element.40.k_ref, bf16[448,128]{1,0:T(8,128)(2,1)} %get-tuple-element.41.v_ref), custom_call_target="tpu_custom_call" | custom-call | tf_op jit(solution)/shard_map/prompt_grad/pallas_call | solution.py:324
  177.5 1.8 all-to-all-done.2.g_ref
  180.2 11.8 %response_grad.1 = (f32[512,256]{1,0:T(8,128)}, f32[1,128]{1,0:T(1,128)}) custom-call(s32[4]{0:T(128)} %lens.7, bf16[16,192,128]{2,1,0:T(8,128)(2,1)} %get-tuple-element.38.q_ref, bf16[16,192,128]{2,1,0:T(8,128)(2,1)} %copy-done.3, bf16[448,128]{1,0:T(8,128)(2,1)} %get-tuple-element.40.k_ref, bf16[448,128]{1,0:T(8,128)(2,1)} %get-tuple-element.41.v_ref, ...), custom_call_target="tpu_custom_call" | custom-call | tf_op jit(solution)/shard_map/response_grad/pallas_call | solution.py:386
  192.3 1.7 collective-permute-start.23
  198.2 2.4 %collective-permute-start.26 = (f32[1,128]{1,0:T(1,128)S(1)}, f32[1,128]{1,0:T(1,128)S(1)}, u32[]{:S(2)}, u32[]{:S(2)}) collective-permute-start(f32[1,128]{1,0:T(1,128)S(1)} %add_add_fusion.2), channel_id=1, source_target_pairs={{0,32},{16,48},{32,0},{48,16},{1,33},{17,49},{33,1},{49,17},{2,34}... | collective-permute-start | bytes 1544 | tf_op jit(solution)/shard_map/ppermute | solution.py:431
  203.0 14.6 %collective-permute-start.28 = (f32[1,128]{1,0:T(1,128)S(1)}, f32[1,128]{1,0:T(1,128)S(1)}, u32[]{:S(2)}, u32[]{:S(2)}) collective-permute-start(f32[1,128]{1,0:T(1,128)S(1)} %add_add_fusion.1), channel_id=1, source_target_pairs={{0,1},{1,2},{2,3},{3,0},{4,5},{5,6},{6,7},{7,4},{8,9},{9,10},{10,1... | collective-permute-start | bytes 1544 | tf_op jit(solution)/shard_map/ppermute | solution.py:431
  218.8 5.1 %collective-permute-done.29 = f32[1,128]{1,0:T(1,128)S(1)} collective-permute-done((f32[1,128]{1,0:T(1,128)S(1)}, f32[1,128]{1,0:T(1,128)S(1)}, u32[]{:S(2)}, u32[]{:S(2)}) %collective-permute-start.29) | collective-permute-done | bytes 544 | tf_op jit(solution)/shard_map/ppermute | solution.py:431
  223.9 1.7 collective-permute-done.30
  225.8 3.2 %collective-permute-start.33 = (f32[1,128]{1,0:T(1,128)S(1)}, f32[1,128]{1,0:T(1,128)S(1)}, u32[]{:S(2)}, u32[]{:S(2)}) collective-permute-start(f32[1,128]{1,0:T(1,128)S(1)} %add_add_fusion), channel_id=1, source_target_pairs={{0,192},{64,0},{128,64},{192,128},{1,193},{65,1},{129,65},{193,129... | collective-permute-start | bytes 1544 | tf_op jit(solution)/shard_map/ppermute | solution.py:431
  231.5 1.9 multiply_bitcast_fusion
  (97 shorter events, 24.4 us)
Async XLA Ops:
  5.5 23.8 %copy-start.7 = (bf16[448,128]{1,0:T(8,128)(2,1)S(1)}, bf16[448,128]{1,0:T(8,128)(2,1)}, u32[]{:S(2)}) copy-start(bf16[448,128]{1,0:T(8,128)(2,1)} %get-tuple-element.41.v_ref) | copy-start | bytes 344068
  5.5 10.7 %collective-permute-start.8 = (bf16[448,128]{1,0:T(8,128)(2,1)}, bf16[448,128]{1,0:T(8,128)(2,1)S(1)}, u32[]{:S(2)}, u32[]{:S(2)}) collective-permute-start(bf16[448,128]{1,0:T(8,128)(2,1)} %get-tuple-element.41.v_ref), channel_id=1, source_target_pairs={{0,16},{16,32},{32,48},{48,0},{1,17},{17,33},{33,49},{49,1},{2,18}... | collective-permute-start | bytes 344072 | tf_op jit(solution)/shard_map/ppermute | solution.py:412
  7.6 10.1 %collective-permute-start.9 = (bf16[448,128]{1,0:T(8,128)(2,1)}, bf16[448,128]{1,0:T(8,128)(2,1)S(1)}, u32[]{:S(2)}, u32[]{:S(2)}) collective-permute-start(bf16[448,128]{1,0:T(8,128)(2,1)} %get-tuple-element.41.v_ref), channel_id=1, source_target_pairs={{0,48},{16,0},{32,16},{48,32},{1,49},{17,1},{33,17},{49,33},{2,50}... | collective-permute-start | bytes 344072 | tf_op jit(solution)/shard_map/ppermute | solution.py:413
  8.9 10.1 %collective-permute-start = (bf16[448,128]{1,0:T(8,128)(2,1)}, bf16[448,128]{1,0:T(8,128)(2,1)S(1)}, u32[]{:S(2)}, u32[]{:S(2)}) collective-permute-start(bf16[448,128]{1,0:T(8,128)(2,1)} %get-tuple-element.40.k_ref), channel_id=1, source_target_pairs={{0,4},{4,8},{8,12},{12,0},{1,5},{5,9},{9,13},{13,1},{2,6},{6,10},{... | collective-permute-start | bytes 344072 | tf_op jit(solution)/shard_map/ppermute | solution.py:412
  10.3 10.2 %collective-permute-start.1 = (bf16[448,128]{1,0:T(8,128)(2,1)}, bf16[448,128]{1,0:T(8,128)(2,1)S(1)}, u32[]{:S(2)}, u32[]{:S(2)}) collective-permute-start(bf16[448,128]{1,0:T(8,128)(2,1)} %get-tuple-element.40.k_ref), channel_id=1, source_target_pairs={{0,12},{4,0},{8,4},{12,8},{1,13},{5,1},{9,5},{13,9},{2,14},{6,2},{... | collective-permute-start | bytes 344072 | tf_op jit(solution)/shard_map/ppermute | solution.py:413
  11.8 20.3 %copy-start.6 = (bf16[448,128]{1,0:T(8,128)(2,1)S(1)}, bf16[448,128]{1,0:T(8,128)(2,1)}, u32[]{:S(2)}) copy-start(bf16[448,128]{1,0:T(8,128)(2,1)} %get-tuple-element.40.k_ref) | copy-start | bytes 344068
  11.8 32.3 %all-to-all-start = ((bf16[16,256,128]{2,1,0:T(8,128)(2,1)}), bf16[16,256,128]{2,1,0:T(8,128)(2,1)S(1)}, u32[]{:S(2)}, u32[]{:S(2)}) async-start(bf16[16,256,128]{2,1,0:T(8,128)(2,1)} %get-tuple-element.37.q_ref), calls=%async_computation | async-start | bytes 2097152 | tf_op jit(solution)/shard_map/all_to_all | solution.py:449
  16.2 13.0 %collective-permute-start.10 = (bf16[224,128]{1,0:T(8,128)(2,1)S(1)}, bf16[224,128]{1,0:T(8,128)(2,1)S(1)}, u32[]{:S(2)}, u32[]{:S(2)}) collective-permute-start(bf16[224,128]{1,0:T(8,128)(2,1)S(1)} %slice.36), channel_id=1, source_target_pairs={{0,16},{16,32},{32,48},{48,0},{1,17},{17,33},{33,49},{49,1},{2,18}... | collective-permute-start | bytes 172040 | tf_op jit(solution)/shard_map/ppermute | solution.py:417
  17.7 11.6 %collective-permute-start.11 = (bf16[224,128]{1,0:T(8,128)(2,1)S(1)}, bf16[224,128]{1,0:T(8,128)(2,1)S(1)}, u32[]{:S(2)}, u32[]{:S(2)}) collective-permute-start(bf16[224,128]{1,0:T(8,128)(2,1)S(1)} %slice.37), channel_id=1, source_target_pairs={{0,48},{16,0},{32,16},{48,32},{1,49},{17,1},{33,17},{49,33},{2,50}... | collective-permute-start | bytes 172040 | tf_op jit(solution)/shard_map/ppermute | solution.py:418
  19.1 13.0 %collective-permute-start.2 = (bf16[224,128]{1,0:T(8,128)(2,1)S(1)}, bf16[224,128]{1,0:T(8,128)(2,1)S(1)}, u32[]{:S(2)}, u32[]{:S(2)}) collective-permute-start(bf16[224,128]{1,0:T(8,128)(2,1)S(1)} %slice.32), channel_id=1, source_target_pairs={{0,4},{4,8},{8,12},{12,0},{1,5},{5,9},{9,13},{13,1},{2,6},{6,10},{... | collective-permute-start | bytes 172040 | tf_op jit(solution)/shard_map/ppermute | solution.py:417
  20.5 11.6 %collective-permute-start.3 = (bf16[224,128]{1,0:T(8,128)(2,1)S(1)}, bf16[224,128]{1,0:T(8,128)(2,1)S(1)}, u32[]{:S(2)}, u32[]{:S(2)}) collective-permute-start(bf16[224,128]{1,0:T(8,128)(2,1)S(1)} %slice.33), channel_id=1, source_target_pairs={{0,12},{4,0},{8,4},{12,8},{1,13},{5,1},{9,5},{13,9},{2,14},{6,2},{... | collective-permute-start | bytes 172040 | tf_op jit(solution)/shard_map/ppermute | solution.py:418
  29.4 10.6 %collective-permute-start.12 = (bf16[4,448,128]{2,1,0:T(8,128)(2,1)S(1)}, bf16[4,448,128]{2,1,0:T(8,128)(2,1)S(1)}, u32[]{:S(2)}, u32[]{:S(2)}) collective-permute-start(bf16[4,448,128]{2,1,0:T(8,128)(2,1)S(1)} %get-tuple-element.68), channel_id=1, source_target_pairs={{0,4},{4,8},{8,12},{12,0},{1,5},{5,9},{9,13},{13,1},{2,6},{6,10},{... | collective-permute-start | bytes 1376264 | tf_op jit(solution)/shard_map/ppermute | solution.py:412
  30.6 10.1 %collective-permute-start.13 = (bf16[4,448,128]{2,1,0:T(8,128)(2,1)S(1)}, bf16[4,448,128]{2,1,0:T(8,128)(2,1)S(1)}, u32[]{:S(2)}, u32[]{:S(2)}) collective-permute-start(bf16[4,448,128]{2,1,0:T(8,128)(2,1)S(1)} %get-tuple-element.68), channel_id=1, source_target_pairs={{0,12},{4,0},{8,4},{12,8},{1,13},{5,1},{9,5},{13,9},{2,14},{6,2},{... | collective-permute-start | bytes 1376264 | tf_op jit(solution)/shard_map/ppermute | solution.py:413
  33.0 14.8 %collective-permute-start.4 = (bf16[4,448,128]{2,1,0:T(8,128)(2,1)}, bf16[4,448,128]{2,1,0:T(8,128)(2,1)}, u32[]{:S(2)}, u32[]{:S(2)}) collective-permute-start(bf16[4,448,128]{2,1,0:T(8,128)(2,1)} %get-tuple-element.70), channel_id=1, source_target_pairs={{0,16},{16,32},{32,48},{48,0},{1,17},{17,33},{33,49},{49,1},{2,18}... | collective-permute-start | bytes 1376264 | tf_op jit(solution)/shard_map/ppermute | solution.py:412
  33.7 16.6 %collective-permute-start.5 = (bf16[4,448,128]{2,1,0:T(8,128)(2,1)}, bf16[4,448,128]{2,1,0:T(8,128)(2,1)}, u32[]{:S(2)}, u32[]{:S(2)}) collective-permute-start(bf16[4,448,128]{2,1,0:T(8,128)(2,1)} %get-tuple-element.70), channel_id=1, source_target_pairs={{0,48},{16,0},{32,16},{48,32},{1,49},{17,1},{33,17},{49,33},{2,50}... | collective-permute-start | bytes 1376264 | tf_op jit(solution)/shard_map/ppermute | solution.py:413
  40.7 12.7 %collective-permute-start.14 = (bf16[2,448,128]{2,1,0:T(8,128)(2,1)}, bf16[2,448,128]{2,1,0:T(8,128)(2,1)S(1)}, u32[]{:S(2)}, u32[]{:S(2)}) collective-permute-start(bf16[2,448,128]{2,1,0:T(8,128)(2,1)} %slice.38), channel_id=1, source_target_pairs={{0,4},{4,8},{8,12},{12,0},{1,5},{5,9},{9,13},{13,1},{2,6},{6,10},{... | collective-permute-start | bytes 688136 | tf_op jit(solution)/shard_map/ppermute | solution.py:417
  40.7 3.4 %copy-start.4 = (bf16[4,448,128]{2,1,0:T(8,128)(2,1)}, bf16[4,448,128]{2,1,0:T(8,128)(2,1)S(1)}, u32[]{:S(2)}) copy-start(bf16[4,448,128]{2,1,0:T(8,128)(2,1)S(1)} %collective-permute-done.13) | copy-start | bytes 1376260
  41.4 11.9 %collective-permute-start.15 = (bf16[2,448,128]{2,1,0:T(8,128)(2,1)}, bf16[2,448,128]{2,1,0:T(8,128)(2,1)}, u32[]{:S(2)}, u32[]{:S(2)}) collective-permute-start(bf16[2,448,128]{2,1,0:T(8,128)(2,1)} %slice.39), channel_id=1, source_target_pairs={{0,12},{4,0},{8,4},{12,8},{1,13},{5,1},{9,5},{13,9},{2,14},{6,2},{... | collective-permute-start | bytes 688136 | tf_op jit(solution)/shard_map/ppermute | solution.py:418
  44.1 16.1 %copy-start = (bf16[16,256,128]{2,1,0:T(8,128)(2,1)}, bf16[16,256,128]{2,1,0:T(8,128)(2,1)S(1)}, u32[]{:S(2)}) copy-start(bf16[16,256,128]{2,1,0:T(8,128)(2,1)S(1)} %all-to-all-done.q_ref.stash_in) | copy-start | bytes 3145732
  44.1 29.7 %all-to-all-start.1 = ((bf16[16,192,128]{2,1,0:T(8,128)(2,1)}), bf16[16,192,128]{2,1,0:T(8,128)(2,1)S(1)}, u32[]{:S(2)}, u32[]{:S(2)}) async-start(bf16[16,192,128]{2,1,0:T(8,128)(2,1)} %get-tuple-element.38.q_ref), calls=%async_computation.1 | async-start | bytes 1572864 | tf_op jit(solution)/shard_map/all_to_all | solution.py:449
  47.8 12.5 %copy-start.5 = (bf16[4,448,128]{2,1,0:T(8,128)(2,1)S(1)}, bf16[4,448,128]{2,1,0:T(8,128)(2,1)}, u32[]{:S(2)}) copy-start(bf16[4,448,128]{2,1,0:T(8,128)(2,1)} %copy-done.4) | copy-start | bytes 1376260
  48.8 11.4 %collective-permute-start.6 = (bf16[2,448,128]{2,1,0:T(8,128)(2,1)S(1)}, bf16[2,448,128]{2,1,0:T(8,128)(2,1)S(1)}, u32[]{:S(2)}, u32[]{:S(2)}) collective-permute-start(bf16[2,448,128]{2,1,0:T(8,128)(2,1)S(1)} %slice.34), channel_id=1, source_target_pairs={{0,16},{16,32},{32,48},{48,0},{1,17},{17,33},{33,49},{49,1},{2,18}... | collective-permute-start | bytes 688136 | tf_op jit(solution)/shard_map/ppermute | solution.py:417
  51.3 8.9 %collective-permute-start.7 = (bf16[2,448,128]{2,1,0:T(8,128)(2,1)S(1)}, bf16[2,448,128]{2,1,0:T(8,128)(2,1)S(1)}, u32[]{:S(2)}, u32[]{:S(2)}) collective-permute-start(bf16[2,448,128]{2,1,0:T(8,128)(2,1)S(1)} %slice.35), channel_id=1, source_target_pairs={{0,48},{16,0},{32,16},{48,32},{1,49},{17,1},{33,17},{49,33},{2,50}... | collective-permute-start | bytes 688136 | tf_op jit(solution)/shard_map/ppermute | solution.py:418
  73.9 12.7 %collective-permute-start.16 = (bf16[256,128]{1,0:T(8,128)(2,1)}, bf16[256,128]{1,0:T(8,128)(2,1)S(1)}, u32[]{:S(2)}, u32[]{:S(2)}) collective-permute-start(bf16[256,128]{1,0:T(8,128)(2,1)} %get-tuple-element.43), channel_id=1, source_target_pairs={{192,128},{193,129},{194,130},{195,131},{196,132},{197,133},{198,1... | collective-permute-start | bytes 196616 | tf_op jit(solution)/shard_map/ppermute | solution.py:465
  87.2 2.1 copy-start.11
  88.6 3.3 %collective-permute-start.17 = (bf16[256,128]{1,0:T(8,128)(2,1)}, bf16[256,128]{1,0:T(8,128)(2,1)S(1)}, u32[]{:S(2)}, u32[]{:S(2)}) collective-permute-start(bf16[256,128]{1,0:T(8,128)(2,1)} %get-tuple-element.49), channel_id=1, source_target_pairs={{128,64},{129,65},{130,66},{131,67},{132,68},{133,69},{134,70},{13... | collective-permute-start | bytes 196616 | tf_op jit(solution)/shard_map/ppermute | solution.py:465
  89.3 0.7 collective-permute-start.18
  92.5 2.7 %copy-start.16 = (bf16[192,128]{1,0:T(8,128)(2,1)S(1)}, bf16[192,128]{1,0:T(8,128)(2,1)}, u32[]{:S(2)}) copy-start(bf16[192,128]{1,0:T(8,128)(2,1)} %get-tuple-element.56) | copy-start | bytes 147460
  93.9 24.5 %collective-permute-start.19 = (bf16[256,128]{1,0:T(8,128)(2,1)}, bf16[256,128]{1,0:T(8,128)(2,1)S(1)}, u32[]{:S(2)}, u32[]{:S(2)}) collective-permute-start(bf16[256,128]{1,0:T(8,128)(2,1)} %get-tuple-element.55), channel_id=1, source_target_pairs={{64,0},{65,1},{66,2},{67,3},{68,4},{69,5},{70,6},{71,7},{72,8},{73... | collective-permute-start | bytes 196616 | tf_op jit(solution)/shard_map/ppermute | solution.py:465
  95.2 0.7 collective-permute-start.20
  128.0 6.0 %copy-start.13 = (bf16[192,128]{1,0:T(8,128)(2,1)S(1)}, bf16[192,128]{1,0:T(8,128)(2,1)}, u32[]{:S(2)}) copy-start(bf16[192,128]{1,0:T(8,128)(2,1)} %get-tuple-element.59) | copy-start | bytes 147460
  128.0 34.2 %all-to-all-start.3 = ((bf16[16,256,128]{2,1,0:T(8,128)(2,1)}), bf16[16,256,128]{2,1,0:T(8,128)(2,1)S(1)}, u32[]{:S(2)}, u32[]{:S(2)}) async-start(bf16[16,256,128]{2,1,0:T(8,128)(2,1)} %get-tuple-element.64), calls=%async_computation.3 | async-start | bytes 2097152 | tf_op jit(solution)/shard_map/all_to_all | solution.py:449
  134.0 18.1 %collective-permute-start.21 = (bf16[192,128]{1,0:T(8,128)(2,1)S(1)}, bf16[192,128]{1,0:T(8,128)(2,1)S(1)}, u32[]{:S(2)}, u32[]{:S(2)}) collective-permute-start(bf16[192,128]{1,0:T(8,128)(2,1)S(1)} %copy-done.13), channel_id=1, source_target_pairs={{64,0},{65,1},{66,2},{67,3},{68,4},{69,5},{70,6},{71,7},{72,8},{73... | collective-permute-start | bytes 147464 | tf_op jit(solution)/shard_map/ppermute | solution.py:469
  162.3 6.7 %copy-start.2 = (bf16[16,256,128]{2,1,0:T(8,128)(2,1)}, bf16[16,256,128]{2,1,0:T(8,128)(2,1)S(1)}, u32[]{:S(2)}) copy-start(bf16[16,256,128]{2,1,0:T(8,128)(2,1)S(1)} %all-to-all-done.3.g_ref) | copy-start | bytes 3145732
  162.3 17.0 %all-to-all-start.2 = ((bf16[16,192,128]{2,1,0:T(8,128)(2,1)}), bf16[16,192,128]{2,1,0:T(8,128)(2,1)S(1)}, u32[]{:S(2)}, u32[]{:S(2)}) async-start(bf16[16,192,128]{2,1,0:T(8,128)(2,1)} %get-tuple-element.61), calls=%async_computation.2 | async-start | bytes 1572864 | tf_op jit(solution)/shard_map/all_to_all | solution.py:449
  179.3 0.9 copy-start.3
  192.0 3.7 %collective-permute-start.22 = (f32[1,128]{1,0:T(1,128)}, f32[1,128]{1,0:T(1,128)S(1)}, u32[]{:S(2)}, u32[]{:S(2)}) collective-permute-start(f32[1,128]{1,0:T(1,128)} %get-tuple-element.66), channel_id=1, source_target_pairs={{0,4},{4,8},{8,12},{12,0},{1,5},{5,9},{9,13},{13,1},{2,6},{6,10},{... | collective-permute-start | bytes 1544 | tf_op jit(solution)/shard_map/ppermute | solution.py:431
  192.3 4.0 %collective-permute-start.23 = (f32[1,128]{1,0:T(1,128)}, f32[1,128]{1,0:T(1,128)S(1)}, u32[]{:S(2)}, u32[]{:S(2)}) collective-permute-start(f32[1,128]{1,0:T(1,128)} %get-tuple-element.66), channel_id=1, source_target_pairs={{0,8},{4,12},{8,0},{12,4},{1,9},{5,13},{9,1},{13,5},{2,10},{6,14},... | collective-permute-start | bytes 1544 | tf_op jit(solution)/shard_map/ppermute | solution.py:431
  193.9 2.4 %collective-permute-start.24 = (f32[1,128]{1,0:T(1,128)}, f32[1,128]{1,0:T(1,128)S(1)}, u32[]{:S(2)}, u32[]{:S(2)}) collective-permute-start(f32[1,128]{1,0:T(1,128)} %get-tuple-element.66), channel_id=1, source_target_pairs={{0,12},{4,0},{8,4},{12,8},{1,13},{5,1},{9,5},{13,9},{2,14},{6,2},{... | collective-permute-start | bytes 1544 | tf_op jit(solution)/shard_map/ppermute | solution.py:431
  197.0 4.8 %collective-permute-start.25 = (f32[1,128]{1,0:T(1,128)S(1)}, f32[1,128]{1,0:T(1,128)S(1)}, u32[]{:S(2)}, u32[]{:S(2)}) collective-permute-start(f32[1,128]{1,0:T(1,128)S(1)} %add_add_fusion.2), channel_id=1, source_target_pairs={{0,16},{16,32},{32,48},{48,0},{1,17},{17,33},{33,49},{49,1},{2,18}... | collective-permute-start | bytes 1544 | tf_op jit(solution)/shard_map/ppermute | solution.py:431
  198.2 3.9 %collective-permute-start.26 = (f32[1,128]{1,0:T(1,128)S(1)}, f32[1,128]{1,0:T(1,128)S(1)}, u32[]{:S(2)}, u32[]{:S(2)}) collective-permute-start(f32[1,128]{1,0:T(1,128)S(1)} %add_add_fusion.2), channel_id=1, source_target_pairs={{0,32},{16,48},{32,0},{48,16},{1,33},{17,49},{33,1},{49,17},{2,34}... | collective-permute-start | bytes 1544 | tf_op jit(solution)/shard_map/ppermute | solution.py:431
  200.6 2.4 %collective-permute-start.27 = (f32[1,128]{1,0:T(1,128)S(1)}, f32[1,128]{1,0:T(1,128)S(1)}, u32[]{:S(2)}, u32[]{:S(2)}) collective-permute-start(f32[1,128]{1,0:T(1,128)S(1)} %add_add_fusion.2), channel_id=1, source_target_pairs={{0,48},{16,0},{32,16},{48,32},{1,49},{17,1},{33,17},{49,33},{2,50}... | collective-permute-start | bytes 1544 | tf_op jit(solution)/shard_map/ppermute | solution.py:431
  203.0 15.8 %collective-permute-start.28 = (f32[1,128]{1,0:T(1,128)S(1)}, f32[1,128]{1,0:T(1,128)S(1)}, u32[]{:S(2)}, u32[]{:S(2)}) collective-permute-start(f32[1,128]{1,0:T(1,128)S(1)} %add_add_fusion.1), channel_id=1, source_target_pairs={{0,1},{1,2},{2,3},{3,0},{4,5},{5,6},{6,7},{7,4},{8,9},{9,10},{10,1... | collective-permute-start | bytes 1544 | tf_op jit(solution)/shard_map/ppermute | solution.py:431
  217.6 6.3 %collective-permute-start.29 = (f32[1,128]{1,0:T(1,128)S(1)}, f32[1,128]{1,0:T(1,128)S(1)}, u32[]{:S(2)}, u32[]{:S(2)}) collective-permute-start(f32[1,128]{1,0:T(1,128)S(1)} %add_add_fusion.1), channel_id=1, source_target_pairs={{0,2},{1,3},{2,0},{3,1},{4,6},{5,7},{6,4},{7,5},{8,10},{9,11},{10,... | collective-permute-start | bytes 1544 | tf_op jit(solution)/shard_map/ppermute | solution.py:431
  218.8 6.9 %collective-permute-start.30 = (f32[1,128]{1,0:T(1,128)S(1)}, f32[1,128]{1,0:T(1,128)S(1)}, u32[]{:S(2)}, u32[]{:S(2)}) collective-permute-start(f32[1,128]{1,0:T(1,128)S(1)} %add_add_fusion.1), channel_id=1, source_target_pairs={{0,3},{1,0},{2,1},{3,2},{4,7},{5,4},{6,5},{7,6},{8,11},{9,8},{10,9... | collective-permute-start | bytes 1544 | tf_op jit(solution)/shard_map/ppermute | solution.py:431
  225.6 4.2 %collective-permute-start.31 = (f32[1,128]{1,0:T(1,128)S(1)}, f32[1,128]{1,0:T(1,128)S(1)}, u32[]{:S(2)}, u32[]{:S(2)}) collective-permute-start(f32[1,128]{1,0:T(1,128)S(1)} %add_add_fusion), channel_id=1, source_target_pairs={{0,64},{64,128},{128,192},{192,0},{1,65},{65,129},{129,193},{193,1... | collective-permute-start | bytes 1544 | tf_op jit(solution)/shard_map/ppermute | solution.py:431
  225.7 4.2 %collective-permute-start.32 = (f32[1,128]{1,0:T(1,128)S(1)}, f32[1,128]{1,0:T(1,128)S(1)}, u32[]{:S(2)}, u32[]{:S(2)}) collective-permute-start(f32[1,128]{1,0:T(1,128)S(1)} %add_add_fusion), channel_id=1, source_target_pairs={{0,128},{64,192},{128,0},{192,64},{1,129},{65,193},{129,1},{193,65... | collective-permute-start | bytes 1544 | tf_op jit(solution)/shard_map/ppermute | solution.py:431
  225.8 4.4 %collective-permute-start.33 = (f32[1,128]{1,0:T(1,128)S(1)}, f32[1,128]{1,0:T(1,128)S(1)}, u32[]{:S(2)}, u32[]{:S(2)}) collective-permute-start(f32[1,128]{1,0:T(1,128)S(1)} %add_add_fusion), channel_id=1, source_target_pairs={{0,192},{64,0},{128,64},{192,128},{1,193},{65,1},{129,65},{193,129... | collective-permute-start | bytes 1544 | tf_op jit(solution)/shard_map/ppermute | solution.py:431
  (7 other events, 4.6 us)

commit v3 on v2

--- a/solution.py
+++ b/solution.py
@@ -33,8 +33,12 @@
     return lax.dot_general(a, b, (((1,), (1,)), ((), ())), preferred_element_type=f32)
 
 
-def params():
-    return pltpu.CompilerParams(vmem_limit_bytes=60 << 20)
+def about(us):
+    return pl.CostEstimate(flops=us * 1_000_000_000, bytes_accessed=0, transcendentals=0)
+
+
+def params(mebibytes=24):
+    return pltpu.CompilerParams(vmem_limit_bytes=mebibytes << 20)
 
 
 def shape(dims, dtype=f32):
@@ -79,31 +83,34 @@
     return jnp.where(col == slot * RLEN + row - start_of(row, lens), 1.0, 0.0).astype(bf16)
 
 
-def pack_kernel(lens, place, x_ref, top_ref, key_ref, value_ref, xp_out, xr_out, tp_out, tr_out, k_out, v_out):
-    chosen = chosen_rows(lens, 0)
+def pack_kernel(lens, place, x_ref, top_ref, key_ref, value_ref, xp_out, xr_out, tp_out, tr_out, k_out, v_out, chosen):
+    @pl.when(pl.program_id(0) == 0)
+    def _():
+        pick = chosen_rows(lens, 0)
+        chosen[...] = pick
+        tp_out[...] = top_ref[:PROMPT]
+        tr_out[...] = dot(pick, top_ref[PROMPT:]).astype(bf16)
+        for ref, out in ((key_ref, k_out), (value_ref, v_out)):
+            out[:PROMPT] = ref[:PROMPT]
+            out[PROMPT:] = dot(pick, ref[PROMPT:]).astype(bf16)
+
+    live = dot(chosen[...], x_ref[PROMPT:]).astype(bf16)
     for h in range(x_ref.shape[1] // HD):
         cols = slice(h * HD, (h + 1) * HD)
         xp_out[h] = x_ref[:PROMPT, cols]
-        xr_out[h] = dot(chosen, x_ref[PROMPT:, cols]).astype(bf16)
-
-    @pl.when(pl.program_id(0) == 0)
-    def _():
-        tp_out[...] = top_ref[:PROMPT]
-        tr_out[...] = dot(chosen, top_ref[PROMPT:]).astype(bf16)
-        for ref, out in ((key_ref, k_out), (value_ref, v_out)):
-            out[:PROMPT] = ref[:PROMPT]
-            out[PROMPT:] = dot(chosen, ref[PROMPT:]).astype(bf16)
+        xr_out[h] = live[:, cols]
 
 
 def pack(lens, place, x, top, key, value):
     rows, width = x.shape
     heads = width // HD
-    steps = 4
+    steps = 2
     some = heads // steps
     whole = lambda *dims: pl.BlockSpec(dims, lambda i, l, p: (0,) * len(dims))
     return pl.pallas_call(
         pack_kernel,
         name="pack",
+        cost_estimate=about(4),
         grid_spec=pltpu.PrefetchScalarGridSpec(
             num_scalar_prefetch=2,
             grid=(steps,),
@@ -121,6 +128,7 @@
                 whole(LIVE, HD),
                 whole(LIVE, HD),
             ],
+            scratch_shapes=[pltpu.VMEM((RESP, NRESP * RLEN), bf16)],
         ),
         out_shape=[
             shape((heads, PROMPT, HD), bf16),
@@ -130,7 +138,7 @@
             shape((LIVE, HD), bf16),
             shape((LIVE, HD), bf16),
         ],
-        compiler_params=params(),
+        compiler_params=params(60),
     )(lens, place, x, top, key, value)
 
 
@@ -145,18 +153,35 @@
 AT_ONCE = 4
 PROMPT_ROW = PROMPT + HD
 RESP_ROW = 2 * PROMPT + HD
+HBM = pl.BlockSpec(memory_space=pl.ANY)
+VMEM = pl.BlockSpec(memory_space=pltpu.VMEM)
+SMEM = pl.BlockSpec(memory_space=pltpu.SMEM)
+
+
+def fetch(parts, held, sems):
+    rows = held.shape[1]
+    return [
+        pltpu.make_async_copy(part.at[:, :rows], held.at[SIDE * j : SIDE * (j + 1)], sems.at[j])
+        for j, part in enumerate(parts)
+    ]
 
 
 def prob_kernel(prompt, lens, ks, vs, q_ref, *refs):
-    k_refs, v_refs = refs[:AT_ONCE], refs[AT_ONCE : 2 * AT_ONCE]
-    out, bias = refs[2 * AT_ONCE :]
-
-    @pl.when(pl.program_id(0) == 0)
-    def _():
+    k_parts, v_parts = refs[:SIDE], refs[SIDE : 2 * SIDE]
+    out, bias, keys, values, k_sems, v_sems = refs[2 * SIDE :]
+    i = pl.program_id(0)
+
+    @pl.when(i == 0)
+    def _():
+        copies = fetch(k_parts, keys, k_sems) + fetch(v_parts, values, v_sems)
+        for copy in copies:
+            copy.start()
         bias[...] = prompt_bias(0) if prompt else response_bias(lens, 0)
+        for copy in copies:
+            copy.wait()
 
     for u in range(AT_ONCE):
-        q, k, v = q_ref[u], k_refs[u][0], v_refs[u][0]
+        q, k, v = q_ref[u], keys[ks[i * AT_ONCE + u]], values[vs[i * AT_ONCE + u]]
         if prompt:
             (p,) = softmax([dot_nt(q, k) + bias[...]], -1)
             out[u, :, :PROMPT] = p
@@ -173,59 +198,48 @@
 def prob(prompt, lens, ks, vs, q, k, v):
     n, rows, _ = q.shape
     keys, width = (PROMPT, PROMPT_ROW) if prompt else (LIVE, RESP_ROW)
-    slot = lambda which, u: pl.BlockSpec(
-        (1, keys, HD), lambda i, *tables: (tables[which][i * AT_ONCE + u], 0, 0)
-    )
     block = lambda w: pl.BlockSpec((AT_ONCE, rows, w), lambda i, *tables: (i, 0, 0))
     return pl.pallas_call(
         functools.partial(prob_kernel, prompt),
         name="prompt_prob" if prompt else "response_prob",
+        cost_estimate=about(9),
         grid_spec=pltpu.PrefetchScalarGridSpec(
             num_scalar_prefetch=3,
             grid=(n // AT_ONCE,),
-            in_specs=[block(HD)]
-            + [slot(1, u) for u in range(AT_ONCE)]
-            + [slot(2, u) for u in range(AT_ONCE)],
+            in_specs=[block(HD)] + [HBM] * (2 * SIDE),
             out_specs=block(width),
-            scratch_shapes=[pltpu.VMEM((rows, rows), f32)],
+            scratch_shapes=[
+                pltpu.VMEM((rows, rows), f32),
+                pltpu.VMEM((n, keys, HD), bf16),
+                pltpu.VMEM((n, keys, HD), bf16),
+                pltpu.SemaphoreType.DMA((SIDE,)),
+                pltpu.SemaphoreType.DMA((SIDE,)),
+            ],
         ),
         out_shape=shape((n, rows, width)),
         compiler_params=params(),
-    )(lens, ks, vs, q, *([k] * AT_ONCE), *([v] * AT_ONCE))
-
-
-AHEAD = 3
-
-
-def chain_kernel(prompt, n, active, ks, vs, g_in, stash_in, prob_hbm, k_hbm, v_hbm, g_out, stash, probs, keys, values, grads, last, sems, out_sems, g_sem):
-    count = keys.shape[1]
-
-    def loads(i):
-        layer = n - 1 - i
-        return (
-            pltpu.make_async_copy(prob_hbm.at[layer], probs.at[layer], sems.at[layer, 0]),
-            pltpu.make_async_copy(k_hbm.at[ks[layer], :count], keys.at[layer], sems.at[layer, 1]),
-            pltpu.make_async_copy(v_hbm.at[vs[layer], :count], values.at[layer], sems.at[layer, 2]),
-        )
-
-    def save(layer):
-        return pltpu.make_async_copy(grads.at[layer], stash.at[layer], out_sems.at[layer])
-
-    def step(i, final):
-        layer = n - 1 - i
-        if not final:
-
-            @pl.when(i + AHEAD < n)
-            def _():
-                for copy in loads(i + AHEAD):
-                    copy.start()
-
-        for copy in loads(i):
-            copy.wait()
-        save(layer).start()
+    )(lens, ks, vs, q, *k, *v)
+
+
+GROUPS = ((14, 16), (12, 14), (8, 12), (4, 8), (0, 4))
+
+
+def chain_kernel(prompt, active, ks, vs, g_in, stash_in, prob_hbm, *refs):
+    k_parts, v_parts = refs[:SIDE], refs[SIDE : 2 * SIDE]
+    g_out, stash, probs, keys, values, grads, p_sems, k_sems, v_sems, out_sems = refs[2 * SIDE :]
+
+    def load(j):
+        span = pl.ds(GROUPS[j][0], GROUPS[j][1] - GROUPS[j][0])
+        return pltpu.make_async_copy(prob_hbm.at[span], probs.at[span], p_sems.at[j])
+
+    def save(j):
+        span = pl.ds(GROUPS[j][0], GROUPS[j][1] - GROUPS[j][0])
+        return pltpu.make_async_copy(grads.at[span], stash.at[span], out_sems.at[j])
+
+    def step(layer):
         d = grads[layer]
         wide = d.astype(f32)
-        k, v = keys[layer], values[layer]
+        k, v = keys[ks[layer]], values[vs[layer]]
         if prompt:
             delta = jnp.sum(wide * probs[layer, :, PROMPT:], -1, keepdims=True)
             ds = (probs[layer, :, :PROMPT] * (dot_nt(d, v) - delta)).astype(bf16)
@@ -235,62 +249,59 @@
             ds1 = (probs[layer, :, :PROMPT] * (dot_nt(d, v[:PROMPT]) - delta)).astype(bf16)
             ds2 = (probs[layer, :, PROMPT:LIVE] * (dot_nt(d, v[PROMPT:]) - delta)).astype(bf16)
             change = dot(ds1, k[:PROMPT]) + dot(ds2, k[PROMPT:])
-        g = (wide + change * SCALE).astype(bf16)
-        if final:
-            last[...] = g
-        else:
-            grads[layer - 1] = g
+        return (wide + change * SCALE).astype(bf16)
 
     @pl.when(active[0] == 1)
     def _():
-        first = pltpu.make_async_copy(g_in, grads.at[n - 1], g_sem)
-        first.start()
-        for i in range(AHEAD):
-            for copy in loads(i):
-                copy.start()
-        first.wait()
-
-        def body(i, carry):
-            step(i, False)
-            return carry
-
-        lax.fori_loop(0, n - 1, body, 0)
-        step(n - 1, True)
-        done = pltpu.make_async_copy(last, g_out, g_sem)
-        done.start()
-
-        def finish(layer, carry):
-            save(layer).wait()
-            return carry
-
-        lax.fori_loop(0, n, finish, 0)
-        done.wait()
+        first = fetch(v_parts, values, v_sems) + [load(0)] + fetch(k_parts, keys, k_sems)
+        for copy in first:
+            copy.start()
+        for j in range(1, len(GROUPS)):
+            load(j).start()
+        grads[GROUPS[0][1] - 1] = g_in[...]
+        for copy in first:
+            copy.wait()
+        for j, (low, high) in enumerate(GROUPS):
+            if j:
+                load(j).wait()
+
+            def body(i, carry, high=high):
+                grads[high - 2 - i] = step(high - 1 - i)
+                return carry
+
+            if low:
+                lax.fori_loop(0, high - low, body, 0)
+            else:
+                lax.fori_loop(0, high - 1, body, 0)
+                g_out[...] = step(0)
+            save(j).start()
+        for j in range(len(GROUPS)):
+            save(j).wait()
 
 
 def chain(prompt, active, ks, vs, g, stash, probs, k, v):
     n, rows, width = probs.shape
     count = PROMPT if prompt else LIVE
-    table = pl.BlockSpec(memory_space=pltpu.SMEM)
-    hbm = pl.BlockSpec(memory_space=pl.ANY)
     return pl.pallas_call(
-        functools.partial(chain_kernel, prompt, n),
+        functools.partial(chain_kernel, prompt),
         name="prompt_chain" if prompt else "response_chain",
-        in_specs=[table] * 3 + [hbm] * 5,
-        out_specs=[hbm] * 2,
+        cost_estimate=about(8),
+        in_specs=[SMEM] * 3 + [VMEM] + [HBM] * (2 + 2 * SIDE),
+        out_specs=[VMEM, HBM],
         scratch_shapes=[
             pltpu.VMEM((n, rows, width), f32),
             pltpu.VMEM((n, count, HD), bf16),
             pltpu.VMEM((n, count, HD), bf16),
             pltpu.VMEM((n, rows, HD), bf16),
-            pltpu.VMEM((rows, HD), bf16),
-            pltpu.SemaphoreType.DMA((n, 3)),
-            pltpu.SemaphoreType.DMA((n,)),
-            pltpu.SemaphoreType.DMA,
+            pltpu.SemaphoreType.DMA((len(GROUPS),)),
+            pltpu.SemaphoreType.DMA((SIDE,)),
+            pltpu.SemaphoreType.DMA((SIDE,)),
+            pltpu.SemaphoreType.DMA((len(GROUPS),)),
         ],
         out_shape=[shape((rows, HD), bf16), shape((n, rows, HD), bf16)],
-        input_output_aliases={3: 0, 4: 1},
+        input_output_aliases={4: 1},
         compiler_params=params(),
-    )(active, ks, vs, g, stash, probs, k, v)
+    )(active, ks, vs, g, stash, probs, *k, *v)
 
 
 HEADS_AT_ONCE = 2
@@ -324,6 +335,7 @@
     return pl.pallas_call(
         prompt_grad_kernel,
         name="prompt_grad",
+        cost_estimate=about(8),
         grid=(n // HEADS_AT_ONCE,),
         in_specs=[block, block, whole(HD), whole(HD)],
         out_specs=whole(2 * HD),
@@ -386,6 +398,7 @@
     return pl.pallas_call(
         response_grad_kernel,
         name="response_grad",
+        cost_estimate=about(11),
         grid_spec=pltpu.PrefetchScalarGridSpec(
             num_scalar_prefetch=1,
             grid=(n // HEADS_AT_ONCE,),
@@ -409,27 +422,12 @@
 
 
 def gathered(block, axis):
-    low = lax.ppermute(block, axis, ring(1))
-    high = lax.ppermute(block, axis, ring(-1))
-    half = block.shape[0] // 2
-    far = jnp.concatenate(
-        [
-            lax.ppermute(low[:half], axis, ring(1)),
-            lax.ppermute(high[half:], axis, ring(-1)),
-        ]
-    )
-    return jnp.stack([block, low, high, far])
+    return [block] + [lax.ppermute(block, axis, ring(step)) for step in (1, -1, 2)]
 
 
 def slot_of(distance):
     distance = distance % SIDE
     return jnp.where(distance == 0, 0, jnp.where(distance == SIDE - 1, 1, distance + 1))
-
-
-def summed(x, axis):
-    size = lax.axis_size(axis)
-    parts = [lax.ppermute(x, axis, ring(step, size)) for step in range(1, size)]
-    return functools.reduce(jnp.add, parts, x)
 
 
 def on_device(hidden_stash, key_stash, value_stash, top_grads, lens):
@@ -447,30 +445,34 @@
     vs = (slot_y * SIDE + slot_x).astype(jnp.int32)
     plane = ("x", "y")
     swap = lambda a: lax.all_to_all(a, plane, 0, 0, tiled=True)
-    all_k = gathered(gathered(k, "y"), "x").reshape(PLANE, LIVE, HD)
-    all_v = gathered(gathered(v, "x"), "y").reshape(PLANE, LIVE, HD)
+    row_k = jnp.stack(gathered(k, "y"))
+    col_v = jnp.stack(gathered(v, "x"))
+    all_k = gathered(row_k, "x")
+    all_v = gathered(col_v, "y")
     my_qp = swap(qp)
     my_qr = swap(lax.optimization_barrier((qr, my_qp))[0])
     prob_p = prob(True, lens, ks, vs, my_qp, all_k, all_v)
+    prob_r = prob(False, lens, ks, vs, my_qr, all_k, all_v)
     stash_p, stash_r = my_qp, my_qr
-    prob_r = None
+    after = lambda x, y: lax.optimization_barrier((x, y))[0]
     for now in range(STAGES - 1, -1, -1):
         active = (stage == now).astype(jnp.int32).reshape(1)
         gp, stash_p = chain(True, active, ks, vs, gp, stash_p, prob_p, all_k, all_v)
-        if prob_r is None:
-            my_qr, gp = lax.optimization_barrier((my_qr, gp))
-            prob_r = prob(False, lens, ks, vs, my_qr, all_k, all_v)
-            stash_r = my_qr
         if now:
-            gp = lax.ppermute(gp, "zl", [(now, now - 1)])
+            sent = lax.ppermute(gp, "zl", [(now, now - 1)])
+            gr = after(gr, gp if now == STAGES - 1 else sent)
+            gp = sent
+        else:
+            gr, stash_p = lax.optimization_barrier((gr, stash_p))
         gr, stash_r = chain(False, active, ks, vs, gr, stash_r, prob_r, all_k, all_v)
-        gp, gr = lax.optimization_barrier((gp, gr))
         if now:
+            gp = after(gp, gr)
             gr = lax.ppermute(gr, "zl", [(now, now - 1)])
-    part = prompt_grad(qp, swap(stash_p), k, v)
+    part = prompt_grad(after(qp, gr), swap(stash_p), k, v)
     raw, squares = response_grad(lens, qr, swap(stash_r), k, v, part)
-    for axis in ("y", "x", "tp", "zl"):
-        squares = summed(squares, axis)
+    for axes, size in ((plane, PLANE), (("zl", "tp"), STAGES * lax.axis_size("tp"))):
+        spread = jnp.broadcast_to(squares, (size, HD))
+        squares = jnp.sum(lax.all_to_all(spread, axes, 0, 0, tiled=True), 0, keepdims=True)
     square_sum = jnp.sum(squares)
     entries = STAGES * PLANE * lax.axis_size("tp") * raw.shape[0] * raw.shape[1]
     clip_limit = clip_rms * math.sqrt(entries)

time: 235 us -> 244 us (1.038)
  blocking collectives: 0 us -> 40.8 us
  starting transfers between devices: 76 us -> 46.4 us
  local copies, waits for them, and re-layouts: 8.31 us -> 27.9 us
  Pallas kernels: 70.8 us -> 61.3 us
  other arithmetic: 9.84 us -> 3.38 us
  waiting for transfers between devices: 67.3 us -> 61.8 us
    all_to_all x0 -> x2, blocking collectives: none -> 40.8 us  [on_device(): lax.all_to_all(spread, axes, 0, 0, tiled=True)]
    ppermute x31 -> x15, starting transfers between devices: 52.7 us -> 21.1 us  [the longest x12 18.3 us: gathered(): lax.ppermute(block, axis, ring(step))]
    unnamed x34 -> x50, local copies, waits for them, and re-layouts: 4.86 us -> 27.9 us
    pallas_call x11, Pallas kernels: 52 us -> 44.2 us  [the longest x8 23.6 us: chain(): pl.pallas_call(functools.partial(chain_kernel, prompt), name='prompt_chai...]
    ppermute x3, waiting for transfers between devices: 16.8 us -> 9.24 us  [on_device(): gr = lax.ppermute(gr, 'zl', [(now, now - 1)])]
    another operation x8 -> x2, other arithmetic: 6.08 us -> 1.92 us  [the longest x1 0.96 us: on_device(): col_v = jnp.stack(gathered(v, 'x'))]
    slice x8 -> x0, local copies, waits for them, and re-layouts: 3.45 us -> none  [the longest x4 1.73 us: gathered(): low[:half]]
    ppermute x31 -> x15, waiting for transfers between devices: 48.7 us -> 49 us  [the longest x12 28.5 us: gathered(): lax.ppermute(block, axis, ring(step))]
  transfers between devices with their start and end apart: 38 -> 22, of which waited for: 15 -> 6; matrix products, arithmetic and copies ran while one was open for 4% -> 1% of each run, Pallas kernels for 18% -> 18%
where the time goes in v3:
time: 244 us; the launch traced here: 243 us
  waiting for transfers between devices  61.8 us (25%)
  Pallas kernels  61.3 us (25%)
  starting transfers between devices  46.4 us (19%)
  blocking collectives  40.8 us (17%)
  local copies, waits for them, and re-layouts  27.9 us (11%)
  other arithmetic  3.38 us (1%)
    all_to_all x2, blocking collectives, on_device(): lax.all_to_all(spread, axes, 0, 0, tiled=True)  40.8 us
    ppermute x12, waiting for transfers between devices, gathered(): lax.ppermute(block, axis, ring(step))  28.5 us
    unnamed x50, local copies, waits for them, and re-layouts  27.9 us
    pallas_call x8, Pallas kernels, chain(): pl.pallas_call(functools.partial(chain_kernel, prompt), name='prompt_chai...  23.6 us
    all_to_all x4, starting transfers between devices, on_device(): swap = lambda a: lax.all_to_all(a, plane, 0, 0, tiled=True)  22.7 us
    ppermute x3, waiting for transfers between devices, on_device(): sent = lax.ppermute(gp, 'zl', [(now, now - 1)])  20.5 us
    ppermute x12, starting transfers between devices, gathered(): lax.ppermute(block, axis, ring(step))  18.3 us
    pallas_call x2, Pallas kernels, prob(): pl.pallas_call(functools.partial(prob_kernel, prompt), name='prompt_prob'...  17.1 us
  transfers between devices with their start and end apart: 22, of which 6 were waited for; matrix products, arithmetic and copies ran while one was open for 1% of the time, Pallas kernels for 18%

profile of v3, /device:TPU:1, one launch (start us, length us, event | category | flops | bytes accessed | tf_op | source)
XLA Modules:
  0.0 242.8 jit_solution(3533330424956093)
XLA Ops:
  0.0 4.0 %pack.1 = (bf16[16,256,128]{2,1,0:T(8,128)(2,1)}, bf16[16,192,128]{2,1,0:T(8,128)(2,1)}, bf16[256,128]{1,0:T(8,128)(2,1)}, bf16[192,128]{1,0:T(8,128)(2,1)}, bf1...) custom-call(s32[4]{0:T(128)} %lens.7, s32[1]{0:T(128)} %bitcast.place, bf16[512,2048]{1,0:T(8,128)(2,1)} %bitcast.32, ...), custom_call_target="tpu_custom_call" | custom-call | flops 4000000000 | tf_op jit(solution)/shard_map/pack/pallas_call | solution.py:110
  4.0 2.0 collective-permute-start.6
  6.1 1.3 collective-permute-start.7
  7.4 1.6 collective-permute-start.8
  9.1 5.5 %all-to-all-start = ((bf16[16,256,128]{2,1,0:T(8,128)(2,1)}), bf16[16,256,128]{2,1,0:T(8,128)(2,1)}, u32[]{:S(2)}, u32[]{:S(2)}) async-start(bf16[16,256,128]{2,1,0:T(8,128)(2,1)} %get-tuple-element.39.q_ref), calls=%async_computation | async-start | bytes 2097152 | tf_op jit(solution)/shard_map/all_to_all | solution.py:447
  14.6 1.0 pad_maximum_fusion.1.refs_4_
  15.6 2.6 %collective-permute-start.10 = (bf16[4,448,128]{2,1,0:T(8,128)(2,1)S(1)}, bf16[4,448,128]{2,1,0:T(8,128)(2,1)S(1)}, u32[]{:S(2)}, u32[]{:S(2)}) collective-permute-start(bf16[4,448,128]{2,1,0:T(8,128)(2,1)S(1)} %pad_maximum_fusion.1.refs_4_), channel_id=1, source_target_pairs={{0,12},{4,0},{8,4},{12,8},{1,13},{5,1},{9,5},{13,9},{2,14},{6,2},{... | collective-permute-start | bytes 1376264 | tf_op jit(solution)/shard_map/ppermute | solution.py:425
  18.9 0.7 collective-permute-start
  19.6 3.6 %collective-permute-start.11 = (bf16[4,448,128]{2,1,0:T(8,128)(2,1)S(1)}, bf16[4,448,128]{2,1,0:T(8,128)(2,1)S(1)}, u32[]{:S(2)}, u32[]{:S(2)}) collective-permute-start(bf16[4,448,128]{2,1,0:T(8,128)(2,1)S(1)} %pad_maximum_fusion.1.refs_4_), channel_id=1, source_target_pairs={{0,8},{4,12},{8,0},{12,4},{1,9},{5,13},{9,1},{13,5},{2,10},{6,14},... | collective-permute-start | bytes 1376264 | tf_op jit(solution)/shard_map/ppermute | solution.py:425
  23.2 16.9 %collective-permute-done.1 = bf16[448,128]{1,0:T(8,128)(2,1)S(1)} collective-permute-done((bf16[448,128]{1,0:T(8,128)(2,1)}, bf16[448,128]{1,0:T(8,128)(2,1)S(1)}, u32[]{:S(2)}, u32[]{:S(2)}) %collective-permute-start.1) | collective-permute-done | bytes 114720 | tf_op jit(solution)/shard_map/ppermute | solution.py:425
  40.5 1.0 pad_maximum_fusion.refs_0_
  41.4 1.9 collective-permute-start.3
  43.3 1.5 collective-permute-start.4
  44.8 1.9 collective-permute-start.5
  46.8 6.4 %all-to-all-start.1 = ((bf16[16,192,128]{2,1,0:T(8,128)(2,1)}), bf16[16,192,128]{2,1,0:T(8,128)(2,1)}, u32[]{:S(2)}, u32[]{:S(2)}) async-start(bf16[16,192,128]{2,1,0:T(8,128)(2,1)} %get-tuple-element.44.q_ref), calls=%async_computation.1 | async-start | bytes 1572864 | tf_op jit(solution)/shard_map/all_to_all | solution.py:447
  53.4 11.4 %collective-permute-done.5.refs_3_ = bf16[4,448,128]{2,1,0:T(8,128)(2,1)} collective-permute-done((bf16[4,448,128]{2,1,0:T(8,128)(2,1)S(1)}, bf16[4,448,128]{2,1,0:T(8,128)(2,1)}, u32[]{:S(2)}, u32[]{:S(2)}) %collective-permute-start.5) | collective-permute-done | bytes 458784 | tf_op jit(solution)/shard_map/ppermute | solution.py:425
  64.8 7.2 %prompt_prob.1.prob_hbm = f32[16,256,384]{2,1,0:T(8,128)S(1)} custom-call(s32[4]{0:T(128)S(1)} %copy-done.12, s32[16]{0:T(128)S(1)} %get-tuple-element.68.ks, s32[16]{0:T(128)S(1)} %get-tuple-element.67.vs, bf16[16,256,128]{2,1,0:T(8,128)(2,1)} %all-to-all-done.q_ref.stash_in, bf16[4,448,128]{2,1,0:T(8,128)(2,1)S(1)} %pad_maximum_fusion.refs_0_, ...), custom_call_target="tpu_custom_call" | custom-call | flops 8999999488 | tf_op jit(solution)/shard_map/prompt_prob/pallas_call | solution.py:202
  72.0 0.7 prompt_chain.4
  72.7 2.0 copy-done.17
  74.7 0.8 collective-permute-start.13
  75.6 9.9 %response_prob.1.prob_hbm = f32[16,192,640]{2,1,0:T(8,128)S(1)} custom-call(s32[4]{0:T(128)S(1)} %copy-done.12, s32[16]{0:T(128)S(1)} %get-tuple-element.68.ks, s32[16]{0:T(128)S(1)} %get-tuple-element.67.vs, bf16[16,192,128]{2,1,0:T(8,128)(2,1)} %all-to-all-done.1.q_ref.stash_in, bf16[4,448,128]{2,1,0:T(8,128)(2,1)S(1)} %pad_maximum_fusion.refs_0_, ...), custom_call_target="tpu_custom_call" | custom-call | flops 8999999488 | tf_op jit(solution)/shard_map/response_prob/pallas_call | solution.py:202
  85.5 0.7 response_chain.4
  86.2 3.2 %copy-done.13 = f32[16,192,640]{2,1,0:T(8,128)} copy-done((f32[16,192,640]{2,1,0:T(8,128)}, f32[16,192,640]{2,1,0:T(8,128)S(1)}, u32[]{:S(2)}) %copy-start.13) | copy-done | bytes 7864344
  89.5 1.6 copy-done.18
  93.2 3.2 %copy-done.14 = f32[16,192,640]{2,1,0:T(8,128)S(1)} copy-done((f32[16,192,640]{2,1,0:T(8,128)S(1)}, f32[16,192,640]{2,1,0:T(8,128)}, u32[]{:S(2)}) %copy-start.14) | copy-done | bytes 7864344
  97.2 2.8 %copy-done.19 = f32[16,256,384]{2,1,0:T(8,128)S(1)} copy-done((f32[16,256,384]{2,1,0:T(8,128)S(1)}, f32[16,256,384]{2,1,0:T(8,128)}, u32[]{:S(2)}) %copy-start.19) | copy-done | bytes 6291480
  100.6 1.3 collective-permute-start.16
  102.6 20.5 %collective-permute-done.16.g_in = bf16[256,128]{1,0:T(8,128)(2,1)S(1)} collective-permute-done((bf16[256,128]{1,0:T(8,128)(2,1)S(1)}, bf16[256,128]{1,0:T(8,128)(2,1)S(1)}, u32[]{:S(2)}, u32[]{:S(2)}) %collective-permute-start.16) | collective-permute-done | bytes 65568 | tf_op jit(solution)/shard_map/ppermute | solution.py:462
  123.2 3.2 %copy-done.15 = f32[16,192,640]{2,1,0:T(8,128)S(1)} copy-done((f32[16,192,640]{2,1,0:T(8,128)S(1)}, f32[16,192,640]{2,1,0:T(8,128)}, u32[]{:S(2)}) %copy-start.15) | copy-done | bytes 7864344
  127.1 1.3 collective-permute-start.17
  128.5 2.8 %copy-done.20 = f32[16,256,384]{2,1,0:T(8,128)S(1)} copy-done((f32[16,256,384]{2,1,0:T(8,128)S(1)}, f32[16,256,384]{2,1,0:T(8,128)}, u32[]{:S(2)}) %copy-start.20) | copy-done | bytes 6291480
  131.2 8.4 %prompt_chain.7 = (bf16[256,128]{1,0:T(8,128)(2,1)}, bf16[16,256,128]{2,1,0:T(8,128)(2,1)}) custom-call(s32[1]{0:T(128)} %bitcast.4.active, s32[16]{0:T(128)S(1)} %get-tuple-element.68.ks, s32[16]{0:T(128)S(1)} %get-tuple-element.67.vs, bf16[256,128]{1,0:T(8,128)(2,1)S(1)} %collective-permute-done.16.g_in, ...), custom_call_target="tpu_custom_call", output_to_operand_aliasing={{1}: (4, {})} | custom-call | flops 8000000000 | tf_op jit(solution)/shard_map/prompt_chain/pallas_call | solution.py:285
  139.6 9.2 %collective-permute-done.17.g_in = bf16[192,128]{1,0:T(8,128)(2,1)S(1)} collective-permute-done((bf16[192,128]{1,0:T(8,128)(2,1)S(1)}, bf16[192,128]{1,0:T(8,128)(2,1)S(1)}, u32[]{:S(2)}, u32[]{:S(2)}) %collective-permute-start.17) | collective-permute-done | bytes 49184 | tf_op jit(solution)/shard_map/ppermute | solution.py:470
  148.9 4.1 %all-to-all-start.3 = ((bf16[16,256,128]{2,1,0:T(8,128)(2,1)}), bf16[16,256,128]{2,1,0:T(8,128)(2,1)S(1)}, u32[]{:S(2)}, u32[]{:S(2)}) async-start(bf16[16,256,128]{2,1,0:T(8,128)(2,1)} %get-tuple-element.64), calls=%async_computation.3 | async-start | bytes 2097152 | tf_op jit(solution)/shard_map/all_to_all | solution.py:447
  153.0 1.0 copy-done.5
  154.0 1.0 copy-done.7
  155.0 1.0 copy-done.9
  156.1 1.0 copy-done.11
  157.1 3.2 %copy-done.16 = f32[16,192,640]{2,1,0:T(8,128)S(1)} copy-done((f32[16,192,640]{2,1,0:T(8,128)S(1)}, f32[16,192,640]{2,1,0:T(8,128)}, u32[]{:S(2)}) %copy-start.16) | copy-done | bytes 7864344
  160.3 10.9 %response_chain.7 = (bf16[192,128]{1,0:T(8,128)(2,1)}, bf16[16,192,128]{2,1,0:T(8,128)(2,1)}) custom-call(s32[1]{0:T(128)} %bitcast.4.active, s32[16]{0:T(128)S(1)} %get-tuple-element.68.ks, s32[16]{0:T(128)S(1)} %get-tuple-element.67.vs, bf16[192,128]{1,0:T(8,128)(2,1)S(1)} %collective-permute-done.17.g_in, ...), custom_call_target="tpu_custom_call", output_to_operand_aliasing={{1}: (4, {})} | custom-call | flops 8000000000 | tf_op jit(solution)/shard_map/response_chain/pallas_call | solution.py:285
  171.2 6.7 %all-to-all-start.2 = ((bf16[16,192,128]{2,1,0:T(8,128)(2,1)}), bf16[16,192,128]{2,1,0:T(8,128)(2,1)}, u32[]{:S(2)}, u32[]{:S(2)}) async-start(bf16[16,192,128]{2,1,0:T(8,128)(2,1)} %get-tuple-element.63), calls=%async_computation.2 | async-start | bytes 1572864 | tf_op jit(solution)/shard_map/all_to_all | solution.py:447
  178.0 6.2 %prompt_grad.1.part_ref = f32[256,256]{1,0:T(8,128)S(1)} custom-call(bf16[16,256,128]{2,1,0:T(8,128)(2,1)S(1)} %copy-done, bf16[16,256,128]{2,1,0:T(8,128)(2,1)S(1)} %all-to-all-done.3.g_ref, bf16[448,128]{1,0:T(8,128)(2,1)S(1)} %copy-done.2, bf16[448,128]{1,0:T(8,128)(2,1)S(1)} %copy-done.3), custom_call_target="tpu_custom_call" | custom-call | flops 8000000000 | tf_op jit(solution)/shard_map/prompt_grad/pallas_call | solution.py:335
  184.9 3.5 %all-to-all-done.2.g_ref = bf16[16,192,128]{2,1,0:T(8,128)(2,1)} async-done(((bf16[16,192,128]{2,1,0:T(8,128)(2,1)}), bf16[16,192,128]{2,1,0:T(8,128)(2,1)}, u32[]{:S(2)}, u32[]{:S(2)}) %all-to-all-start.2) | async-done | bytes 786464 | tf_op jit(solution)/shard_map/all_to_all | solution.py:447
  188.4 0.9 copy-done.24
  189.3 10.5 %response_grad.1 = (f32[512,256]{1,0:T(8,128)S(1)}, f32[1,128]{1,0:T(1,128)S(1)}) custom-call(s32[4]{0:T(128)S(1)} %copy-done.12, bf16[16,192,128]{2,1,0:T(8,128)(2,1)S(1)} %copy-done.1, bf16[16,192,128]{2,1,0:T(8,128)(2,1)} %all-to-all-done.2.g_ref, bf16[448,128]{1,0:T(8,128)(2,1)S(1)} %copy-done.2, bf16[448,128]{1,0:T(8,128)(2,1)S(1)} %copy-done.3, ...), custom_call_target="tpu_custom_call" | custom-call | flops 11000000512 | tf_op jit(solution)/shard_map/response_grad/pallas_call | solution.py:398
  199.8 9.5 %all_to_all.32 = f32[16,1,128]{2,1,0:T(1,128)S(1)} all-to-all(f32[16,1,128]{2,1,0:T(1,128)S(1)} %broadcast_in_dim.20), channel_id=1, replica_groups=mesh['zl'=4,'x'=4,'y'=4,'tp'=4] {'x','y'}, dimensions={0} | all-to-all | bytes 16384 | tf_op jit(solution)/shard_map/all_to_all | solution.py:475
  209.3 31.4 %all_to_all.33 = f32[16,1,128]{2,1,0:T(1,128)S(1)} all-to-all(f32[16,1,128]{2,1,0:T(1,128)S(1)} %broadcast_in_dim.21), channel_id=1, replica_groups=mesh['zl'=4,'x'=4,'y'=4,'tp'=4] {'zl','tp'}, dimensions={0} | all-to-all | bytes 16384 | tf_op jit(solution)/shard_map/all_to_all | solution.py:475
  242.0 0.8 multiply_bitcast_fusion
  (69 shorter events, 7.5 us)
Async XLA Ops:
  0.0 64.8 %copy-start.12 = (s32[4]{0:T(128)S(1)}, s32[4]{0:T(128)}, u32[]{:S(2)}) copy-start(s32[4]{0:T(128)} %lens.7) | copy-start | bytes 52
  4.0 10.6 %collective-permute-start.6 = (bf16[448,128]{1,0:T(8,128)(2,1)}, bf16[448,128]{1,0:T(8,128)(2,1)S(1)}, u32[]{:S(2)}, u32[]{:S(2)}) collective-permute-start(bf16[448,128]{1,0:T(8,128)(2,1)} %get-tuple-element.41.v_ref), channel_id=1, source_target_pairs={{0,16},{16,32},{32,48},{48,0},{1,17},{17,33},{33,49},{49,1},{2,18}... | collective-permute-start | bytes 344072 | tf_op jit(solution)/shard_map/ppermute | solution.py:425
  6.1 8.5 %collective-permute-start.7 = (bf16[448,128]{1,0:T(8,128)(2,1)}, bf16[448,128]{1,0:T(8,128)(2,1)S(1)}, u32[]{:S(2)}, u32[]{:S(2)}) collective-permute-start(bf16[448,128]{1,0:T(8,128)(2,1)} %get-tuple-element.41.v_ref), channel_id=1, source_target_pairs={{0,48},{16,0},{32,16},{48,32},{1,49},{17,1},{33,17},{49,33},{2,50}... | collective-permute-start | bytes 344072 | tf_op jit(solution)/shard_map/ppermute | solution.py:425
  7.4 7.2 %collective-permute-start.8 = (bf16[448,128]{1,0:T(8,128)(2,1)}, bf16[448,128]{1,0:T(8,128)(2,1)S(1)}, u32[]{:S(2)}, u32[]{:S(2)}) collective-permute-start(bf16[448,128]{1,0:T(8,128)(2,1)} %get-tuple-element.41.v_ref), channel_id=1, source_target_pairs={{0,32},{16,48},{32,0},{48,16},{1,33},{17,49},{33,1},{49,17},{2,34}... | collective-permute-start | bytes 344072 | tf_op jit(solution)/shard_map/ppermute | solution.py:425
  9.1 37.7 %all-to-all-start = ((bf16[16,256,128]{2,1,0:T(8,128)(2,1)}), bf16[16,256,128]{2,1,0:T(8,128)(2,1)}, u32[]{:S(2)}, u32[]{:S(2)}) async-start(bf16[16,256,128]{2,1,0:T(8,128)(2,1)} %get-tuple-element.39.q_ref), calls=%async_computation | async-start | bytes 2097152 | tf_op jit(solution)/shard_map/all_to_all | solution.py:447
  15.6 29.3 %collective-permute-start.10 = (bf16[4,448,128]{2,1,0:T(8,128)(2,1)S(1)}, bf16[4,448,128]{2,1,0:T(8,128)(2,1)S(1)}, u32[]{:S(2)}, u32[]{:S(2)}) collective-permute-start(bf16[4,448,128]{2,1,0:T(8,128)(2,1)S(1)} %pad_maximum_fusion.1.refs_4_), channel_id=1, source_target_pairs={{0,12},{4,0},{8,4},{12,8},{1,13},{5,1},{9,5},{13,9},{2,14},{6,2},{... | collective-permute-start | bytes 1376264 | tf_op jit(solution)/shard_map/ppermute | solution.py:425
  18.2 22.0 %collective-permute-start.1 = (bf16[448,128]{1,0:T(8,128)(2,1)}, bf16[448,128]{1,0:T(8,128)(2,1)S(1)}, u32[]{:S(2)}, u32[]{:S(2)}) collective-permute-start(bf16[448,128]{1,0:T(8,128)(2,1)} %get-tuple-element.40.k_ref), channel_id=1, source_target_pairs={{0,12},{4,0},{8,4},{12,8},{1,13},{5,1},{9,5},{13,9},{2,14},{6,2},{... | collective-permute-start | bytes 344072 | tf_op jit(solution)/shard_map/ppermute | solution.py:425
  18.7 21.7 %collective-permute-start.2 = (bf16[448,128]{1,0:T(8,128)(2,1)}, bf16[448,128]{1,0:T(8,128)(2,1)S(1)}, u32[]{:S(2)}, u32[]{:S(2)}) collective-permute-start(bf16[448,128]{1,0:T(8,128)(2,1)} %get-tuple-element.40.k_ref), channel_id=1, source_target_pairs={{0,8},{4,12},{8,0},{12,4},{1,9},{5,13},{9,1},{13,5},{2,10},{6,14},... | collective-permute-start | bytes 344072 | tf_op jit(solution)/shard_map/ppermute | solution.py:425
  18.9 21.6 %collective-permute-start = (bf16[448,128]{1,0:T(8,128)(2,1)}, bf16[448,128]{1,0:T(8,128)(2,1)S(1)}, u32[]{:S(2)}, u32[]{:S(2)}) collective-permute-start(bf16[448,128]{1,0:T(8,128)(2,1)} %get-tuple-element.40.k_ref), channel_id=1, source_target_pairs={{0,4},{4,8},{8,12},{12,0},{1,5},{5,9},{9,13},{13,1},{2,6},{6,10},{... | collective-permute-start | bytes 344072 | tf_op jit(solution)/shard_map/ppermute | solution.py:425
  19.6 33.6 %collective-permute-start.11 = (bf16[4,448,128]{2,1,0:T(8,128)(2,1)S(1)}, bf16[4,448,128]{2,1,0:T(8,128)(2,1)S(1)}, u32[]{:S(2)}, u32[]{:S(2)}) collective-permute-start(bf16[4,448,128]{2,1,0:T(8,128)(2,1)S(1)} %pad_maximum_fusion.1.refs_4_), channel_id=1, source_target_pairs={{0,8},{4,12},{8,0},{12,4},{1,9},{5,13},{9,1},{13,5},{2,10},{6,14},... | collective-permute-start | bytes 1376264 | tf_op jit(solution)/shard_map/ppermute | solution.py:425
  40.1 13.1 %collective-permute-start.9 = (bf16[4,448,128]{2,1,0:T(8,128)(2,1)S(1)}, bf16[4,448,128]{2,1,0:T(8,128)(2,1)S(1)}, u32[]{:S(2)}, u32[]{:S(2)}) collective-permute-start(bf16[4,448,128]{2,1,0:T(8,128)(2,1)S(1)} %pad_maximum_fusion.1.refs_4_), channel_id=1, source_target_pairs={{0,4},{4,8},{8,12},{12,0},{1,5},{5,9},{9,13},{13,1},{2,6},{6,10},{... | collective-permute-start | bytes 1376264 | tf_op jit(solution)/shard_map/ppermute | solution.py:425
  41.4 11.8 %collective-permute-start.3 = (bf16[4,448,128]{2,1,0:T(8,128)(2,1)S(1)}, bf16[4,448,128]{2,1,0:T(8,128)(2,1)S(1)}, u32[]{:S(2)}, u32[]{:S(2)}) collective-permute-start(bf16[4,448,128]{2,1,0:T(8,128)(2,1)S(1)} %pad_maximum_fusion.refs_0_), channel_id=1, source_target_pairs={{0,16},{16,32},{32,48},{48,0},{1,17},{17,33},{33,49},{49,1},{2,18}... | collective-permute-start | bytes 1376264 | tf_op jit(solution)/shard_map/ppermute | solution.py:425
  43.3 10.1 %collective-permute-start.4 = (bf16[4,448,128]{2,1,0:T(8,128)(2,1)S(1)}, bf16[4,448,128]{2,1,0:T(8,128)(2,1)}, u32[]{:S(2)}, u32[]{:S(2)}) collective-permute-start(bf16[4,448,128]{2,1,0:T(8,128)(2,1)S(1)} %pad_maximum_fusion.refs_0_), channel_id=1, source_target_pairs={{0,48},{16,0},{32,16},{48,32},{1,49},{17,1},{33,17},{49,33},{2,50}... | collective-permute-start | bytes 1376264 | tf_op jit(solution)/shard_map/ppermute | solution.py:425
  44.8 83.6 %copy-start.4 = (bf16[4,448,128]{2,1,0:T(8,128)(2,1)}, bf16[4,448,128]{2,1,0:T(8,128)(2,1)S(1)}, u32[]{:S(2)}) copy-start(bf16[4,448,128]{2,1,0:T(8,128)(2,1)S(1)} %collective-permute-done.10.refs_6_) | copy-start | bytes 1376260
  44.8 19.9 %collective-permute-start.5 = (bf16[4,448,128]{2,1,0:T(8,128)(2,1)S(1)}, bf16[4,448,128]{2,1,0:T(8,128)(2,1)}, u32[]{:S(2)}, u32[]{:S(2)}) collective-permute-start(bf16[4,448,128]{2,1,0:T(8,128)(2,1)S(1)} %pad_maximum_fusion.refs_0_), channel_id=1, source_target_pairs={{0,32},{16,48},{32,0},{48,16},{1,33},{17,49},{33,1},{49,17},{2,34}... | collective-permute-start | bytes 1376264 | tf_op jit(solution)/shard_map/ppermute | solution.py:425
  46.8 28.8 %all-to-all-start.1 = ((bf16[16,192,128]{2,1,0:T(8,128)(2,1)}), bf16[16,192,128]{2,1,0:T(8,128)(2,1)}, u32[]{:S(2)}, u32[]{:S(2)}) async-start(bf16[16,192,128]{2,1,0:T(8,128)(2,1)} %get-tuple-element.44.q_ref), calls=%async_computation.1 | async-start | bytes 1572864 | tf_op jit(solution)/shard_map/all_to_all | solution.py:447
  53.2 75.2 %copy-start.6 = (bf16[4,448,128]{2,1,0:T(8,128)(2,1)}, bf16[4,448,128]{2,1,0:T(8,128)(2,1)S(1)}, u32[]{:S(2)}) copy-start(bf16[4,448,128]{2,1,0:T(8,128)(2,1)S(1)} %collective-permute-done.11.refs_7_) | copy-start | bytes 1376260
  53.2 75.2 %copy-start.8 = (bf16[4,448,128]{2,1,0:T(8,128)(2,1)}, bf16[4,448,128]{2,1,0:T(8,128)(2,1)S(1)}, u32[]{:S(2)}) copy-start(bf16[4,448,128]{2,1,0:T(8,128)(2,1)S(1)} %collective-permute-done.9.refs_5_) | copy-start | bytes 1376260
  53.3 75.2 %copy-start.10 = (bf16[4,448,128]{2,1,0:T(8,128)(2,1)}, bf16[4,448,128]{2,1,0:T(8,128)(2,1)S(1)}, u32[]{:S(2)}) copy-start(bf16[4,448,128]{2,1,0:T(8,128)(2,1)S(1)} %collective-permute-done.3.refs_1_) | copy-start | bytes 1376260
  64.8 7.2 %copy-start.21 = (bf16[256,128]{1,0:T(8,128)(2,1)S(1)}, bf16[256,128]{1,0:T(8,128)(2,1)}, u32[]{:S(2)}) copy-start(bf16[256,128]{1,0:T(8,128)(2,1)} %get-tuple-element.38.g_in) | copy-start | bytes 196612
  72.0 2.7 %copy-start.17 = (f32[16,256,384]{2,1,0:T(8,128)}, f32[16,256,384]{2,1,0:T(8,128)S(1)}, u32[]{:S(2)}) copy-start(f32[16,256,384]{2,1,0:T(8,128)S(1)} %prompt_prob.1.prob_hbm) | copy-start | bytes 18874372
  74.7 14.8 %collective-permute-start.13 = (bf16[256,128]{1,0:T(8,128)(2,1)S(1)}, bf16[256,128]{1,0:T(8,128)(2,1)S(1)}, u32[]{:S(2)}, u32[]{:S(2)}) collective-permute-start(bf16[256,128]{1,0:T(8,128)(2,1)S(1)} %get-tuple-element.42), channel_id=1, source_target_pairs={{192,128},{193,129},{194,130},{195,131},{196,132},{197,133},{198,1... | collective-permute-start | bytes 196616 | tf_op jit(solution)/shard_map/ppermute | solution.py:462
  75.5 9.9 %copy-start.22 = (bf16[192,128]{1,0:T(8,128)(2,1)S(1)}, bf16[192,128]{1,0:T(8,128)(2,1)}, u32[]{:S(2)}) copy-start(bf16[192,128]{1,0:T(8,128)(2,1)} %get-tuple-element.43.g_in) | copy-start | bytes 147460
  85.5 4.0 %copy-start.13 = (f32[16,192,640]{2,1,0:T(8,128)}, f32[16,192,640]{2,1,0:T(8,128)S(1)}, u32[]{:S(2)}) copy-start(f32[16,192,640]{2,1,0:T(8,128)S(1)} %response_prob.1.prob_hbm) | copy-start | bytes 23592964
  85.5 5.6 %copy-start.18 = (f32[16,256,384]{2,1,0:T(8,128)S(1)}, f32[16,256,384]{2,1,0:T(8,128)}, u32[]{:S(2)}) copy-start(f32[16,256,384]{2,1,0:T(8,128)} %copy-done.17) | copy-start | bytes 18874372
  91.8 1.4 collective-permute-start.14
  92.5 0.7 collective-permute-start.12
  93.2 3.2 %copy-start.14 = (f32[16,192,640]{2,1,0:T(8,128)S(1)}, f32[16,192,640]{2,1,0:T(8,128)}, u32[]{:S(2)}) copy-start(f32[16,192,640]{2,1,0:T(8,128)} %copy-done.13) | copy-start | bytes 23592964
  97.1 2.8 %copy-start.19 = (f32[16,256,384]{2,1,0:T(8,128)S(1)}, f32[16,256,384]{2,1,0:T(8,128)}, u32[]{:S(2)}) copy-start(f32[16,256,384]{2,1,0:T(8,128)} %copy-done.17) | copy-start | bytes 18874372
  100.6 22.5 %collective-permute-start.16 = (bf16[256,128]{1,0:T(8,128)(2,1)S(1)}, bf16[256,128]{1,0:T(8,128)(2,1)S(1)}, u32[]{:S(2)}, u32[]{:S(2)}) collective-permute-start(bf16[256,128]{1,0:T(8,128)(2,1)S(1)} %get-tuple-element.54), channel_id=1, source_target_pairs={{64,0},{65,1},{66,2},{67,3},{68,4},{69,5},{70,6},{71,7},{72,8},{73... | collective-permute-start | bytes 196616 | tf_op jit(solution)/shard_map/ppermute | solution.py:462
  101.9 0.7 collective-permute-start.15
  123.2 3.2 %copy-start.15 = (f32[16,192,640]{2,1,0:T(8,128)S(1)}, f32[16,192,640]{2,1,0:T(8,128)}, u32[]{:S(2)}) copy-start(f32[16,192,640]{2,1,0:T(8,128)} %copy-done.13) | copy-start | bytes 23592964
  127.1 21.8 %collective-permute-start.17 = (bf16[192,128]{1,0:T(8,128)(2,1)S(1)}, bf16[192,128]{1,0:T(8,128)(2,1)S(1)}, u32[]{:S(2)}, u32[]{:S(2)}) collective-permute-start(bf16[192,128]{1,0:T(8,128)(2,1)S(1)} %get-tuple-element.57), channel_id=1, source_target_pairs={{64,0},{65,1},{66,2},{67,3},{68,4},{69,5},{70,6},{71,7},{72,8},{73... | collective-permute-start | bytes 147464 | tf_op jit(solution)/shard_map/ppermute | solution.py:470
  128.5 2.8 %copy-start.20 = (f32[16,256,384]{2,1,0:T(8,128)S(1)}, f32[16,256,384]{2,1,0:T(8,128)}, u32[]{:S(2)}) copy-start(f32[16,256,384]{2,1,0:T(8,128)} %copy-done.17) | copy-start | bytes 18874372
  148.9 22.4 %all-to-all-start.3 = ((bf16[16,256,128]{2,1,0:T(8,128)(2,1)}), bf16[16,256,128]{2,1,0:T(8,128)(2,1)S(1)}, u32[]{:S(2)}, u32[]{:S(2)}) async-start(bf16[16,256,128]{2,1,0:T(8,128)(2,1)} %get-tuple-element.64), calls=%async_computation.3 | async-start | bytes 2097152 | tf_op jit(solution)/shard_map/all_to_all | solution.py:447
  153.0 1.0 copy-start.5
  154.0 1.0 copy-start.7
  155.0 1.0 copy-start.9
  156.1 1.0 copy-start.11
  157.1 3.2 %copy-start.16 = (f32[16,192,640]{2,1,0:T(8,128)S(1)}, f32[16,192,640]{2,1,0:T(8,128)}, u32[]{:S(2)}) copy-start(f32[16,192,640]{2,1,0:T(8,128)} %copy-done.13) | copy-start | bytes 23592964
  160.3 17.7 %copy-start = (bf16[16,256,128]{2,1,0:T(8,128)(2,1)S(1)}, bf16[16,256,128]{2,1,0:T(8,128)(2,1)}, u32[]{:S(2)}) copy-start(bf16[16,256,128]{2,1,0:T(8,128)(2,1)} %get-tuple-element.39.q_ref) | copy-start | bytes 3145732
  160.3 17.7 %copy-start.2 = (bf16[448,128]{1,0:T(8,128)(2,1)S(1)}, bf16[448,128]{1,0:T(8,128)(2,1)}, u32[]{:S(2)}) copy-start(bf16[448,128]{1,0:T(8,128)(2,1)} %get-tuple-element.40.k_ref) | copy-start | bytes 344068
  160.3 17.7 %copy-start.3 = (bf16[448,128]{1,0:T(8,128)(2,1)S(1)}, bf16[448,128]{1,0:T(8,128)(2,1)}, u32[]{:S(2)}) copy-start(bf16[448,128]{1,0:T(8,128)(2,1)} %get-tuple-element.41.v_ref) | copy-start | bytes 344068
  171.2 17.1 %all-to-all-start.2 = ((bf16[16,192,128]{2,1,0:T(8,128)(2,1)}), bf16[16,192,128]{2,1,0:T(8,128)(2,1)}, u32[]{:S(2)}, u32[]{:S(2)}) async-start(bf16[16,192,128]{2,1,0:T(8,128)(2,1)} %get-tuple-element.63), calls=%async_computation.2 | async-start | bytes 1572864 | tf_op jit(solution)/shard_map/all_to_all | solution.py:447
  178.0 10.4 %copy-start.1 = (bf16[16,192,128]{2,1,0:T(8,128)(2,1)S(1)}, bf16[16,192,128]{2,1,0:T(8,128)(2,1)}, u32[]{:S(2)}) copy-start(bf16[16,192,128]{2,1,0:T(8,128)(2,1)} %get-tuple-element.44.q_ref) | copy-start | bytes 2359300
  184.2 0.7 copy-start.23
  188.4 1.0 copy-start.24

commit v4 on v3

v4 whole, which is shorter than its diff:
```python
import functools
import math

import jax
import jax.numpy as jnp
from jax import lax
from jax.experimental import pallas as pl
from jax.experimental.pallas import tpu as pltpu
from jax.sharding import Mesh, PartitionSpec as P

HD = 128
PROMPT = 256
NRESP = 4
RLEN = 64
RESP = 192
LIVE = PROMPT + RESP
STAGES = 4
SIDE = 4
PLANE = SIDE * SIDE

clip_rms = 0.5
SCALE = 1.0 / math.sqrt(HD)
EXP2_SCALE = SCALE * math.log2(math.e)
f32 = jnp.float32
bf16 = jnp.bfloat16


def dot(a, b):
    return lax.dot_general(a, b, (((1,), (0,)), ((), ())), preferred_element_type=f32)


def dot_nt(a, b):
    return lax.dot_general(a, b, (((1,), (1,)), ((), ())), preferred_element_type=f32)


def about(us):
    return pl.CostEstimate(flops=us * 1_000_000_000, bytes_accessed=0, transcendentals=0)


def params(mebibytes=24):
    return pltpu.CompilerParams(vmem_limit_bytes=mebibytes << 20)


def shape(dims, dtype=f32):
    return jax.ShapeDtypeStruct(dims, dtype)


def starts(lens):
    first = lens[0]
    second = first + lens[1]
    return first, second, second + lens[2]


def start_of(row, lens):
    one, two, three = starts(lens)
    return jnp.where(
        row >= three, three, jnp.where(row >= two, two, jnp.where(row >= one, one, 0))
    )


def prompt_bias(query_dim):
    q = lax.broadcasted_iota(jnp.int32, (PROMPT, PROMPT), query_dim)
    k = lax.broadcasted_iota(jnp.int32, (PROMPT, PROMPT), 1 - query_dim)
    return jnp.where(k <= q, 0.0, -jnp.inf).astype(f32)


def response_bias(lens, query_dim):
    q = lax.broadcasted_iota(jnp.int32, (RESP, RESP), query_dim)
    k = lax.broadcasted_iota(jnp.int32, (RESP, RESP), 1 - query_dim)
    return jnp.where((k <= q) & (k >= start_of(q, lens)), 0.0, -jnp.inf).astype(f32)


def chosen_rows(lens, row_dim):
    dims = (RESP, NRESP * RLEN) if row_dim == 0 else (NRESP * RLEN, RESP)
    row = lax.broadcasted_iota(jnp.int32, dims, row_dim)
    col = lax.broadcasted_iota(jnp.int32, dims, 1 - row_dim)
    one, two, three = starts(lens)
    slot = (
        (row >= one).astype(jnp.int32)
        + (row >= two).astype(jnp.int32)
        + (row >= three).astype(jnp.int32)
    )
    return jnp.where(col == slot * RLEN + row - start_of(row, lens), 1.0, 0.0).astype(bf16)


def pack_kernel(lens, place, x_ref, top_ref, key_ref, value_ref, xp_out, xr_out, tp_out, tr_out, k_out, v_out, chosen):
    @pl.when(pl.program_id(0) == 0)
    def _():
        pick = chosen_rows(lens, 0)
        chosen[...] = pick
        tp_out[...] = top_ref[:PROMPT]
        tr_out[...] = dot(pick, top_ref[PROMPT:]).astype(bf16)
        for ref, out in ((key_ref, k_out), (value_ref, v_out)):
            out[:PROMPT] = ref[:PROMPT]
            out[PROMPT:] = dot(pick, ref[PROMPT:]).astype(bf16)

    live = dot(chosen[...], x_ref[PROMPT:]).astype(bf16)
    for h in range(x_ref.shape[1] // HD):
        cols = slice(h * HD, (h + 1) * HD)
        xp_out[h] = x_ref[:PROMPT, cols]
        xr_out[h] = live[:, cols]


def pack(lens, place, x, top, key, value):
    rows, width = x.shape
    heads = width // HD
    steps = 2
    some = heads // steps
    whole = lambda *dims: pl.BlockSpec(dims, lambda i, l, p: (0,) * len(dims))
    return pl.pallas_call(
        pack_kernel,
        name="pack",
        cost_estimate=about(4),
        grid_spec=pltpu.PrefetchScalarGridSpec(
            num_scalar_prefetch=2,
            grid=(steps,),
            in_specs=[
                pl.BlockSpec((rows, some * HD), lambda i, l, p: (0, i)),
                pl.BlockSpec((rows, HD), lambda i, l, p: (0, p[0])),
                whole(rows, HD),
                whole(rows, HD),
            ],
            out_specs=[
                pl.BlockSpec((some, PROMPT, HD), lambda i, l, p: (i, 0, 0)),
                pl.BlockSpec((some, RESP, HD), lambda i, l, p: (i, 0, 0)),
                whole(PROMPT, HD),
                whole(RESP, HD),
                whole(LIVE, HD),
                whole(LIVE, HD),
            ],
            scratch_shapes=[pltpu.VMEM((RESP, NRESP * RLEN), bf16)],
        ),
        out_shape=[
            shape((heads, PROMPT, HD), bf16),
            shape((heads, RESP, HD), bf16),
            shape((PROMPT, HD), bf16),
            shape((RESP, HD), bf16),
            shape((LIVE, HD), bf16),
            shape((LIVE, HD), bf16),
        ],
        compiler_params=params(60),
    )(lens, place, x, top, key, value)


def softmax(scores, dim):
    top = functools.reduce(jnp.maximum, [jnp.max(x, dim, keepdims=True) for x in scores])
    weights = [jnp.exp2((x - top) * EXP2_SCALE) for x in scores]
    total = functools.reduce(jnp.add, [jnp.sum(w, dim, keepdims=True) for w in weights])
    share = 1.0 / total
    return [w * share for w in weights]


AT_ONCE = 4
PROMPT_ROW = PROMPT + HD
RESP_ROW = 2 * PROMPT + HD
VMEM = pl.BlockSpec(memory_space=pltpu.VMEM)
SMEM = pl.BlockSpec(memory_space=pltpu.SMEM)
HBM = pl.BlockSpec(memory_space=pltpu.HBM)


def kept(x):
    return pltpu.with_memory_space_constraint(x, pltpu.VMEM)


def in_hbm(x):
    return pltpu.with_memory_space_constraint(x, pltpu.HBM)


def prob_kernel(prompt, lens, k_from, v_from, q_ref, *refs):
    half = (len(refs) - 9) // 2
    k_parts, v_parts = refs[:half], refs[half : 2 * half]
    probs_out, keys_out, values_out, probs, keys, values, bias, sems, kv_sems = refs[2 * half :]
    n, count, _ = keys.shape
    bias[...] = prompt_bias(0) if prompt else response_bias(lens, 0)
    for parts, held, table in ((k_parts, keys, k_from), (v_parts, values, v_from)):
        at = 0
        for part in parts:
            for i in range(part.shape[0]):
                held[table[at]] = part[i, :count]
                at += 1
    ordered = [
        pltpu.make_async_copy(held, out, kv_sems.at[j])
        for j, (held, out) in enumerate(((keys, keys_out), (values, values_out)))
    ]
    for copy in ordered:
        copy.start()

    def done(i):
        some = pl.ds(i * AT_ONCE, AT_ONCE)
        return pltpu.make_async_copy(probs.at[some], probs_out.at[some], sems.at[i])

    def body(i, carry):
        for u in range(AT_ONCE):
            layer = i * AT_ONCE + u
            q, k, v = q_ref[layer], keys[layer], values[layer]
            if prompt:
                (p,) = softmax([dot_nt(q, k) + bias[...]], -1)
                probs[layer, :, :PROMPT] = p
                probs[layer, :, PROMPT:] = dot(p.astype(bf16), v)
            else:
                p1, p2 = softmax([dot_nt(q, k[:PROMPT]), dot_nt(q, k[PROMPT:]) + bias[...]], -1)
                probs[layer, :, :PROMPT] = p1
                probs[layer, :, PROMPT:LIVE] = p2
                probs[layer, :, 2 * PROMPT :] = dot(p1.astype(bf16), v[:PROMPT]) + dot(
                    p2.astype(bf16), v[PROMPT:]
                )
        done(i).start()
        return carry

    lax.fori_loop(0, n // AT_ONCE, body, 0)
    for copy in ordered + [done(i) for i in range(n // AT_ONCE)]:
        copy.wait()


def prob(prompt, lens, k_from, v_from, q, k, v):
    n, rows, _ = q.shape
    count, width = (PROMPT, PROMPT_ROW) if prompt else (LIVE, RESP_ROW)
    results = [((n, rows, width), f32), ((n, count, HD), bf16), ((n, count, HD), bf16)]
    return pl.pallas_call(
        functools.partial(prob_kernel, prompt),
        name="prompt_prob" if prompt else "response_prob",
        cost_estimate=about(7),
        in_specs=[SMEM] * 3 + [VMEM] * (1 + len(k) + len(v)),
        out_specs=[HBM] * 3,
        scratch_shapes=[pltpu.VMEM(*r) for r in results]
        + [
            pltpu.VMEM((rows, rows), f32),
            pltpu.SemaphoreType.DMA((n // AT_ONCE,)),
            pltpu.SemaphoreType.DMA((2,)),
        ],
        out_shape=[pltpu.HBM(*r) for r in results],
        compiler_params=params(22),
    )(lens, k_from, v_from, q, *k, *v)


GROUPS = ((15, 16), (14, 15), (12, 14), (8, 12), (4, 8), (0, 4))
AHEAD = 3


def chain_kernel(prompt, active, g_in, stash_in, probs_in, keys_in, values_in, g_out, stash, probs, keys, values, grads, sems, save_sems):
    n = keys.shape[0]

    def loads(j):
        span = pl.ds(GROUPS[j][0], GROUPS[j][1] - GROUPS[j][0])
        return [
            pltpu.make_async_copy(source.at[span], held.at[span], sems.at[j, i])
            for i, (source, held) in enumerate(
                ((values_in, values), (probs_in, probs), (keys_in, keys))
            )
        ]

    def step(layer):
        d = grads[layer]
        wide = d.astype(f32)
        k, v = keys[layer], values[layer]
        if prompt:
            delta = jnp.sum(wide * probs[layer, :, PROMPT:], -1, keepdims=True)
            ds = (probs[layer, :, :PROMPT] * (dot_nt(d, v) - delta)).astype(bf16)
            change = dot(ds, k)
        else:
            delta = jnp.sum(wide * probs[layer, :, 2 * PROMPT :], -1, keepdims=True)
            ds1 = (probs[layer, :, :PROMPT] * (dot_nt(d, v[:PROMPT]) - delta)).astype(bf16)
            ds2 = (probs[layer, :, PROMPT:LIVE] * (dot_nt(d, v[PROMPT:]) - delta)).astype(bf16)
            change = dot(ds1, k[:PROMPT]) + dot(ds2, k[PROMPT:])
        return (wide + change * SCALE).astype(bf16)

    def save(j):
        half = pl.ds(j * n // 2, n // 2)
        return pltpu.make_async_copy(grads.at[half], stash.at[half], save_sems.at[j])

    @pl.when(active[0] == 1)
    def _():
        for j in range(AHEAD):
            for copy in loads(j):
                copy.start()
        grads[n - 1] = g_in[...]
        for j, (low, high) in enumerate(GROUPS):
            for copy in loads(j):
                copy.wait()
            if j + AHEAD < len(GROUPS):
                for copy in loads(j + AHEAD):
                    copy.start()

            def body(i, carry, high=high):
                grads[high - 2 - i] = step(high - 1 - i)
                return carry

            if high - low == 1:
                body(0, 0)
            else:
                lax.fori_loop(0, high - max(low, 1), body, 0)
            if low == n // 2:
                save(1).start()
        save(0).start()
        g_out[...] = step(0)
        save(1).wait()
        save(0).wait()


def chain(prompt, active, g, stash, probs, k, v):
    n, rows, _ = probs.shape
    anywhere = pl.BlockSpec(memory_space=pl.ANY)
    return pl.pallas_call(
        functools.partial(chain_kernel, prompt),
        name="prompt_chain" if prompt else "response_chain",
        cost_estimate=about(7),
        in_specs=[SMEM, VMEM, anywhere] + [HBM] * 3,
        out_specs=[VMEM, anywhere],
        scratch_shapes=[
            pltpu.VMEM(probs.shape, f32),
            pltpu.VMEM(k.shape, bf16),
            pltpu.VMEM(v.shape, bf16),
            pltpu.VMEM((n, rows, HD), bf16),
            pltpu.SemaphoreType.DMA((len(GROUPS), 3)),
            pltpu.SemaphoreType.DMA((2,)),
        ],
        out_shape=[shape((rows, HD), bf16), shape((n, rows, HD), bf16)],
        input_output_aliases={2: 1},
        compiler_params=params(22),
    )(active, g, stash, in_hbm(probs), in_hbm(k), in_hbm(v))


HEADS_AT_ONCE = 2


def own_prob_kernel(prompt, lens, q_ref, k_ref, probs, bias):
    bias[...] = prompt_bias(1) if prompt else response_bias(lens, 1)
    k1, k2 = k_ref[:PROMPT], k_ref[PROMPT:]

    def body(i, carry):
        for u in range(AT_ONCE):
            head = i * AT_ONCE + u
            q = q_ref[head]
            if prompt:
                (probs[head],) = softmax([dot_nt(k1, q) + bias[...]], 0)
            else:
                p1, p2 = softmax([dot_nt(k1, q), dot_nt(k2, q) + bias[...]], 0)
                probs[head, :PROMPT] = p1
                probs[head, PROMPT:] = p2
        return carry

    lax.fori_loop(0, q_ref.shape[0] // AT_ONCE, body, 0)


def own_prob(prompt, lens, q, k):
    n, rows, _ = q.shape
    return pl.pallas_call(
        functools.partial(own_prob_kernel, prompt),
        name="own_prompt_prob" if prompt else "own_response_prob",
        cost_estimate=about(5),
        in_specs=[SMEM, VMEM, VMEM],
        out_specs=VMEM,
        scratch_shapes=[pltpu.VMEM((rows, rows), f32)],
        out_shape=pltpu.VMEM((n, PROMPT if prompt else LIVE, rows), f32),
        compiler_params=params(12),
    )(lens, q, k)


def response_grad_kernel(lens, probs, q_ref, g_ref, v_ref, prompt_out, out_ref, sum_ref, acc):
    acc[...] = jnp.zeros_like(acc)
    v1, v2 = v_ref[:PROMPT], v_ref[PROMPT:]

    def body(i, carry):
        dk1, dk2, dv1, dv2 = 0.0, 0.0, 0.0, 0.0
        for u in range(HEADS_AT_ONCE):
            head = i * HEADS_AT_ONCE + u
            q, g = q_ref[head], g_ref[head]
            p1, p2 = probs[head, :PROMPT], probs[head, PROMPT:]
            dp1, dp2 = dot_nt(v1, g), dot_nt(v2, g)
            pb1, pb2 = p1.astype(bf16), p2.astype(bf16)
            delta = jnp.sum(pb1.astype(f32) * dp1, 0, keepdims=True) + jnp.sum(
                pb2.astype(f32) * dp2, 0, keepdims=True
            )
            ds1 = (p1 * (dp1 - delta)).astype(bf16)
            ds2 = (p2 * (dp2 - delta)).astype(bf16)
            dk1, dk2 = dk1 + dot(ds1, q), dk2 + dot(ds2, q)
            dv1, dv2 = dv1 + dot(pb1, g), dv2 + dot(pb2, g)
        acc[:PROMPT, :HD] += dk1 * SCALE
        acc[PROMPT:, :HD] += dk2 * SCALE
        acc[:PROMPT, HD:] += dv1
        acc[PROMPT:, HD:] += dv2
        return carry

    lax.fori_loop(0, q_ref.shape[0] // HEADS_AT_ONCE, body, 0)
    prompt_out[...] = acc[:PROMPT]
    left = acc[PROMPT:]
    squares = jnp.sum(left * left, 0, keepdims=True)
    sum_ref[...] = squares[:, :HD] + squares[:, HD:]
    spread = chosen_rows(lens, 1)
    placed = jnp.zeros((NRESP * RLEN, 2 * HD), f32)
    for _ in range(3):
        term = left.astype(bf16)
        placed = placed + dot(spread, term)
        left = left - term.astype(f32)
    out_ref[...] = placed


def response_grad(lens, probs, q, g, v):
    return pl.pallas_call(
        response_grad_kernel,
        name="response_grad",
        cost_estimate=about(8),
        in_specs=[SMEM] + [VMEM] * 4,
        out_specs=[VMEM] * 3,
        scratch_shapes=[pltpu.VMEM((LIVE, 2 * HD), f32)],
        out_shape=[shape((PROMPT, 2 * HD)), shape((NRESP * RLEN, 2 * HD)), shape((1, HD))],
        compiler_params=params(12),
    )(lens, kept(probs), q, g, v)


def prompt_grad_kernel(probs, q_ref, g_ref, v_ref, part_ref, response_ref, squares_ref, out_ref, sum_ref, acc):
    acc[...] = part_ref[...]
    v = v_ref[:PROMPT]

    def body(i, carry):
        dk, dv = 0.0, 0.0
        for u in range(HEADS_AT_ONCE):
            head = i * HEADS_AT_ONCE + u
            q, g, p = q_ref[head], g_ref[head], probs[head]
            dp = dot_nt(v, g)
            pb = p.astype(bf16)
            delta = jnp.sum(pb.astype(f32) * dp, 0, keepdims=True)
            ds = (p * (dp - delta)).astype(bf16)
            dk = dk + dot(ds, q)
            dv = dv + dot(pb, g)
        acc[:, :HD] += dk * SCALE
        acc[:, HD:] += dv
        return carry

    lax.fori_loop(0, q_ref.shape[0] // HEADS_AT_ONCE, body, 0)
    total = acc[...]
    squares = jnp.sum(total * total, 0, keepdims=True)
    sum_ref[...] = squares_ref[...] + squares[:, :HD] + squares[:, HD:]
    out_ref[:PROMPT] = total
    out_ref[PROMPT:] = response_ref[...]


def prompt_grad(probs, q, g, v, part, response, squares):
    return pl.pallas_call(
        prompt_grad_kernel,
        name="prompt_grad",
        cost_estimate=about(5),
        in_specs=[VMEM] * 7,
        out_specs=[VMEM] * 2,
        scratch_shapes=[pltpu.VMEM((PROMPT, 2 * HD), f32)],
        out_shape=[shape((PROMPT + NRESP * RLEN, 2 * HD)), shape((1, HD))],
        compiler_params=params(12),
    )(kept(probs), q, g, v, part, response, squares)


def ring(step, size=SIDE):
    return [(i, (i + step) % size) for i in range(size)]


def gathered(block, axis):
    return [block] + [lax.ppermute(block, axis, ring(step)) for step in (1, -1, 2)]


def gathered_halves(block, axis):
    low, high = (lax.ppermute(block, axis, ring(step)) for step in (1, -1))
    half = block.shape[0] // 2
    return [
        block,
        low,
        high,
        lax.ppermute(low[:half], axis, ring(1)),
        lax.ppermute(high[half:], axis, ring(-1)),
    ]


def on_device(hidden_stash, key_stash, value_stash, top_grads, lens):
    stage = lax.axis_index("zl")
    my_x = lax.axis_index("x")
    my_y = lax.axis_index("y")
    place = (my_x * SIDE + my_y).reshape(1).astype(jnp.int32)
    qp, qr, gp, gr, k, v = pack(
        lens, place, hidden_stash[0], top_grads, key_stash[0], value_stash[0]
    )
    parts = jnp.arange(PLANE, dtype=jnp.int32)
    away = lambda slot: jnp.where(slot == 1, 3, jnp.where(slot == 2, 1, jnp.where(slot == 3, 2, 0)))
    outer, inner = away(parts // SIDE), away(parts % SIDE)
    k_from = ((my_x + outer) % SIDE * SIDE + (my_y + inner) % SIDE).astype(jnp.int32)
    v_from = ((my_x + inner) % SIDE * SIDE + (my_y + outer) % SIDE).astype(jnp.int32)
    plane = ("x", "y")
    swap = lambda a: lax.all_to_all(a, plane, 0, 0, tiled=True)
    after = lambda x, y: lax.optimization_barrier((x, y))[0]
    row_k = jnp.stack(gathered(k, "y"))
    col_v = jnp.stack(gathered(v, "x"))
    row_k, col_v, qp = lax.optimization_barrier((row_k, col_v, qp))
    my_qp = swap(qp)
    all_k = gathered_halves(row_k, "x")
    all_v = gathered_halves(col_v, "y")
    my_qr = swap(after(qr, my_qp))
    prob_p, key_p, value_p = prob(True, lens, k_from, v_from, my_qp, all_k, all_v)
    prob_r, key_r, value_r = prob(False, lens, k_from, v_from, my_qr, all_k, all_v)
    stash_p, stash_r = my_qp, my_qr
    for now in range(STAGES - 1, -1, -1):
        active = (stage == now).astype(jnp.int32).reshape(1)
        gp, stash_p = chain(True, active, gp, stash_p, prob_p, key_p, value_p)
        if now:
            sent = lax.ppermute(gp, "zl", [(now, now - 1)])
            gr = after(gr, gp if now == STAGES - 1 else sent)
            gp = sent
        else:
            gr, stash_p = lax.optimization_barrier((gr, stash_p))
        gr, stash_r = chain(False, active, gr, stash_r, prob_r, key_r, value_r)
        if now:
            gp = after(gp, gr)
            gr = lax.ppermute(gr, "zl", [(now, now - 1)])
    own_gr, own_gp = swap(stash_r), swap(after(stash_p, gr))
    qp, qr = after(qp, gr), after(qr, gr)
    own_r = own_prob(False, lens, qr, k)
    part, response, squares = response_grad(lens, own_r, qr, own_gr, v)
    own_p = own_prob(True, lens, qp, k)
    raw, squares = prompt_grad(own_p, qp, own_gp, v, part, response, squares)
    for axes, size in ((plane, PLANE), (("zl", "tp"), STAGES * lax.axis_size("tp"))):
        spread = jnp.broadcast_to(squares, (size, HD))
        squares = jnp.sum(lax.all_to_all(spread, axes, 0, 0, tiled=True), 0, keepdims=True)
    square_sum = jnp.sum(squares)
    entries = STAGES * PLANE * lax.axis_size("tp") * raw.shape[0] * raw.shape[1]
    clip_limit = clip_rms * math.sqrt(entries)
    factor = clip_limit / jnp.maximum(jnp.sqrt(square_sum), clip_limit)
    return (raw * factor)[None]


def solution(mesh):
    parts = mesh.devices.reshape(STAGES, SIDE, SIDE, -1)
    finer = Mesh(parts, ("zl", "x", "y", "tp"))
    pipe = ("zl", "x", "y")
    placed = (
        P(pipe, None, "tp"),
        P(pipe, None, "tp"),
        P(pipe, None, "tp"),
        P(None, "tp"),
        P(),
    )
    return jax.shard_map(
        on_device, mesh=finer, in_specs=placed, out_specs=P(pipe, None, "tp"), check_vma=False
    )
```

time: 244 us -> 214 us (0.88)
  local copies, waits for them, and re-layouts: 27.9 us -> 11.6 us
  blocking collectives: 40.8 us -> 33.5 us
  waiting for transfers between devices: 61.8 us -> 57.1 us
  Pallas kernels: 61.3 us -> 58.5 us
    ppermute x12 -> x6, waiting for transfers between devices: 28.5 us -> 3.78 us  [gathered(): lax.ppermute(block, axis, ring(step))]
    unnamed x50 -> x24, local copies, waits for them, and re-layouts: 27.9 us -> 8.73 us
    ppermute x0 -> x8, waiting for transfers between devices: none -> 17.5 us  [the longest x4 17.5 us: gathered_halves(): low, high = (lax.ppermute(block, axis, ring(step)) for step in (1, -1))]
    ppermute x0 -> x8, starting transfers between devices: none -> 12.2 us  [the longest x4 5.43 us: gathered_halves(): low, high = (lax.ppermute(block, axis, ring(step)) for step in (1, -1))]
    ppermute x12 -> x6, starting transfers between devices: 18.3 us -> 8.87 us  [gathered(): lax.ppermute(block, axis, ring(step))]
    pallas_call x0 -> x2, Pallas kernels: none -> 7.3 us  [own_prob(): pl.pallas_call(functools.partial(own_prob_kernel, prompt), name='own_prom...]
    all_to_all x2, blocking collectives: 40.8 us -> 33.5 us  [on_device(): lax.all_to_all(spread, axes, 0, 0, tiled=True)]
    pallas_call x8, Pallas kernels: 23.6 us -> 18.6 us  [chain(): pl.pallas_call(functools.partial(chain_kernel, prompt), name='prompt_chai...]
  transfers between devices with their start and end apart: 22 -> 24, of which waited for: 6 -> 7; matrix products, arithmetic and copies ran while one was open for 1% -> 2% of each run, Pallas kernels for 18% -> 19%
where the time goes in v4:
time: 214 us; the launch traced here: 213 us
  Pallas kernels  58.5 us (27%)
  waiting for transfers between devices  57.1 us (27%)
  starting transfers between devices  48 us (22%)
  blocking collectives  33.5 us (16%)
  local copies, waits for them, and re-layouts  11.6 us (5%)
  other arithmetic  3.38 us (2%)
    all_to_all x2, blocking collectives, on_device(): lax.all_to_all(spread, axes, 0, 0, tiled=True)  33.5 us
    all_to_all x4, starting transfers between devices, on_device(): swap = lambda a: lax.all_to_all(a, plane, 0, 0, tiled=True)  21.7 us
    ppermute x3, waiting for transfers between devices, on_device(): sent = lax.ppermute(gp, 'zl', [(now, now - 1)])  20.2 us
    pallas_call x8, Pallas kernels, chain(): pl.pallas_call(functools.partial(chain_kernel, prompt), name='prompt_chai...  18.6 us
    ppermute x4, waiting for transfers between devices, gathered_halves(): low, high = (lax.ppermute(block, axis, ring(step)) for step in (1, -1))  17.5 us
    pallas_call x2, Pallas kernels, prob(): pl.pallas_call(functools.partial(prob_kernel, prompt), name='prompt_prob'...  16.5 us
    ppermute x3, waiting for transfers between devices, on_device(): gr = lax.ppermute(gr, 'zl', [(now, now - 1)])  9.65 us
    ppermute x6, starting transfers between devices, gathered(): lax.ppermute(block, axis, ring(step))  8.87 us
  transfers between devices with their start and end apart: 24, of which 7 were waited for; matrix products, arithmetic and copies ran while one was open for 2% of the time, Pallas kernels for 19%

profile of v4, /device:TPU:1, one launch (start us, length us, event | category | flops | bytes accessed | tf_op | source)
XLA Modules:
  0.0 213.3 jit_solution(16523931175109426339)
XLA Ops:
  0.0 3.9 %pack.1 = (bf16[16,256,128]{2,1,0:T(8,128)(2,1)}, bf16[16,192,128]{2,1,0:T(8,128)(2,1)}, bf16[256,128]{1,0:T(8,128)(2,1)}, bf16[192,128]{1,0:T(8,128)(2,1)}, bf1...) custom-call(s32[4]{0:T(128)} %lens.11, s32[1]{0:T(128)} %bitcast.place, bf16[512,2048]{1,0:T(8,128)(2,1)} %bitcast.32, ...), custom_call_target="tpu_custom_call" | custom-call | flops 4000000000 | tf_op jit(solution)/shard_map/pack/pallas_call | solution.py:110
  3.9 3.4 %collective-permute-start.4 = (bf16[448,128]{1,0:T(8,128)(2,1)}, bf16[448,128]{1,0:T(8,128)(2,1)S(1)}, u32[]{:S(2)}, u32[]{:S(2)}) collective-permute-start(bf16[448,128]{1,0:T(8,128)(2,1)} %get-tuple-element.53.v_ref), channel_id=1, source_target_pairs={{0,48},{16,0},{32,16},{48,32},{1,49},{17,1},{33,17},{49,33},{2,50}... | collective-permute-start | bytes 344072 | tf_op jit(solution)/shard_map/ppermute | solution.py:456
  8.4 1.3 collective-permute-start
  9.6 1.4 collective-permute-start.1
  11.1 1.6 collective-permute-start.2
  12.7 3.3 %collective-permute-done.3 = bf16[448,128]{1,0:T(8,128)(2,1)S(1)} collective-permute-done((bf16[448,128]{1,0:T(8,128)(2,1)}, bf16[448,128]{1,0:T(8,128)(2,1)S(1)}, u32[]{:S(2)}, u32[]{:S(2)}) %collective-permute-start.3) | collective-permute-done | bytes 114720 | tf_op jit(solution)/shard_map/ppermute | solution.py:456
  16.0 1.0 pad_maximum_fusion.1.refs_5_
  17.5 1.0 pad_maximum_fusion.refs_0_
  18.5 7.2 %all-to-all-start = ((bf16[16,256,128]{2,1,0:T(8,128)(2,1)}), bf16[16,256,128]{2,1,0:T(8,128)(2,1)}, u32[]{:S(2)}, u32[]{:S(2)}) async-start(bf16[16,256,128]{2,1,0:T(8,128)(2,1)} %get-tuple-element.89.q_ref), calls=%async_computation | async-start | bytes 2097152 | tf_op jit(solution)/shard_map/all_to_all | solution.py:485
  25.7 1.3 collective-permute-start.10
  27.0 1.4 collective-permute-start.11
  28.4 1.2 collective-permute-start.6
  29.7 1.4 collective-permute-start.7
  31.1 17.5 %collective-permute-done.10.refs_6_ = bf16[4,448,128]{2,1,0:T(8,128)(2,1)S(1)} collective-permute-done((bf16[4,448,128]{2,1,0:T(8,128)(2,1)S(1)}, bf16[4,448,128]{2,1,0:T(8,128)(2,1)S(1)}, u32[]{:S(2)}, u32[]{:S(2)}) %collective-permute-start.10) | collective-permute-done | bytes 458784 | tf_op jit(solution)/shard_map/ppermute | solution.py:460
  48.6 0.7 slice.18
  49.3 0.7 slice.19
  50.0 2.7 %collective-permute-start.13 = (bf16[2,448,128]{2,1,0:T(8,128)(2,1)}, bf16[2,448,128]{2,1,0:T(8,128)(2,1)S(1)}, u32[]{:S(2)}, u32[]{:S(2)}) collective-permute-start(bf16[2,448,128]{2,1,0:T(8,128)(2,1)} %slice.19), channel_id=1, source_target_pairs={{0,12},{4,0},{8,4},{12,8},{1,13},{5,1},{9,5},{13,9},{2,14},{6,2},{... | collective-permute-start | bytes 688136 | tf_op jit(solution)/shard_map/ppermute | solution.py:467
  52.7 0.7 slice.16
  53.4 2.6 %collective-permute-start.8 = (bf16[2,448,128]{2,1,0:T(8,128)(2,1)}, bf16[2,448,128]{2,1,0:T(8,128)(2,1)S(1)}, u32[]{:S(2)}, u32[]{:S(2)}) collective-permute-start(bf16[2,448,128]{2,1,0:T(8,128)(2,1)} %slice.16), channel_id=1, source_target_pairs={{0,16},{16,32},{32,48},{48,0},{1,17},{17,33},{33,49},{49,1},{2,18}... | collective-permute-start | bytes 688136 | tf_op jit(solution)/shard_map/ppermute | solution.py:466
  56.0 0.7 slice.17
  56.7 1.5 collective-permute-start.9
  58.2 4.5 %all-to-all-start.1 = ((bf16[16,192,128]{2,1,0:T(8,128)(2,1)}), bf16[16,192,128]{2,1,0:T(8,128)(2,1)}, u32[]{:S(2)}, u32[]{:S(2)}) async-start(bf16[16,192,128]{2,1,0:T(8,128)(2,1)} %get-tuple-element.92.q_ref), calls=%async_computation.1 | async-start | bytes 1572864 | tf_op jit(solution)/shard_map/all_to_all | solution.py:485
  62.8 7.2 %prompt_prob.1 = (f32[16,256,384]{2,1,0:T(8,128)}, bf16[16,256,128]{2,1,0:T(8,128)(2,1)}, bf16[16,256,128]{2,1,0:T(8,128)(2,1)}) custom-call(s32[4]{0:T(128)S(1)} %copy-done.3, s32[16]{0:T(128)S(1)} %get-tuple-element.99.k_from, s32[16]{0:T(128)S(1)} %get-tuple-element.100.v_from, bf16[16,256,128]{2,1,0:T(8,128)(2,1)} %all-to-all-done.q_ref.stash_in, ...), custom_call_target="tpu_custom_call" | custom-call | flops 7000000000 | tf_op jit(solution)/shard_map/prompt_prob/pallas_call | solution.py:219
  69.9 0.8 prompt_chain.4
  70.8 0.7 collective-permute-start.15
  71.4 3.0 %all-to-all-done.1.q_ref.stash_in = bf16[16,192,128]{2,1,0:T(8,128)(2,1)} async-done(((bf16[16,192,128]{2,1,0:T(8,128)(2,1)}), bf16[16,192,128]{2,1,0:T(8,128)(2,1)}, u32[]{:S(2)}, u32[]{:S(2)}) %all-to-all-start.1) | async-done | bytes 786464 | tf_op jit(solution)/shard_map/all_to_all | solution.py:485
  74.5 9.4 %response_prob.1 = (f32[16,192,640]{2,1,0:T(8,128)}, bf16[16,448,128]{2,1,0:T(8,128)(2,1)}, bf16[16,448,128]{2,1,0:T(8,128)(2,1)}) custom-call(s32[4]{0:T(128)S(1)} %copy-done.3, s32[16]{0:T(128)S(1)} %get-tuple-element.99.k_from, s32[16]{0:T(128)S(1)} %get-tuple-element.100.v_from, bf16[16,192,128]{2,1,0:T(8,128)(2,1)} %all-to-all-done.1.q_ref.stash_in, ...), custom_call_target="tpu_custom_call" | custom-call | flops 7000000000 | tf_op jit(solution)/shard_map/response_prob/pallas_call | solution.py:219
  86.0 1.3 collective-permute-start.18
  88.0 20.2 %collective-permute-done.18.g_in = bf16[256,128]{1,0:T(8,128)(2,1)S(1)} collective-permute-done((bf16[256,128]{1,0:T(8,128)(2,1)S(1)}, bf16[256,128]{1,0:T(8,128)(2,1)S(1)}, u32[]{:S(2)}, u32[]{:S(2)}) %collective-permute-start.18) | collective-permute-done | bytes 65568 | tf_op jit(solution)/shard_map/ppermute | solution.py:501
  108.4 1.3 collective-permute-start.19
  109.7 8.3 %prompt_chain.7 = (bf16[256,128]{1,0:T(8,128)(2,1)}, bf16[16,256,128]{2,1,0:T(8,128)(2,1)}) custom-call(s32[1]{0:T(128)} %bitcast.12.active, bf16[256,128]{1,0:T(8,128)(2,1)S(1)} %collective-permute-done.18.g_in, bf16[16,256,128]{2,1,0:T(8,128)(2,1)} %get-tuple-element.84.stash_in, ...), custom_call_target="tpu_custom_call", output_to_operand_aliasing={{1}: (2, {})} | custom-call | flops 7000000000 | tf_op jit(solution)/shard_map/prompt_chain/pallas_call | solution.py:303
  118.0 9.6 %collective-permute-done.19.g_in = bf16[192,128]{1,0:T(8,128)(2,1)S(1)} collective-permute-done((bf16[192,128]{1,0:T(8,128)(2,1)S(1)}, bf16[192,128]{1,0:T(8,128)(2,1)S(1)}, u32[]{:S(2)}, u32[]{:S(2)}) %collective-permute-start.19) | collective-permute-done | bytes 49184 | tf_op jit(solution)/shard_map/ppermute | solution.py:509
  127.6 8.6 %response_chain.7 = (bf16[192,128]{1,0:T(8,128)(2,1)}, bf16[16,192,128]{2,1,0:T(8,128)(2,1)}) custom-call(s32[1]{0:T(128)} %bitcast.12.active, bf16[192,128]{1,0:T(8,128)(2,1)S(1)} %collective-permute-done.19.g_in, bf16[16,192,128]{2,1,0:T(8,128)(2,1)} %get-tuple-element.87.stash_in, ...), custom_call_target="tpu_custom_call", output_to_operand_aliasing={{1}: (2, {})} | custom-call | flops 7000000000 | tf_op jit(solution)/shard_map/response_chain/pallas_call | solution.py:303
  136.2 6.4 %all-to-all-start.3 = ((bf16[16,192,128]{2,1,0:T(8,128)(2,1)}), bf16[16,192,128]{2,1,0:T(8,128)(2,1)S(1)}, u32[]{:S(2)}, u32[]{:S(2)}) async-start(bf16[16,192,128]{2,1,0:T(8,128)(2,1)} %get-tuple-element.93), calls=%async_computation.3 | async-start | bytes 1572864 | tf_op jit(solution)/shard_map/all_to_all | solution.py:485
  142.6 4.5 %own_response_prob.1.probs = f32[16,448,192]{2,1,0:T(8,128)S(1)} custom-call(s32[4]{0:T(128)S(1)} %copy-done.3, bf16[16,192,128]{2,1,0:T(8,128)(2,1)} %get-tuple-element.92.q_ref, bf16[448,128]{1,0:T(8,128)(2,1)S(1)} %copy-done.2), custom_call_target="tpu_custom_call" | custom-call | flops 5000000000 | tf_op jit(solution)/shard_map/own_response_prob/pallas_call | solution.py:347
  147.2 2.9 %copy-done.4 = f32[16,448,192]{2,1,0:T(8,128)} copy-done((f32[16,448,192]{2,1,0:T(8,128)}, f32[16,448,192]{2,1,0:T(8,128)S(1)}, u32[]{:S(2)}) %copy-start.4) | copy-done | bytes 5505048
  150.1 3.0 %all-to-all-done.3.g_ref = bf16[16,192,128]{2,1,0:T(8,128)(2,1)S(1)} async-done(((bf16[16,192,128]{2,1,0:T(8,128)(2,1)}), bf16[16,192,128]{2,1,0:T(8,128)(2,1)S(1)}, u32[]{:S(2)}, u32[]{:S(2)}) %all-to-all-start.3) | async-done | bytes 786464 | tf_op jit(solution)/shard_map/all_to_all | solution.py:485
  153.0 3.7 %all-to-all-start.2 = ((bf16[16,256,128]{2,1,0:T(8,128)(2,1)}), bf16[16,256,128]{2,1,0:T(8,128)(2,1)S(1)}, u32[]{:S(2)}, u32[]{:S(2)}) async-start(bf16[16,256,128]{2,1,0:T(8,128)(2,1)} %get-tuple-element.91), calls=%async_computation.2 | async-start | bytes 2097152 | tf_op jit(solution)/shard_map/all_to_all | solution.py:485
  156.8 2.8 %own_prompt_prob.1.probs = f32[16,256,256]{2,1,0:T(8,128)S(1)} custom-call(s32[4]{0:T(128)S(1)} %copy-done.3, bf16[16,256,128]{2,1,0:T(8,128)(2,1)S(1)} %copy-done, bf16[448,128]{1,0:T(8,128)(2,1)S(1)} %copy-done.2), custom_call_target="tpu_custom_call" | custom-call | flops 5000000000 | tf_op jit(solution)/shard_map/own_prompt_prob/pallas_call | solution.py:347
  159.5 2.0 copy-done.6
  161.5 7.7 %response_grad.1 = (f32[256,256]{1,0:T(8,128)S(1)}, f32[256,256]{1,0:T(8,128)S(1)}, f32[1,128]{1,0:T(1,128)S(1)}) custom-call(s32[4]{0:T(128)S(1)} %copy-done.3, f32[16,448,192]{2,1,0:T(8,128)S(1)} %copy-done.5, bf16[16,192,128]{2,1,0:T(8,128)(2,1)} %get-tuple-element.92.q_ref, bf16[16,192,128]{2,1,0:T(8,128)(2,1)S(1)} %all-to-all-done.3.g_ref, ...), custom_call_target="tpu_custom_call" | custom-call | flops 8000000000 | tf_op jit(solution)/shard_map/response_grad/pallas_call | solution.py:399
  169.3 0.7 copy-done.8
  170.0 2.2 %copy-done.7 = f32[16,256,256]{2,1,0:T(8,128)S(1)} copy-done((f32[16,256,256]{2,1,0:T(8,128)S(1)}, f32[16,256,256]{2,1,0:T(8,128)}, u32[]{:S(2)}) %copy-start.7) | copy-done | bytes 4194328
  172.2 0.9 copy-done.9
  173.1 4.5 %prompt_grad.1 = (f32[512,256]{1,0:T(8,128)S(1)}, f32[1,128]{1,0:T(1,128)S(1)}) custom-call(f32[16,256,256]{2,1,0:T(8,128)S(1)} %copy-done.7, bf16[16,256,128]{2,1,0:T(8,128)(2,1)S(1)} %copy-done, bf16[16,256,128]{2,1,0:T(8,128)(2,1)S(1)} %all-to-all-done.2.g_ref, bf16[448,128]{1,0:T(8,128)(2,1)S(1)} %copy-done.1, ...), custom_call_target="tpu_custom_call" | custom-call | flops 5000000000 | tf_op jit(solution)/shard_map/prompt_grad/pallas_call | solution.py:439
  177.6 12.9 %all_to_all.32 = f32[16,1,128]{2,1,0:T(1,128)S(1)} all-to-all(f32[16,1,128]{2,1,0:T(1,128)S(1)} %broadcast_in_dim.26), channel_id=1, replica_groups=mesh['zl'=4,'x'=4,'y'=4,'tp'=4] {'x','y'}, dimensions={0} | all-to-all | bytes 16384 | tf_op jit(solution)/shard_map/all_to_all | solution.py:518
  190.5 20.7 %all_to_all.33 = f32[16,1,128]{2,1,0:T(1,128)S(1)} all-to-all(f32[16,1,128]{2,1,0:T(1,128)S(1)} %broadcast_in_dim.27), channel_id=1, replica_groups=mesh['zl'=4,'x'=4,'y'=4,'tp'=4] {'zl','tp'}, dimensions={0} | all-to-all | bytes 16384 | tf_op jit(solution)/shard_map/all_to_all | solution.py:518
  212.5 0.8 multiply_bitcast_fusion
  (53 shorter events, 5.3 us)
Async XLA Ops:
  3.9 58.9 %copy-start.3 = (s32[4]{0:T(128)S(1)}, s32[4]{0:T(128)}, u32[]{:S(2)}) copy-start(s32[4]{0:T(128)} %lens.11) | copy-start | bytes 52
  3.9 7.2 %collective-permute-start.4 = (bf16[448,128]{1,0:T(8,128)(2,1)}, bf16[448,128]{1,0:T(8,128)(2,1)S(1)}, u32[]{:S(2)}, u32[]{:S(2)}) collective-permute-start(bf16[448,128]{1,0:T(8,128)(2,1)} %get-tuple-element.53.v_ref), channel_id=1, source_target_pairs={{0,48},{16,0},{32,16},{48,32},{1,49},{17,1},{33,17},{49,33},{2,50}... | collective-permute-start | bytes 344072 | tf_op jit(solution)/shard_map/ppermute | solution.py:456
  7.2 5.5 %collective-permute-start.5 = (bf16[448,128]{1,0:T(8,128)(2,1)}, bf16[448,128]{1,0:T(8,128)(2,1)S(1)}, u32[]{:S(2)}, u32[]{:S(2)}) collective-permute-start(bf16[448,128]{1,0:T(8,128)(2,1)} %get-tuple-element.53.v_ref), channel_id=1, source_target_pairs={{0,32},{16,48},{32,0},{48,16},{1,33},{17,49},{33,1},{49,17},{2,34}... | collective-permute-start | bytes 344072 | tf_op jit(solution)/shard_map/ppermute | solution.py:456
  7.7 8.3 %collective-permute-start.3 = (bf16[448,128]{1,0:T(8,128)(2,1)}, bf16[448,128]{1,0:T(8,128)(2,1)S(1)}, u32[]{:S(2)}, u32[]{:S(2)}) collective-permute-start(bf16[448,128]{1,0:T(8,128)(2,1)} %get-tuple-element.53.v_ref), channel_id=1, source_target_pairs={{0,16},{16,32},{32,48},{48,0},{1,17},{17,33},{33,49},{49,1},{2,18}... | collective-permute-start | bytes 344072 | tf_op jit(solution)/shard_map/ppermute | solution.py:456
  8.4 8.6 %collective-permute-start = (bf16[448,128]{1,0:T(8,128)(2,1)}, bf16[448,128]{1,0:T(8,128)(2,1)S(1)}, u32[]{:S(2)}, u32[]{:S(2)}) collective-permute-start(bf16[448,128]{1,0:T(8,128)(2,1)} %get-tuple-element.52.k_ref), channel_id=1, source_target_pairs={{0,4},{4,8},{8,12},{12,0},{1,5},{5,9},{9,13},{13,1},{2,6},{6,10},{... | collective-permute-start | bytes 344072 | tf_op jit(solution)/shard_map/ppermute | solution.py:456
  9.6 7.4 %collective-permute-start.1 = (bf16[448,128]{1,0:T(8,128)(2,1)}, bf16[448,128]{1,0:T(8,128)(2,1)S(1)}, u32[]{:S(2)}, u32[]{:S(2)}) collective-permute-start(bf16[448,128]{1,0:T(8,128)(2,1)} %get-tuple-element.52.k_ref), channel_id=1, source_target_pairs={{0,12},{4,0},{8,4},{12,8},{1,13},{5,1},{9,5},{13,9},{2,14},{6,2},{... | collective-permute-start | bytes 344072 | tf_op jit(solution)/shard_map/ppermute | solution.py:456
  11.1 6.4 %collective-permute-start.2 = (bf16[448,128]{1,0:T(8,128)(2,1)}, bf16[448,128]{1,0:T(8,128)(2,1)S(1)}, u32[]{:S(2)}, u32[]{:S(2)}) collective-permute-start(bf16[448,128]{1,0:T(8,128)(2,1)} %get-tuple-element.52.k_ref), channel_id=1, source_target_pairs={{0,8},{4,12},{8,0},{12,4},{1,9},{5,13},{9,1},{13,5},{2,10},{6,14},... | collective-permute-start | bytes 344072 | tf_op jit(solution)/shard_map/ppermute | solution.py:456
  18.5 39.8 %all-to-all-start = ((bf16[16,256,128]{2,1,0:T(8,128)(2,1)}), bf16[16,256,128]{2,1,0:T(8,128)(2,1)}, u32[]{:S(2)}, u32[]{:S(2)}) async-start(bf16[16,256,128]{2,1,0:T(8,128)(2,1)} %get-tuple-element.89.q_ref), calls=%async_computation | async-start | bytes 2097152 | tf_op jit(solution)/shard_map/all_to_all | solution.py:485
  25.7 22.9 %collective-permute-start.10 = (bf16[4,448,128]{2,1,0:T(8,128)(2,1)S(1)}, bf16[4,448,128]{2,1,0:T(8,128)(2,1)S(1)}, u32[]{:S(2)}, u32[]{:S(2)}) collective-permute-start(bf16[4,448,128]{2,1,0:T(8,128)(2,1)S(1)} %pad_maximum_fusion.1.refs_5_), channel_id=1, source_target_pairs={{0,4},{4,8},{8,12},{12,0},{1,5},{5,9},{9,13},{13,1},{2,6},{6,10},{... | collective-permute-start | bytes 1376264 | tf_op jit(solution)/shard_map/ppermute | solution.py:460
  27.0 22.4 %collective-permute-start.11 = (bf16[4,448,128]{2,1,0:T(8,128)(2,1)S(1)}, bf16[4,448,128]{2,1,0:T(8,128)(2,1)S(1)}, u32[]{:S(2)}, u32[]{:S(2)}) collective-permute-start(bf16[4,448,128]{2,1,0:T(8,128)(2,1)S(1)} %pad_maximum_fusion.1.refs_5_), channel_id=1, source_target_pairs={{0,12},{4,0},{8,4},{12,8},{1,13},{5,1},{9,5},{13,9},{2,14},{6,2},{... | collective-permute-start | bytes 1376264 | tf_op jit(solution)/shard_map/ppermute | solution.py:460
  28.4 24.3 %collective-permute-start.6 = (bf16[4,448,128]{2,1,0:T(8,128)(2,1)S(1)}, bf16[4,448,128]{2,1,0:T(8,128)(2,1)S(1)}, u32[]{:S(2)}, u32[]{:S(2)}) collective-permute-start(bf16[4,448,128]{2,1,0:T(8,128)(2,1)S(1)} %pad_maximum_fusion.refs_0_), channel_id=1, source_target_pairs={{0,16},{16,32},{32,48},{48,0},{1,17},{17,33},{33,49},{49,1},{2,18}... | collective-permute-start | bytes 1376264 | tf_op jit(solution)/shard_map/ppermute | solution.py:460
  29.7 26.4 %collective-permute-start.7 = (bf16[4,448,128]{2,1,0:T(8,128)(2,1)S(1)}, bf16[4,448,128]{2,1,0:T(8,128)(2,1)S(1)}, u32[]{:S(2)}, u32[]{:S(2)}) collective-permute-start(bf16[4,448,128]{2,1,0:T(8,128)(2,1)S(1)} %pad_maximum_fusion.refs_0_), channel_id=1, source_target_pairs={{0,48},{16,0},{32,16},{48,32},{1,49},{17,1},{33,17},{49,33},{2,50}... | collective-permute-start | bytes 1376264 | tf_op jit(solution)/shard_map/ppermute | solution.py:460
  49.3 13.4 %collective-permute-start.12 = (bf16[2,448,128]{2,1,0:T(8,128)(2,1)}, bf16[2,448,128]{2,1,0:T(8,128)(2,1)S(1)}, u32[]{:S(2)}, u32[]{:S(2)}) collective-permute-start(bf16[2,448,128]{2,1,0:T(8,128)(2,1)} %slice.18), channel_id=1, source_target_pairs={{0,4},{4,8},{8,12},{12,0},{1,5},{5,9},{9,13},{13,1},{2,6},{6,10},{... | collective-permute-start | bytes 688136 | tf_op jit(solution)/shard_map/ppermute | solution.py:466
  50.0 12.7 %collective-permute-start.13 = (bf16[2,448,128]{2,1,0:T(8,128)(2,1)}, bf16[2,448,128]{2,1,0:T(8,128)(2,1)S(1)}, u32[]{:S(2)}, u32[]{:S(2)}) collective-permute-start(bf16[2,448,128]{2,1,0:T(8,128)(2,1)} %slice.19), channel_id=1, source_target_pairs={{0,12},{4,0},{8,4},{12,8},{1,13},{5,1},{9,5},{13,9},{2,14},{6,2},{... | collective-permute-start | bytes 688136 | tf_op jit(solution)/shard_map/ppermute | solution.py:467
  53.4 9.3 %collective-permute-start.8 = (bf16[2,448,128]{2,1,0:T(8,128)(2,1)}, bf16[2,448,128]{2,1,0:T(8,128)(2,1)S(1)}, u32[]{:S(2)}, u32[]{:S(2)}) collective-permute-start(bf16[2,448,128]{2,1,0:T(8,128)(2,1)} %slice.16), channel_id=1, source_target_pairs={{0,16},{16,32},{32,48},{48,0},{1,17},{17,33},{33,49},{49,1},{2,18}... | collective-permute-start | bytes 688136 | tf_op jit(solution)/shard_map/ppermute | solution.py:466
  56.7 6.0 %collective-permute-start.9 = (bf16[2,448,128]{2,1,0:T(8,128)(2,1)}, bf16[2,448,128]{2,1,0:T(8,128)(2,1)}, u32[]{:S(2)}, u32[]{:S(2)}) collective-permute-start(bf16[2,448,128]{2,1,0:T(8,128)(2,1)} %slice.17), channel_id=1, source_target_pairs={{0,48},{16,0},{32,16},{48,32},{1,49},{17,1},{33,17},{49,33},{2,50}... | collective-permute-start | bytes 688136 | tf_op jit(solution)/shard_map/ppermute | solution.py:467
  58.2 16.2 %all-to-all-start.1 = ((bf16[16,192,128]{2,1,0:T(8,128)(2,1)}), bf16[16,192,128]{2,1,0:T(8,128)(2,1)}, u32[]{:S(2)}, u32[]{:S(2)}) async-start(bf16[16,192,128]{2,1,0:T(8,128)(2,1)} %get-tuple-element.92.q_ref), calls=%async_computation.1 | async-start | bytes 1572864 | tf_op jit(solution)/shard_map/all_to_all | solution.py:485
  62.8 7.2 %copy-start.10 = (bf16[256,128]{1,0:T(8,128)(2,1)S(1)}, bf16[256,128]{1,0:T(8,128)(2,1)}, u32[]{:S(2)}) copy-start(bf16[256,128]{1,0:T(8,128)(2,1)} %get-tuple-element.57.g_in) | copy-start | bytes 196612
  70.8 13.3 %collective-permute-start.15 = (bf16[256,128]{1,0:T(8,128)(2,1)}, bf16[256,128]{1,0:T(8,128)(2,1)S(1)}, u32[]{:S(2)}, u32[]{:S(2)}) collective-permute-start(bf16[256,128]{1,0:T(8,128)(2,1)} %get-tuple-element.63), channel_id=1, source_target_pairs={{192,128},{193,129},{194,130},{195,131},{196,132},{197,133},{198,1... | collective-permute-start | bytes 196616 | tf_op jit(solution)/shard_map/ppermute | solution.py:501
  74.5 9.4 %copy-start.11 = (bf16[192,128]{1,0:T(8,128)(2,1)S(1)}, bf16[192,128]{1,0:T(8,128)(2,1)}, u32[]{:S(2)}) copy-start(bf16[192,128]{1,0:T(8,128)(2,1)} %get-tuple-element.64.g_in) | copy-start | bytes 147460
  84.3 1.4 collective-permute-start.16
  85.0 0.7 collective-permute-start.14
  86.0 22.2 %collective-permute-start.18 = (bf16[256,128]{1,0:T(8,128)(2,1)S(1)}, bf16[256,128]{1,0:T(8,128)(2,1)S(1)}, u32[]{:S(2)}, u32[]{:S(2)}) collective-permute-start(bf16[256,128]{1,0:T(8,128)(2,1)S(1)} %get-tuple-element.79), channel_id=1, source_target_pairs={{64,0},{65,1},{66,2},{67,3},{68,4},{69,5},{70,6},{71,7},{72,8},{73... | collective-permute-start | bytes 196616 | tf_op jit(solution)/shard_map/ppermute | solution.py:501
  87.3 0.7 collective-permute-start.17
  108.4 19.2 %collective-permute-start.19 = (bf16[192,128]{1,0:T(8,128)(2,1)S(1)}, bf16[192,128]{1,0:T(8,128)(2,1)S(1)}, u32[]{:S(2)}, u32[]{:S(2)}) collective-permute-start(bf16[192,128]{1,0:T(8,128)(2,1)S(1)} %get-tuple-element.82), channel_id=1, source_target_pairs={{64,0},{65,1},{66,2},{67,3},{68,4},{69,5},{70,6},{71,7},{72,8},{73... | collective-permute-start | bytes 147464 | tf_op jit(solution)/shard_map/ppermute | solution.py:509
  127.6 15.0 %copy-start.2 = (bf16[448,128]{1,0:T(8,128)(2,1)S(1)}, bf16[448,128]{1,0:T(8,128)(2,1)}, u32[]{:S(2)}) copy-start(bf16[448,128]{1,0:T(8,128)(2,1)} %get-tuple-element.52.k_ref) | copy-start | bytes 344068
  136.2 16.8 %all-to-all-start.3 = ((bf16[16,192,128]{2,1,0:T(8,128)(2,1)}), bf16[16,192,128]{2,1,0:T(8,128)(2,1)S(1)}, u32[]{:S(2)}, u32[]{:S(2)}) async-start(bf16[16,192,128]{2,1,0:T(8,128)(2,1)} %get-tuple-element.93), calls=%async_computation.3 | async-start | bytes 1572864 | tf_op jit(solution)/shard_map/all_to_all | solution.py:485
  142.6 14.1 %copy-start = (bf16[16,256,128]{2,1,0:T(8,128)(2,1)S(1)}, bf16[16,256,128]{2,1,0:T(8,128)(2,1)}, u32[]{:S(2)}) copy-start(bf16[16,256,128]{2,1,0:T(8,128)(2,1)} %get-tuple-element.89.q_ref) | copy-start | bytes 3145732
  147.2 2.9 %copy-start.4 = (f32[16,448,192]{2,1,0:T(8,128)}, f32[16,448,192]{2,1,0:T(8,128)S(1)}, u32[]{:S(2)}) copy-start(f32[16,448,192]{2,1,0:T(8,128)S(1)} %own_response_prob.1.probs) | copy-start | bytes 16515076
  153.0 16.9 %all-to-all-start.2 = ((bf16[16,256,128]{2,1,0:T(8,128)(2,1)}), bf16[16,256,128]{2,1,0:T(8,128)(2,1)S(1)}, u32[]{:S(2)}, u32[]{:S(2)}) async-start(bf16[16,256,128]{2,1,0:T(8,128)(2,1)} %get-tuple-element.91), calls=%async_computation.2 | async-start | bytes 2097152 | tf_op jit(solution)/shard_map/all_to_all | solution.py:485
  156.7 4.8 %copy-start.1 = (bf16[448,128]{1,0:T(8,128)(2,1)S(1)}, bf16[448,128]{1,0:T(8,128)(2,1)}, u32[]{:S(2)}) copy-start(bf16[448,128]{1,0:T(8,128)(2,1)} %get-tuple-element.53.v_ref) | copy-start | bytes 344068
  156.8 4.8 %copy-start.5 = (f32[16,448,192]{2,1,0:T(8,128)S(1)}, f32[16,448,192]{2,1,0:T(8,128)}, u32[]{:S(2)}) copy-start(f32[16,448,192]{2,1,0:T(8,128)} %copy-done.4) | copy-start | bytes 16515076
  159.5 2.0 copy-start.6
  169.3 0.7 copy-start.8
  170.0 2.2 %copy-start.7 = (f32[16,256,256]{2,1,0:T(8,128)S(1)}, f32[16,256,256]{2,1,0:T(8,128)}, u32[]{:S(2)}) copy-start(f32[16,256,256]{2,1,0:T(8,128)} %copy-done.6) | copy-start | bytes 12582916
  172.2 0.9 copy-start.9

commit v5 on v4

--- a/solution.py
+++ b/solution.py
@@ -25,6 +25,11 @@
 bf16 = jnp.bfloat16
 
 
+VMEM = pl.BlockSpec(memory_space=pltpu.VMEM)
+SMEM = pl.BlockSpec(memory_space=pltpu.SMEM)
+HBM = pl.BlockSpec(memory_space=pltpu.HBM)
+
+
 def dot(a, b):
     return lax.dot_general(a, b, (((1,), (0,)), ((), ())), preferred_element_type=f32)
 
@@ -64,9 +69,12 @@
     return jnp.where(k <= q, 0.0, -jnp.inf).astype(f32)
 
 
-def response_bias(lens, query_dim):
-    q = lax.broadcasted_iota(jnp.int32, (RESP, RESP), query_dim)
-    k = lax.broadcasted_iota(jnp.int32, (RESP, RESP), 1 - query_dim)
+def response_bias(lens, query_dim, repeats=1):
+    dims = (RESP, repeats * RESP)
+    q = lax.broadcasted_iota(jnp.int32, dims, query_dim)
+    k = lax.broadcasted_iota(jnp.int32, dims, 1 - query_dim)
+    for _ in range(repeats - 1):
+        q = jnp.where(q >= RESP, q - RESP, q)
     return jnp.where((k <= q) & (k >= start_of(q, lens)), 0.0, -jnp.inf).astype(f32)
 
 
@@ -83,16 +91,13 @@
     return jnp.where(col == slot * RLEN + row - start_of(row, lens), 1.0, 0.0).astype(bf16)
 
 
-def pack_kernel(lens, place, x_ref, top_ref, key_ref, value_ref, xp_out, xr_out, tp_out, tr_out, k_out, v_out, chosen):
+def pack_kernel(lens, place, x_ref, top_ref, xp_out, xr_out, tp_out, tr_out, chosen):
     @pl.when(pl.program_id(0) == 0)
     def _():
         pick = chosen_rows(lens, 0)
         chosen[...] = pick
         tp_out[...] = top_ref[:PROMPT]
         tr_out[...] = dot(pick, top_ref[PROMPT:]).astype(bf16)
-        for ref, out in ((key_ref, k_out), (value_ref, v_out)):
-            out[:PROMPT] = ref[:PROMPT]
-            out[PROMPT:] = dot(pick, ref[PROMPT:]).astype(bf16)
 
     live = dot(chosen[...], x_ref[PROMPT:]).astype(bf16)
     for h in range(x_ref.shape[1] // HD):
@@ -101,12 +106,12 @@
         xr_out[h] = live[:, cols]
 
 
-def pack(lens, place, x, top, key, value):
+def pack(lens, place, x, top):
     rows, width = x.shape
     heads = width // HD
     steps = 2
     some = heads // steps
-    whole = lambda *dims: pl.BlockSpec(dims, lambda i, l, p: (0,) * len(dims))
+    whole = lambda n: pl.BlockSpec((n, HD), lambda i, l, p: (0, 0))
     return pl.pallas_call(
         pack_kernel,
         name="pack",
@@ -117,16 +122,12 @@
             in_specs=[
                 pl.BlockSpec((rows, some * HD), lambda i, l, p: (0, i)),
                 pl.BlockSpec((rows, HD), lambda i, l, p: (0, p[0])),
-                whole(rows, HD),
-                whole(rows, HD),
             ],
             out_specs=[
                 pl.BlockSpec((some, PROMPT, HD), lambda i, l, p: (i, 0, 0)),
                 pl.BlockSpec((some, RESP, HD), lambda i, l, p: (i, 0, 0)),
-                whole(PROMPT, HD),
-                whole(RESP, HD),
-                whole(LIVE, HD),
-                whole(LIVE, HD),
+                whole(PROMPT),
+                whole(RESP),
             ],
             scratch_shapes=[pltpu.VMEM((RESP, NRESP * RLEN), bf16)],
         ),
@@ -135,11 +136,30 @@
             shape((heads, RESP, HD), bf16),
             shape((PROMPT, HD), bf16),
             shape((RESP, HD), bf16),
-            shape((LIVE, HD), bf16),
-            shape((LIVE, HD), bf16),
         ],
         compiler_params=params(60),
-    )(lens, place, x, top, key, value)
+    )(lens, place, x, top)
+
+
+def stack_live_kernel(lens, *refs):
+    out_k, out_v = refs[2 * SIDE :]
+    chosen = chosen_rows(lens, 0)
+    for parts, out in ((refs[:SIDE], out_k), (refs[SIDE : 2 * SIDE], out_v)):
+        for i, part in enumerate(parts):
+            out[i, :PROMPT] = part[:PROMPT]
+            out[i, PROMPT:] = dot(chosen, part[PROMPT:]).astype(bf16)
+
+
+def stack_live(lens, keys, values):
+    return pl.pallas_call(
+        stack_live_kernel,
+        name="stack_live",
+        cost_estimate=about(2),
+        in_specs=[SMEM] + [VMEM] * (2 * SIDE),
+        out_specs=[VMEM] * 2,
+        out_shape=[shape((SIDE, LIVE, HD), bf16)] * 2,
+        compiler_params=params(8),
+    )(lens, *keys, *values)
 
 
 def softmax(scores, dim):
@@ -153,15 +173,6 @@
 AT_ONCE = 4
 PROMPT_ROW = PROMPT + HD
 RESP_ROW = 2 * PROMPT + HD
-VMEM = pl.BlockSpec(memory_space=pltpu.VMEM)
-SMEM = pl.BlockSpec(memory_space=pltpu.SMEM)
-HBM = pl.BlockSpec(memory_space=pltpu.HBM)
-
-
-def kept(x):
-    return pltpu.with_memory_space_constraint(x, pltpu.VMEM)
-
-
 def in_hbm(x):
     return pltpu.with_memory_space_constraint(x, pltpu.HBM)
 
@@ -323,129 +334,177 @@
 HEADS_AT_ONCE = 2
 
 
-def own_prob_kernel(prompt, lens, q_ref, k_ref, probs, bias):
-    bias[...] = prompt_bias(1) if prompt else response_bias(lens, 1)
-    k1, k2 = k_ref[:PROMPT], k_ref[PROMPT:]
-
-    def body(i, carry):
-        for u in range(AT_ONCE):
-            head = i * AT_ONCE + u
-            q = q_ref[head]
+def own_prob_kernel(prompt, active, lens, q_ref, k_ref, *refs):
+    out, probs, queries, bias, sems, q_sem = refs[-6:]
+    steps = queries.shape[0] // AT_ONCE
+
+    def done(i):
+        some = pl.ds(i * AT_ONCE, AT_ONCE) if prompt else pl.ds(i, 1)
+        return pltpu.make_async_copy(probs.at[some], out.at[some], sems.at[i])
+
+    @pl.when(active[0] == 1)
+    def _():
+        fetch = pltpu.make_async_copy(q_ref, queries, q_sem)
+        fetch.start()
+        if prompt:
+            bias[...] = prompt_bias(1)
+        else:
+            bias[...] = response_bias(lens, 1, AT_ONCE)
+        k1, k2 = k_ref[:PROMPT], k_ref[PROMPT:]
+        fetch.wait()
+
+        def body(i, carry):
             if prompt:
-                (probs[head],) = softmax([dot_nt(k1, q) + bias[...]], 0)
+                for u in range(AT_ONCE):
+                    head = i * AT_ONCE + u
+                    (probs[head],) = softmax([dot_nt(k1, queries[head]) + bias[...]], 0)
             else:
+                q = queries[pl.ds(i * AT_ONCE, AT_ONCE)].reshape(AT_ONCE * RESP, HD)
                 p1, p2 = softmax([dot_nt(k1, q), dot_nt(k2, q) + bias[...]], 0)
-                probs[head, :PROMPT] = p1
-                probs[head, PROMPT:] = p2
-        return carry
-
-    lax.fori_loop(0, q_ref.shape[0] // AT_ONCE, body, 0)
-
-
-def own_prob(prompt, lens, q, k):
+                probs[i, :PROMPT] = p1
+                probs[i, PROMPT:] = p2
+            done(i).start()
+            return carry
+
+        lax.fori_loop(0, steps, body, 0)
+        for i in range(steps):
+            done(i).wait()
+
+
+def own_prob(prompt, active, lens, q, k, earlier=None, us=5):
     n, rows, _ = q.shape
+    dims = (n, PROMPT, rows) if prompt else (n // AT_ONCE, LIVE, AT_ONCE * RESP)
+    more = [] if earlier is None else [in_hbm(earlier)]
     return pl.pallas_call(
         functools.partial(own_prob_kernel, prompt),
         name="own_prompt_prob" if prompt else "own_response_prob",
-        cost_estimate=about(5),
-        in_specs=[SMEM, VMEM, VMEM],
-        out_specs=VMEM,
-        scratch_shapes=[pltpu.VMEM((rows, rows), f32)],
-        out_shape=pltpu.VMEM((n, PROMPT if prompt else LIVE, rows), f32),
-        compiler_params=params(12),
-    )(lens, q, k)
-
-
-def response_grad_kernel(lens, probs, q_ref, g_ref, v_ref, prompt_out, out_ref, sum_ref, acc):
-    acc[...] = jnp.zeros_like(acc)
-    v1, v2 = v_ref[:PROMPT], v_ref[PROMPT:]
-
-    def body(i, carry):
-        dk1, dk2, dv1, dv2 = 0.0, 0.0, 0.0, 0.0
-        for u in range(HEADS_AT_ONCE):
-            head = i * HEADS_AT_ONCE + u
-            q, g = q_ref[head], g_ref[head]
-            p1, p2 = probs[head, :PROMPT], probs[head, PROMPT:]
-            dp1, dp2 = dot_nt(v1, g), dot_nt(v2, g)
-            pb1, pb2 = p1.astype(bf16), p2.astype(bf16)
-            delta = jnp.sum(pb1.astype(f32) * dp1, 0, keepdims=True) + jnp.sum(
-                pb2.astype(f32) * dp2, 0, keepdims=True
-            )
-            ds1 = (p1 * (dp1 - delta)).astype(bf16)
-            ds2 = (p2 * (dp2 - delta)).astype(bf16)
-            dk1, dk2 = dk1 + dot(ds1, q), dk2 + dot(ds2, q)
-            dv1, dv2 = dv1 + dot(pb1, g), dv2 + dot(pb2, g)
-        acc[:PROMPT, :HD] += dk1 * SCALE
-        acc[PROMPT:, :HD] += dk2 * SCALE
-        acc[:PROMPT, HD:] += dv1
-        acc[PROMPT:, HD:] += dv2
-        return carry
-
-    lax.fori_loop(0, q_ref.shape[0] // HEADS_AT_ONCE, body, 0)
-    prompt_out[...] = acc[:PROMPT]
-    left = acc[PROMPT:]
-    squares = jnp.sum(left * left, 0, keepdims=True)
-    sum_ref[...] = squares[:, :HD] + squares[:, HD:]
-    spread = chosen_rows(lens, 1)
-    placed = jnp.zeros((NRESP * RLEN, 2 * HD), f32)
-    for _ in range(3):
-        term = left.astype(bf16)
-        placed = placed + dot(spread, term)
-        left = left - term.astype(f32)
-    out_ref[...] = placed
-
-
-def response_grad(lens, probs, q, g, v):
-    return pl.pallas_call(
-        response_grad_kernel,
-        name="response_grad",
-        cost_estimate=about(8),
-        in_specs=[SMEM] + [VMEM] * 4,
-        out_specs=[VMEM] * 3,
-        scratch_shapes=[pltpu.VMEM((LIVE, 2 * HD), f32)],
-        out_shape=[shape((PROMPT, 2 * HD)), shape((NRESP * RLEN, 2 * HD)), shape((1, HD))],
-        compiler_params=params(12),
-    )(lens, kept(probs), q, g, v)
-
-
-def prompt_grad_kernel(probs, q_ref, g_ref, v_ref, part_ref, response_ref, squares_ref, out_ref, sum_ref, acc):
-    acc[...] = part_ref[...]
-    v = v_ref[:PROMPT]
-
-    def body(i, carry):
+        cost_estimate=about(us),
+        in_specs=[SMEM, SMEM, HBM, VMEM] + [HBM] * len(more),
+        out_specs=HBM,
+        scratch_shapes=[
+            pltpu.VMEM(dims, f32),
+            pltpu.VMEM(q.shape, bf16),
+            pltpu.VMEM((rows, rows if prompt else AT_ONCE * RESP), f32),
+            pltpu.SemaphoreType.DMA((n // AT_ONCE,)),
+            pltpu.SemaphoreType.DMA,
+        ],
+        out_shape=pltpu.HBM(dims, f32),
+        input_output_aliases={4: 0} if more else {},
+        compiler_params=params(16),
+    )(active, lens, in_hbm(q), k, *more)
+
+
+def prompt_grad_kernel(probs, q_ref, g_ref, v_ref, out_ref):
+    @pl.when(pl.program_id(0) == 0)
+    def _():
+        out_ref[...] = jnp.zeros_like(out_ref)
+
+    v = v_ref[...]
+
+    def body(j, carry):
         dk, dv = 0.0, 0.0
-        for u in range(HEADS_AT_ONCE):
-            head = i * HEADS_AT_ONCE + u
-            q, g, p = q_ref[head], g_ref[head], probs[head]
+        for i in range(HEADS_AT_ONCE):
+            u = j * HEADS_AT_ONCE + i
+            q, g, p = q_ref[u], g_ref[u], probs[u]
             dp = dot_nt(v, g)
             pb = p.astype(bf16)
             delta = jnp.sum(pb.astype(f32) * dp, 0, keepdims=True)
             ds = (p * (dp - delta)).astype(bf16)
             dk = dk + dot(ds, q)
             dv = dv + dot(pb, g)
-        acc[:, :HD] += dk * SCALE
-        acc[:, HD:] += dv
+        out_ref[:, :HD] += dk * SCALE
+        out_ref[:, HD:] += dv
         return carry
 
     lax.fori_loop(0, q_ref.shape[0] // HEADS_AT_ONCE, body, 0)
-    total = acc[...]
-    squares = jnp.sum(total * total, 0, keepdims=True)
-    sum_ref[...] = squares_ref[...] + squares[:, :HD] + squares[:, HD:]
-    out_ref[:PROMPT] = total
-    out_ref[PROMPT:] = response_ref[...]
-
-
-def prompt_grad(probs, q, g, v, part, response, squares):
+
+
+def prompt_grad(probs, q, g, v):
+    n = q.shape[0]
+    block = lambda *dims: pl.BlockSpec((AT_ONCE,) + dims, lambda i: (i, 0, 0))
+    whole = lambda *dims: pl.BlockSpec(dims, lambda i: (0, 0))
     return pl.pallas_call(
         prompt_grad_kernel,
         name="prompt_grad",
         cost_estimate=about(5),
-        in_specs=[VMEM] * 7,
-        out_specs=[VMEM] * 2,
-        scratch_shapes=[pltpu.VMEM((PROMPT, 2 * HD), f32)],
-        out_shape=[shape((PROMPT + NRESP * RLEN, 2 * HD)), shape((1, HD))],
+        grid=(n // AT_ONCE,),
+        in_specs=[
+            block(PROMPT, PROMPT),
+            block(PROMPT, HD),
+            block(PROMPT, HD),
+            whole(PROMPT, HD),
+        ],
+        out_specs=whole(PROMPT, 2 * HD),
+        out_shape=shape((PROMPT, 2 * HD)),
         compiler_params=params(12),
-    )(kept(probs), q, g, v, part, response, squares)
+    )(in_hbm(probs), q, g, v)
+
+
+def response_grad_kernel(lens, probs, q_ref, g_ref, v_ref, part_ref, out_ref, sum_ref, acc):
+    i = pl.program_id(0)
+
+    @pl.when(i == 0)
+    def _():
+        acc[:PROMPT] = part_ref[...]
+        acc[PROMPT:] = jnp.zeros((RESP, 2 * HD), f32)
+
+    v1, v2 = v_ref[:PROMPT], v_ref[PROMPT:]
+    q = q_ref[...].reshape(AT_ONCE * RESP, HD)
+    g = g_ref[...].reshape(AT_ONCE * RESP, HD)
+    p1, p2 = probs[0, :PROMPT], probs[0, PROMPT:]
+    dp1, dp2 = dot_nt(v1, g), dot_nt(v2, g)
+    pb1, pb2 = p1.astype(bf16), p2.astype(bf16)
+    delta = jnp.sum(pb1.astype(f32) * dp1, 0, keepdims=True) + jnp.sum(
+        pb2.astype(f32) * dp2, 0, keepdims=True
+    )
+    ds1 = (p1 * (dp1 - delta)).astype(bf16)
+    ds2 = (p2 * (dp2 - delta)).astype(bf16)
+    acc[:PROMPT, :HD] += dot(ds1, q) * SCALE
+    acc[PROMPT:, :HD] += dot(ds2, q) * SCALE
+    acc[:PROMPT, HD:] += dot(pb1, g)
+    acc[PROMPT:, HD:] += dot(pb2, g)
+
+    @pl.when(i == pl.num_programs(0) - 1)
+    def _():
+        total = acc[...]
+        squares = jnp.sum(total * total, 0, keepdims=True)
+        sum_ref[...] = squares[:, :HD] + squares[:, HD:]
+        out_ref[:PROMPT] = total[:PROMPT]
+        left = total[PROMPT:]
+        spread = chosen_rows(lens, 1)
+        placed = jnp.zeros((NRESP * RLEN, 2 * HD), f32)
+        for _ in range(3):
+            term = left.astype(bf16)
+            placed = placed + dot(spread, term)
+            left = left - term.astype(f32)
+        out_ref[PROMPT:] = placed
+
+
+def response_grad(lens, probs, q, g, v, part):
+    n = q.shape[0]
+    rows = PROMPT + NRESP * RLEN
+    block = lambda *dims: pl.BlockSpec((AT_ONCE,) + dims, lambda i, a: (i, 0, 0))
+    whole = lambda *dims: pl.BlockSpec(dims, lambda i, a: (0, 0))
+    return pl.pallas_call(
+        response_grad_kernel,
+        name="response_grad",
+        cost_estimate=about(8),
+        grid_spec=pltpu.PrefetchScalarGridSpec(
+            num_scalar_prefetch=1,
+            grid=(n // AT_ONCE,),
+            in_specs=[
+                pl.BlockSpec((1, LIVE, AT_ONCE * RESP), lambda i, a: (i, 0, 0)),
+                block(RESP, HD),
+                block(RESP, HD),
+                whole(LIVE, HD),
+                whole(PROMPT, 2 * HD),
+            ],
+            out_specs=[whole(rows, 2 * HD), whole(1, HD)],
+            scratch_shapes=[pltpu.VMEM((LIVE, 2 * HD), f32)],
+        ),
+        out_shape=[shape((rows, 2 * HD)), shape((1, HD))],
+        compiler_params=params(12),
+    )(lens, in_hbm(probs), q, g, v, part)
 
 
 def ring(step, size=SIDE):
@@ -473,9 +532,7 @@
     my_x = lax.axis_index("x")
     my_y = lax.axis_index("y")
     place = (my_x * SIDE + my_y).reshape(1).astype(jnp.int32)
-    qp, qr, gp, gr, k, v = pack(
-        lens, place, hidden_stash[0], top_grads, key_stash[0], value_stash[0]
-    )
+    qp, qr, gp, gr = pack(lens, place, hidden_stash[0], top_grads)
     parts = jnp.arange(PLANE, dtype=jnp.int32)
     away = lambda slot: jnp.where(slot == 1, 3, jnp.where(slot == 2, 1, jnp.where(slot == 3, 2, 0)))
     outer, inner = away(parts // SIDE), away(parts % SIDE)
@@ -484,9 +541,11 @@
     plane = ("x", "y")
     swap = lambda a: lax.all_to_all(a, plane, 0, 0, tiled=True)
     after = lambda x, y: lax.optimization_barrier((x, y))[0]
-    row_k = jnp.stack(gathered(k, "y"))
-    col_v = jnp.stack(gathered(v, "x"))
+    row_k, col_v = stack_live(
+        lens, gathered(key_stash[0], "y"), gathered(value_stash[0], "x")
+    )
     row_k, col_v, qp = lax.optimization_barrier((row_k, col_v, qp))
+    k, v = row_k[0], col_v[0]
     my_qp = swap(qp)
     all_k = gathered_halves(row_k, "x")
     all_v = gathered_halves(col_v, "y")
@@ -494,46 +553,56 @@
     prob_p, key_p, value_p = prob(True, lens, k_from, v_from, my_qp, all_k, all_v)
     prob_r, key_r, value_r = prob(False, lens, k_from, v_from, my_qr, all_k, all_v)
     stash_p, stash_r = my_qp, my_qr
+    busy = (stage >= STAGES // 2).astype(jnp.int32).reshape(1)
+    actives = [(stage == now).astype(jnp.int32).reshape(1) for now in range(STAGES)]
+    lower = lambda a: lax.ppermute(a, "zl", [(now, now - 1)])
     for now in range(STAGES - 1, -1, -1):
-        active = (stage == now).astype(jnp.int32).reshape(1)
-        gp, stash_p = chain(True, active, gp, stash_p, prob_p, key_p, value_p)
         if now:
-            sent = lax.ppermute(gp, "zl", [(now, now - 1)])
+            gp, stash_p = chain(True, actives[now], gp, stash_p, prob_p, key_p, value_p)
+            if now == STAGES - 2:
+                own_p = own_prob(True, 1 - busy, lens, after(qp, gp), k)
+                own_r = own_prob(False, 1 - busy, lens, after(qr, own_p), k)
+            sent = lower(gp)
             gr = after(gr, gp if now == STAGES - 1 else sent)
             gp = sent
-        else:
-            gr, stash_p = lax.optimization_barrier((gr, stash_p))
-        gr, stash_r = chain(False, active, gr, stash_r, prob_r, key_r, value_r)
+        if now == 1:
+            gp, stash_p = chain(True, actives[0], gp, stash_p, prob_p, key_p, value_p)
+            own_gp = swap(stash_p)
+            gr = after(gr, stash_p)
+        gr, stash_r = chain(False, actives[now], gr, stash_r, prob_r, key_r, value_r)
+        if now == STAGES - 2:
+            gp = after(gp, own_r)
         if now:
             gp = after(gp, gr)
-            gr = lax.ppermute(gr, "zl", [(now, now - 1)])
-    own_gr, own_gp = swap(stash_r), swap(after(stash_p, gr))
-    qp, qr = after(qp, gr), after(qr, gr)
-    own_r = own_prob(False, lens, qr, k)
-    part, response, squares = response_grad(lens, own_r, qr, own_gr, v)
-    own_p = own_prob(True, lens, qp, k)
-    raw, squares = prompt_grad(own_p, qp, own_gp, v, part, response, squares)
-    for axes, size in ((plane, PLANE), (("zl", "tp"), STAGES * lax.axis_size("tp"))):
+            gr = lower(gr)
+    own_p = own_prob(True, busy, lens, after(qp, gr), k, own_p)
+    own_gr = swap(stash_r)
+    part = prompt_grad(after(own_p, gr), qp, own_gp, v)
+    own_r = own_prob(False, busy, lens, after(qr, part), k, own_r)
+    raw, squares = response_grad(lens, own_r, qr, own_gr, v, part)
+    for axes in (("x", "y", "core"), ("zl", "zh")):
+        size = lax.axis_size(axes)
         spread = jnp.broadcast_to(squares, (size, HD))
         squares = jnp.sum(lax.all_to_all(spread, axes, 0, 0, tiled=True), 0, keepdims=True)
     square_sum = jnp.sum(squares)
-    entries = STAGES * PLANE * lax.axis_size("tp") * raw.shape[0] * raw.shape[1]
+    entries = STAGES * PLANE * lax.axis_size(("zh", "core")) * raw.shape[0] * raw.shape[1]
     clip_limit = clip_rms * math.sqrt(entries)
     factor = clip_limit / jnp.maximum(jnp.sqrt(square_sum), clip_limit)
     return (raw * factor)[None]
 
 
 def solution(mesh):
-    parts = mesh.devices.reshape(STAGES, SIDE, SIDE, -1)
-    finer = Mesh(parts, ("zl", "x", "y", "tp"))
+    parts = mesh.devices.reshape(STAGES, SIDE, SIDE, 2, -1)
+    finer = Mesh(parts, ("zl", "x", "y", "zh", "core"))
+    tp = ("zh", "core")
     pipe = ("zl", "x", "y")
     placed = (
-        P(pipe, None, "tp"),
-        P(pipe, None, "tp"),
-        P(pipe, None, "tp"),
-        P(None, "tp"),
+        P(pipe, None, tp),
+        P(pipe, None, tp),
+        P(pipe, None, tp),
+        P(None, tp),
         P(),
     )
     return jax.shard_map(
-        on_device, mesh=finer, in_specs=placed, out_specs=P(pipe, None, "tp"), check_vma=False
+        on_device, mesh=finer, in_specs=placed, out_specs=P(pipe, None, tp), check_vma=False
     )

time: 214 us -> 190 us (0.89)
  waiting for transfers between devices: 57.1 us -> 39.2 us
  local copies, waits for them, and re-layouts: 11.6 us -> 2.89 us
  Pallas kernels: 58.5 us -> 63.2 us
    ppermute x6, waiting for transfers between devices: 29.8 us -> 15.2 us  [on_device(): lower = lambda a: lax.ppermute(a, 'zl', [(now, now - 1)])]
    unnamed x24 -> x10, local copies, waits for them, and re-layouts: 8.73 us -> 0.02 us
    pallas_call x2 -> x4, Pallas kernels: 7.3 us -> 11.6 us  [own_prob(): pl.pallas_call(functools.partial(own_prob_kernel, prompt), name='own_prom...]
    ppermute x2, starting transfers between devices: 2.59 us -> 0.01 us  [gathered_halves(): lax.ppermute(low[:half], axis, ring(1))]
    ppermute x6, waiting for transfers between devices: 3.78 us -> 1.4 us  [gathered(): lax.ppermute(block, axis, ring(step))]
  transfers between devices with their start and end apart: 24 -> 24, of which waited for: 7 -> 7; matrix products, arithmetic and copies ran while one was open for 2% -> 2% of each run, Pallas kernels for 19% -> 25%
where the time goes in v5:
time: 190 us; the launch traced here: 189 us
  Pallas kernels  63.2 us (33%)
  starting transfers between devices  47.6 us (25%)
  waiting for transfers between devices  39.2 us (21%)
  blocking collectives  33.4 us (18%)
  local copies, waits for them, and re-layouts  2.89 us (2%)
    all_to_all x2, blocking collectives, on_device(): lax.all_to_all(spread, axes, 0, 0, tiled=True)  33.4 us
    all_to_all x4, starting transfers between devices, on_device(): swap = lambda a: lax.all_to_all(a, plane, 0, 0, tiled=True)  22.9 us
    pallas_call x8, Pallas kernels, chain(): pl.pallas_call(functools.partial(chain_kernel, prompt), name='prompt_chai...  17.7 us
    pallas_call x2, Pallas kernels, prob(): pl.pallas_call(functools.partial(prob_kernel, prompt), name='prompt_prob'...  16.8 us
    ppermute x4, waiting for transfers between devices, gathered_halves(): low, high = (lax.ppermute(block, axis, ring(step)) for step in (1, -1))  16.3 us
    ppermute x6, waiting for transfers between devices, on_device(): lower = lambda a: lax.ppermute(a, 'zl', [(now, now - 1)])  15.2 us
    pallas_call x4, Pallas kernels, own_prob(): pl.pallas_call(functools.partial(own_prob_kernel, prompt), name='own_prom...  11.6 us
    ppermute x6, starting transfers between devices, gathered(): lax.ppermute(block, axis, ring(step))  9.42 us
  transfers between devices with their start and end apart: 24, of which 7 were waited for; matrix products, arithmetic and copies ran while one was open for 2% of the time, Pallas kernels for 25%

profile of v5, /device:TPU:1, one launch (start us, length us, event | category | flops | bytes accessed | tf_op | source)
XLA Modules:
  0.0 189.0 jit_solution(5206160524650018192)
XLA Ops:
  0.0 3.7 %collective-permute-start.2 = (bf16[512,128]{1,0:T(8,128)(2,1)}, bf16[512,128]{1,0:T(8,128)(2,1)S(1)}, u32[]{:S(2)}, u32[]{:S(2)}) collective-permute-start(bf16[512,128]{1,0:T(8,128)(2,1)} %bitcast.19), channel_id=1, source_target_pairs={{0,8},{4,12},{8,0},{12,4},{1,9},{5,13},{9,1},{13,5},{2,10},{6,14},... | collective-permute-start | bytes 393224 | tf_op jit(solution)/shard_map/ppermute | solution.py:515
  3.7 0.8 collective-permute-start.1
  4.5 0.7 collective-permute-start
  5.2 2.7 %collective-permute-start.5 = (bf16[512,128]{1,0:T(8,128)(2,1)}, bf16[512,128]{1,0:T(8,128)(2,1)S(1)}, u32[]{:S(2)}, u32[]{:S(2)}) collective-permute-start(bf16[512,128]{1,0:T(8,128)(2,1)} %bitcast.23), channel_id=1, source_target_pairs={{0,32},{16,48},{32,0},{48,16},{1,33},{17,49},{33,1},{49,17},{2,34}... | collective-permute-start | bytes 393224 | tf_op jit(solution)/shard_map/ppermute | solution.py:515
  8.0 0.9 collective-permute-start.4
  8.8 0.6 collective-permute-start.3
  9.4 3.8 %pack.1 = (bf16[16,256,128]{2,1,0:T(8,128)(2,1)}, bf16[16,192,128]{2,1,0:T(8,128)(2,1)}, bf16[256,128]{1,0:T(8,128)(2,1)}, bf16[192,128]{1,0:T(8,128)(2,1)}) custom-call(s32[4]{0:T(128)} %lens.17, s32[1]{0:T(128)} %bitcast.1.place, bf16[512,2048]{1,0:T(8,128)(2,1)} %bitcast.29, bf16[512,2048]{1,0:T(8,128)(2,1)} %top_ref.1), custom_call_target="tpu_custom_call" | custom-call | flops 4000000000 | tf_op jit(solution)/shard_map/pack/pallas_call | solution.py:115
  13.3 1.3 collective-permute-done.3.refs_5_
  14.6 0.9 stack_live.1
  15.6 5.0 %all-to-all-start = ((bf16[16,256,128]{2,1,0:T(8,128)(2,1)}), bf16[16,256,128]{2,1,0:T(8,128)(2,1)}, u32[]{:S(2)}, u32[]{:S(2)}) async-start(bf16[16,256,128]{2,1,0:T(8,128)(2,1)} %get-tuple-element.89.q_ref), calls=%async_computation | async-start | bytes 2097152 | tf_op jit(solution)/shard_map/all_to_all | solution.py:542
  20.6 2.5 %collective-permute-start.7 = (bf16[4,448,128]{2,1,0:T(8,128)(2,1)S(1)}, bf16[4,448,128]{2,1,0:T(8,128)(2,1)S(1)}, u32[]{:S(2)}, u32[]{:S(2)}) collective-permute-start(bf16[4,448,128]{2,1,0:T(8,128)(2,1)S(1)} %get-tuple-element.57.refs_0_), channel_id=1, source_target_pairs={{0,48},{16,0},{32,16},{48,32},{1,49},{17,1},{33,17},{49,33},{2,50}... | collective-permute-start | bytes 1376264 | tf_op jit(solution)/shard_map/ppermute | solution.py:519
  23.1 2.4 %collective-permute-start.11 = (bf16[4,448,128]{2,1,0:T(8,128)(2,1)S(1)}, bf16[4,448,128]{2,1,0:T(8,128)(2,1)S(1)}, u32[]{:S(2)}, u32[]{:S(2)}) collective-permute-start(bf16[4,448,128]{2,1,0:T(8,128)(2,1)S(1)} %get-tuple-element.58.refs_5_), channel_id=1, source_target_pairs={{0,12},{4,0},{8,4},{12,8},{1,13},{5,1},{9,5},{13,9},{2,14},{6,2},{... | collective-permute-start | bytes 1376264 | tf_op jit(solution)/shard_map/ppermute | solution.py:519
  25.5 16.3 %collective-permute-done.7.refs_2_ = bf16[4,448,128]{2,1,0:T(8,128)(2,1)S(1)} collective-permute-done((bf16[4,448,128]{2,1,0:T(8,128)(2,1)S(1)}, bf16[4,448,128]{2,1,0:T(8,128)(2,1)S(1)}, u32[]{:S(2)}, u32[]{:S(2)}) %collective-permute-start.7) | collective-permute-done | bytes 458784 | tf_op jit(solution)/shard_map/ppermute | solution.py:519
  41.8 0.7 slice.25
  42.5 2.5 %collective-permute-start.9 = (bf16[2,448,128]{2,1,0:T(8,128)(2,1)}, bf16[2,448,128]{2,1,0:T(8,128)(2,1)S(1)}, u32[]{:S(2)}, u32[]{:S(2)}) collective-permute-start(bf16[2,448,128]{2,1,0:T(8,128)(2,1)} %slice.25), channel_id=1, source_target_pairs={{0,48},{16,0},{32,16},{48,32},{1,49},{17,1},{33,17},{49,33},{2,50}... | collective-permute-start | bytes 688136 | tf_op jit(solution)/shard_map/ppermute | solution.py:526
  45.0 0.7 slice.24
  45.8 0.7 slice.27
  46.5 2.6 %collective-permute-start.13 = (bf16[2,448,128]{2,1,0:T(8,128)(2,1)}, bf16[2,448,128]{2,1,0:T(8,128)(2,1)}, u32[]{:S(2)}, u32[]{:S(2)}) collective-permute-start(bf16[2,448,128]{2,1,0:T(8,128)(2,1)} %slice.27), channel_id=1, source_target_pairs={{0,12},{4,0},{8,4},{12,8},{1,13},{5,1},{9,5},{13,9},{2,14},{6,2},{... | collective-permute-start | bytes 688136 | tf_op jit(solution)/shard_map/ppermute | solution.py:526
  49.1 0.7 slice.26
  49.8 6.5 %all-to-all-start.1 = ((bf16[16,192,128]{2,1,0:T(8,128)(2,1)}), bf16[16,192,128]{2,1,0:T(8,128)(2,1)}, u32[]{:S(2)}, u32[]{:S(2)}) async-start(bf16[16,192,128]{2,1,0:T(8,128)(2,1)} %get-tuple-element.91.q_ref), calls=%async_computation.1 | async-start | bytes 1572864 | tf_op jit(solution)/shard_map/all_to_all | solution.py:542
  56.4 7.3 %prompt_prob.1 = (f32[16,256,384]{2,1,0:T(8,128)}, bf16[16,256,128]{2,1,0:T(8,128)(2,1)}, bf16[16,256,128]{2,1,0:T(8,128)(2,1)}) custom-call(s32[4]{0:T(128)S(1)} %copy-done.2, s32[16]{0:T(128)S(1)} %get-tuple-element.95.k_from, s32[16]{0:T(128)S(1)} %get-tuple-element.96.v_from, bf16[16,256,128]{2,1,0:T(8,128)(2,1)} %all-to-all-done.q_ref.stash_in, ...), custom_call_target="tpu_custom_call" | custom-call | flops 7000000000 | tf_op jit(solution)/shard_map/prompt_prob/pallas_call | solution.py:230
  63.9 0.7 collective-permute-start.15
  64.6 2.5 %all-to-all-done.1.q_ref.stash_in = bf16[16,192,128]{2,1,0:T(8,128)(2,1)} async-done(((bf16[16,192,128]{2,1,0:T(8,128)(2,1)}), bf16[16,192,128]{2,1,0:T(8,128)(2,1)}, u32[]{:S(2)}, u32[]{:S(2)}) %all-to-all-start.1) | async-done | bytes 786464 | tf_op jit(solution)/shard_map/all_to_all | solution.py:542
  67.1 9.5 %response_prob.1 = (f32[16,192,640]{2,1,0:T(8,128)}, bf16[16,448,128]{2,1,0:T(8,128)(2,1)}, bf16[16,448,128]{2,1,0:T(8,128)(2,1)}) custom-call(s32[4]{0:T(128)S(1)} %copy-done.2, s32[16]{0:T(128)S(1)} %get-tuple-element.95.k_from, s32[16]{0:T(128)S(1)} %get-tuple-element.96.v_from, bf16[16,192,128]{2,1,0:T(8,128)(2,1)} %all-to-all-done.1.q_ref.stash_in, ...), custom_call_target="tpu_custom_call" | custom-call | flops 7000000000 | tf_op jit(solution)/shard_map/response_prob/pallas_call | solution.py:230
  76.8 0.7 collective-permute-start.14
  77.5 0.2 prompt_chain.5
  77.7 0.7 collective-permute-start.16
  78.4 5.0 %own_prompt_prob.2.refs_0_ = f32[16,256,256]{2,1,0:T(8,128)} custom-call(s32[1]{0:T(128)S(6)} %sub.11.active, s32[4]{0:T(128)S(1)} %copy-done.2, bf16[16,256,128]{2,1,0:T(8,128)(2,1)} %get-tuple-element.89.q_ref, bf16[448,128]{1,0:T(8,128)(2,1)S(1)} %slice_bitcast_fusion.1.k_ref), custom_call_target="tpu_custom_call" | custom-call | flops 5000000000 | tf_op jit(solution)/shard_map/own_prompt_prob/pallas_call | solution.py:378
  83.3 5.4 %own_response_prob.2.refs_0_ = f32[4,448,768]{2,1,0:T(8,128)} custom-call(s32[1]{0:T(128)S(6)} %sub.11.active, s32[4]{0:T(128)S(1)} %copy-done.2, bf16[16,192,128]{2,1,0:T(8,128)(2,1)} %get-tuple-element.91.q_ref, bf16[448,128]{1,0:T(8,128)(2,1)S(1)} %slice_bitcast_fusion.1.k_ref), custom_call_target="tpu_custom_call" | custom-call | flops 5000000000 | tf_op jit(solution)/shard_map/own_response_prob/pallas_call | solution.py:378
  89.0 0.2 prompt_chain.6
  89.2 1.3 collective-permute-start.18
  90.5 0.7 collective-permute-start.17
  91.2 11.1 %collective-permute-done.18.g_in = bf16[256,128]{1,0:T(8,128)(2,1)S(1)} collective-permute-done((bf16[256,128]{1,0:T(8,128)(2,1)S(1)}, bf16[256,128]{1,0:T(8,128)(2,1)S(1)}, u32[]{:S(2)}, u32[]{:S(2)}) %collective-permute-start.18) | collective-permute-done | bytes 65568 | tf_op jit(solution)/shard_map/ppermute | solution.py:558
  102.3 8.0 %prompt_chain.7 = (bf16[256,128]{1,0:T(8,128)(2,1)}, bf16[16,256,128]{2,1,0:T(8,128)(2,1)}) custom-call(s32[1]{0:T(128)} %bitcast.5.active, bf16[256,128]{1,0:T(8,128)(2,1)S(1)} %collective-permute-done.18.g_in, bf16[16,256,128]{2,1,0:T(8,128)(2,1)} %get-tuple-element.82.stash_in, ...), custom_call_target="tpu_custom_call", output_to_operand_aliasing={{1}: (2, {})} | custom-call | flops 7000000000 | tf_op jit(solution)/shard_map/prompt_chain/pallas_call | solution.py:314
  110.5 1.3 collective-permute-start.19
  111.8 4.7 %all-to-all-start.2 = ((bf16[16,256,128]{2,1,0:T(8,128)(2,1)}), bf16[16,256,128]{2,1,0:T(8,128)(2,1)S(1)}, u32[]{:S(2)}, u32[]{:S(2)}) async-start(bf16[16,256,128]{2,1,0:T(8,128)(2,1)} %get-tuple-element.83), calls=%async_computation.2 | async-start | bytes 2097152 | tf_op jit(solution)/shard_map/all_to_all | solution.py:542
  116.6 4.2 %collective-permute-done.19.g_in = bf16[192,128]{1,0:T(8,128)(2,1)S(1)} collective-permute-done((bf16[192,128]{1,0:T(8,128)(2,1)S(1)}, bf16[192,128]{1,0:T(8,128)(2,1)S(1)}, u32[]{:S(2)}, u32[]{:S(2)}) %collective-permute-start.19) | collective-permute-done | bytes 49184 | tf_op jit(solution)/shard_map/ppermute | solution.py:558
  120.7 8.6 %response_chain.7 = (bf16[192,128]{1,0:T(8,128)(2,1)}, bf16[16,192,128]{2,1,0:T(8,128)(2,1)}) custom-call(s32[1]{0:T(128)} %bitcast.5.active, bf16[192,128]{1,0:T(8,128)(2,1)S(1)} %collective-permute-done.19.g_in, bf16[16,192,128]{2,1,0:T(8,128)(2,1)} %get-tuple-element.87.stash_in, ...), custom_call_target="tpu_custom_call", output_to_operand_aliasing={{1}: (2, {})} | custom-call | flops 7000000000 | tf_op jit(solution)/shard_map/response_chain/pallas_call | solution.py:314
  129.3 0.6 own_prompt_prob.3.probs
  129.9 6.6 %all-to-all-start.3 = ((bf16[16,192,128]{2,1,0:T(8,128)(2,1)}), bf16[16,192,128]{2,1,0:T(8,128)(2,1)S(1)}, u32[]{:S(2)}, u32[]{:S(2)}) async-start(bf16[16,192,128]{2,1,0:T(8,128)(2,1)} %get-tuple-element.92), calls=%async_computation.3 | async-start | bytes 1572864 | tf_op jit(solution)/shard_map/all_to_all | solution.py:542
  136.5 6.0 %prompt_grad.1.part_ref = f32[256,256]{1,0:T(8,128)S(1)} custom-call(f32[16,256,256]{2,1,0:T(8,128)} %own_prompt_prob.3.probs, bf16[16,256,128]{2,1,0:T(8,128)(2,1)} %get-tuple-element.89.q_ref, bf16[16,256,128]{2,1,0:T(8,128)(2,1)S(1)} %all-to-all-done.2.g_ref, bf16[448,128]{1,0:T(8,128)(2,1)S(1)} %slice_bitcast_fusion.v_ref), custom_call_target="tpu_custom_call" | custom-call | flops 5000000000 | tf_op jit(solution)/shard_map/prompt_grad/pallas_call | solution.py:426
  142.5 0.6 own_response_prob.3.probs
  143.1 3.8 %all-to-all-done.3.g_ref = bf16[16,192,128]{2,1,0:T(8,128)(2,1)S(1)} async-done(((bf16[16,192,128]{2,1,0:T(8,128)(2,1)}), bf16[16,192,128]{2,1,0:T(8,128)(2,1)S(1)}, u32[]{:S(2)}, u32[]{:S(2)}) %all-to-all-start.3) | async-done | bytes 786464 | tf_op jit(solution)/shard_map/all_to_all | solution.py:542
  146.9 6.4 %response_grad.1 = (f32[512,256]{1,0:T(8,128)S(1)}, f32[1,128]{1,0:T(1,128)S(1)}) custom-call(s32[4]{0:T(128)S(1)} %copy-done.2, f32[4,448,768]{2,1,0:T(8,128)} %own_response_prob.3.probs, bf16[16,192,128]{2,1,0:T(8,128)(2,1)} %get-tuple-element.91.q_ref, bf16[16,192,128]{2,1,0:T(8,128)(2,1)S(1)} %all-to-all-done.3.g_ref, ...), custom_call_target="tpu_custom_call" | custom-call | flops 8000000000 | tf_op jit(solution)/shard_map/response_grad/pallas_call | solution.py:488
  153.3 17.8 %all_to_all.32 = f32[32,1,128]{2,1,0:T(1,128)S(1)} all-to-all(f32[32,1,128]{2,1,0:T(1,128)S(1)} %broadcast_in_dim.26), channel_id=1, replica_groups=mesh['zl'=4,'x'=4,'y'=4,'zh'=2,'core'=2] {'x','y','core'}, dimensions={0} | all-to-all | bytes 32768 | tf_op jit(solution)/shard_map/all_to_all | solution.py:586
  171.2 15.6 %all_to_all.33 = f32[8,1,128]{2,1,0:T(1,128)S(1)} all-to-all(f32[8,1,128]{2,1,0:T(1,128)S(1)} %broadcast_in_dim.27), channel_id=1, replica_groups=mesh['zl'=4,'x'=4,'y'=4,'zh'=2,'core'=2] {'zl','zh'}, dimensions={0} | all-to-all | bytes 8192 | tf_op jit(solution)/shard_map/all_to_all | solution.py:586
  186.8 0.6 reduce_sum.20
  188.1 0.8 multiply_bitcast_fusion
  (42 shorter events, 1.0 us)
Async XLA Ops:
  0.0 8.8 %collective-permute-start.2 = (bf16[512,128]{1,0:T(8,128)(2,1)}, bf16[512,128]{1,0:T(8,128)(2,1)S(1)}, u32[]{:S(2)}, u32[]{:S(2)}) collective-permute-start(bf16[512,128]{1,0:T(8,128)(2,1)} %bitcast.19), channel_id=1, source_target_pairs={{0,8},{4,12},{8,0},{12,4},{1,9},{5,13},{9,1},{13,5},{2,10},{6,14},... | collective-permute-start | bytes 393224 | tf_op jit(solution)/shard_map/ppermute | solution.py:515
  3.7 9.5 %collective-permute-start.1 = (bf16[512,128]{1,0:T(8,128)(2,1)}, bf16[512,128]{1,0:T(8,128)(2,1)S(1)}, u32[]{:S(2)}, u32[]{:S(2)}) collective-permute-start(bf16[512,128]{1,0:T(8,128)(2,1)} %bitcast.20), channel_id=1, source_target_pairs={{0,12},{4,0},{8,4},{12,8},{1,13},{5,1},{9,5},{13,9},{2,14},{6,2},{... | collective-permute-start | bytes 393224 | tf_op jit(solution)/shard_map/ppermute | solution.py:515
  4.5 8.7 %collective-permute-start = (bf16[512,128]{1,0:T(8,128)(2,1)}, bf16[512,128]{1,0:T(8,128)(2,1)S(1)}, u32[]{:S(2)}, u32[]{:S(2)}) collective-permute-start(bf16[512,128]{1,0:T(8,128)(2,1)} %bitcast.21), channel_id=1, source_target_pairs={{0,4},{4,8},{8,12},{12,0},{1,5},{5,9},{9,13},{13,1},{2,6},{6,10},{... | collective-permute-start | bytes 393224 | tf_op jit(solution)/shard_map/ppermute | solution.py:515
  5.2 8.0 %collective-permute-start.5 = (bf16[512,128]{1,0:T(8,128)(2,1)}, bf16[512,128]{1,0:T(8,128)(2,1)S(1)}, u32[]{:S(2)}, u32[]{:S(2)}) collective-permute-start(bf16[512,128]{1,0:T(8,128)(2,1)} %bitcast.23), channel_id=1, source_target_pairs={{0,32},{16,48},{32,0},{48,16},{1,33},{17,49},{33,1},{49,17},{2,34}... | collective-permute-start | bytes 393224 | tf_op jit(solution)/shard_map/ppermute | solution.py:515
  8.0 5.3 %collective-permute-start.4 = (bf16[512,128]{1,0:T(8,128)(2,1)}, bf16[512,128]{1,0:T(8,128)(2,1)S(1)}, u32[]{:S(2)}, u32[]{:S(2)}) collective-permute-start(bf16[512,128]{1,0:T(8,128)(2,1)} %bitcast.24), channel_id=1, source_target_pairs={{0,48},{16,0},{32,16},{48,32},{1,49},{17,1},{33,17},{49,33},{2,50}... | collective-permute-start | bytes 393224 | tf_op jit(solution)/shard_map/ppermute | solution.py:515
  8.8 5.8 %collective-permute-start.3 = (bf16[512,128]{1,0:T(8,128)(2,1)}, bf16[512,128]{1,0:T(8,128)(2,1)S(1)}, u32[]{:S(2)}, u32[]{:S(2)}) collective-permute-start(bf16[512,128]{1,0:T(8,128)(2,1)} %bitcast.25), channel_id=1, source_target_pairs={{0,16},{16,32},{32,48},{48,0},{1,17},{17,33},{33,49},{49,1},{2,18}... | collective-permute-start | bytes 393224 | tf_op jit(solution)/shard_map/ppermute | solution.py:515
  9.4 5.2 %copy-start = (bf16[1,512,128]{2,1,0:T(8,128)(2,1)S(1)}, bf16[1,512,128]{2,1,0:T(8,128)(2,1)}, u32[]{:S(2)}) copy-start(bf16[1,512,128]{2,1,0:T(8,128)(2,1)} %param.6) | copy-start | bytes 393220
  9.4 5.2 %copy-start.1 = (bf16[1,512,128]{2,1,0:T(8,128)(2,1)S(1)}, bf16[1,512,128]{2,1,0:T(8,128)(2,1)}, u32[]{:S(2)}) copy-start(bf16[1,512,128]{2,1,0:T(8,128)(2,1)} %param.7) | copy-start | bytes 393220
  9.4 5.2 %copy-start.2 = (s32[4]{0:T(128)S(1)}, s32[4]{0:T(128)}, u32[]{:S(2)}) copy-start(s32[4]{0:T(128)} %lens.17) | copy-start | bytes 52
  15.6 34.3 %all-to-all-start = ((bf16[16,256,128]{2,1,0:T(8,128)(2,1)}), bf16[16,256,128]{2,1,0:T(8,128)(2,1)}, u32[]{:S(2)}, u32[]{:S(2)}) async-start(bf16[16,256,128]{2,1,0:T(8,128)(2,1)} %get-tuple-element.89.q_ref), calls=%async_computation | async-start | bytes 2097152 | tf_op jit(solution)/shard_map/all_to_all | solution.py:542
  20.6 21.2 %collective-permute-start.7 = (bf16[4,448,128]{2,1,0:T(8,128)(2,1)S(1)}, bf16[4,448,128]{2,1,0:T(8,128)(2,1)S(1)}, u32[]{:S(2)}, u32[]{:S(2)}) collective-permute-start(bf16[4,448,128]{2,1,0:T(8,128)(2,1)S(1)} %get-tuple-element.57.refs_0_), channel_id=1, source_target_pairs={{0,48},{16,0},{32,16},{48,32},{1,49},{17,1},{33,17},{49,33},{2,50}... | collective-permute-start | bytes 1376264 | tf_op jit(solution)/shard_map/ppermute | solution.py:519
  23.1 21.9 %collective-permute-start.6 = (bf16[4,448,128]{2,1,0:T(8,128)(2,1)S(1)}, bf16[4,448,128]{2,1,0:T(8,128)(2,1)S(1)}, u32[]{:S(2)}, u32[]{:S(2)}) collective-permute-start(bf16[4,448,128]{2,1,0:T(8,128)(2,1)S(1)} %get-tuple-element.57.refs_0_), channel_id=1, source_target_pairs={{0,16},{16,32},{32,48},{48,0},{1,17},{17,33},{33,49},{49,1},{2,18}... | collective-permute-start | bytes 1376264 | tf_op jit(solution)/shard_map/ppermute | solution.py:519
  23.1 22.6 %collective-permute-start.11 = (bf16[4,448,128]{2,1,0:T(8,128)(2,1)S(1)}, bf16[4,448,128]{2,1,0:T(8,128)(2,1)S(1)}, u32[]{:S(2)}, u32[]{:S(2)}) collective-permute-start(bf16[4,448,128]{2,1,0:T(8,128)(2,1)S(1)} %get-tuple-element.58.refs_5_), channel_id=1, source_target_pairs={{0,12},{4,0},{8,4},{12,8},{1,13},{5,1},{9,5},{13,9},{2,14},{6,2},{... | collective-permute-start | bytes 1376264 | tf_op jit(solution)/shard_map/ppermute | solution.py:519
  25.5 23.6 %collective-permute-start.10 = (bf16[4,448,128]{2,1,0:T(8,128)(2,1)S(1)}, bf16[4,448,128]{2,1,0:T(8,128)(2,1)S(1)}, u32[]{:S(2)}, u32[]{:S(2)}) collective-permute-start(bf16[4,448,128]{2,1,0:T(8,128)(2,1)S(1)} %get-tuple-element.58.refs_5_), channel_id=1, source_target_pairs={{0,4},{4,8},{8,12},{12,0},{1,5},{5,9},{9,13},{13,1},{2,6},{6,10},{... | collective-permute-start | bytes 1376264 | tf_op jit(solution)/shard_map/ppermute | solution.py:519
  42.5 13.9 %collective-permute-start.9 = (bf16[2,448,128]{2,1,0:T(8,128)(2,1)}, bf16[2,448,128]{2,1,0:T(8,128)(2,1)S(1)}, u32[]{:S(2)}, u32[]{:S(2)}) collective-permute-start(bf16[2,448,128]{2,1,0:T(8,128)(2,1)} %slice.25), channel_id=1, source_target_pairs={{0,48},{16,0},{32,16},{48,32},{1,49},{17,1},{33,17},{49,33},{2,50}... | collective-permute-start | bytes 688136 | tf_op jit(solution)/shard_map/ppermute | solution.py:526
  45.7 10.6 %collective-permute-start.8 = (bf16[2,448,128]{2,1,0:T(8,128)(2,1)}, bf16[2,448,128]{2,1,0:T(8,128)(2,1)S(1)}, u32[]{:S(2)}, u32[]{:S(2)}) collective-permute-start(bf16[2,448,128]{2,1,0:T(8,128)(2,1)} %slice.24), channel_id=1, source_target_pairs={{0,16},{16,32},{32,48},{48,0},{1,17},{17,33},{33,49},{49,1},{2,18}... | collective-permute-start | bytes 688136 | tf_op jit(solution)/shard_map/ppermute | solution.py:525
  46.5 9.9 %collective-permute-start.13 = (bf16[2,448,128]{2,1,0:T(8,128)(2,1)}, bf16[2,448,128]{2,1,0:T(8,128)(2,1)}, u32[]{:S(2)}, u32[]{:S(2)}) collective-permute-start(bf16[2,448,128]{2,1,0:T(8,128)(2,1)} %slice.27), channel_id=1, source_target_pairs={{0,12},{4,0},{8,4},{12,8},{1,13},{5,1},{9,5},{13,9},{2,14},{6,2},{... | collective-permute-start | bytes 688136 | tf_op jit(solution)/shard_map/ppermute | solution.py:526
  49.8 6.6 %collective-permute-start.12 = (bf16[2,448,128]{2,1,0:T(8,128)(2,1)}, bf16[2,448,128]{2,1,0:T(8,128)(2,1)}, u32[]{:S(2)}, u32[]{:S(2)}) collective-permute-start(bf16[2,448,128]{2,1,0:T(8,128)(2,1)} %slice.26), channel_id=1, source_target_pairs={{0,4},{4,8},{8,12},{12,0},{1,5},{5,9},{9,13},{13,1},{2,6},{6,10},{... | collective-permute-start | bytes 688136 | tf_op jit(solution)/shard_map/ppermute | solution.py:525
  49.8 17.3 %all-to-all-start.1 = ((bf16[16,192,128]{2,1,0:T(8,128)(2,1)}), bf16[16,192,128]{2,1,0:T(8,128)(2,1)}, u32[]{:S(2)}, u32[]{:S(2)}) async-start(bf16[16,192,128]{2,1,0:T(8,128)(2,1)} %get-tuple-element.91.q_ref), calls=%async_computation.1 | async-start | bytes 1572864 | tf_op jit(solution)/shard_map/all_to_all | solution.py:542
  56.4 7.3 %copy-start.3 = (bf16[256,128]{1,0:T(8,128)(2,1)S(1)}, bf16[256,128]{1,0:T(8,128)(2,1)}, u32[]{:S(2)}) copy-start(bf16[256,128]{1,0:T(8,128)(2,1)} %get-tuple-element.56.g_in) | copy-start | bytes 196612
  63.9 13.6 %collective-permute-start.15 = (bf16[256,128]{1,0:T(8,128)(2,1)S(1)}, bf16[256,128]{1,0:T(8,128)(2,1)S(1)}, u32[]{:S(2)}, u32[]{:S(2)}) collective-permute-start(bf16[256,128]{1,0:T(8,128)(2,1)S(1)} %get-tuple-element.62), channel_id=1, source_target_pairs={{192,128},{193,129},{194,130},{195,131},{196,132},{197,133},{198,1... | collective-permute-start | bytes 196616 | tf_op jit(solution)/shard_map/ppermute | solution.py:558
  67.1 9.5 %copy-start.4 = (bf16[192,128]{1,0:T(8,128)(2,1)S(1)}, bf16[192,128]{1,0:T(8,128)(2,1)}, u32[]{:S(2)}) copy-start(bf16[192,128]{1,0:T(8,128)(2,1)} %get-tuple-element.63.g_in) | copy-start | bytes 147460
  76.8 12.0 %collective-permute-start.14 = (bf16[192,128]{1,0:T(8,128)(2,1)S(1)}, bf16[192,128]{1,0:T(8,128)(2,1)S(1)}, u32[]{:S(2)}, u32[]{:S(2)}) collective-permute-start(bf16[192,128]{1,0:T(8,128)(2,1)S(1)} %get-tuple-element.68), channel_id=1, source_target_pairs={{192,128},{193,129},{194,130},{195,131},{196,132},{197,133},{198,1... | collective-permute-start | bytes 147464 | tf_op jit(solution)/shard_map/ppermute | solution.py:558
  77.7 11.1 %collective-permute-start.16 = (bf16[256,128]{1,0:T(8,128)(2,1)S(1)}, bf16[256,128]{1,0:T(8,128)(2,1)S(1)}, u32[]{:S(2)}, u32[]{:S(2)}) collective-permute-start(bf16[256,128]{1,0:T(8,128)(2,1)S(1)} %get-tuple-element.71), channel_id=1, source_target_pairs={{128,64},{129,65},{130,66},{131,67},{132,68},{133,69},{134,70},{13... | collective-permute-start | bytes 196616 | tf_op jit(solution)/shard_map/ppermute | solution.py:558
  89.2 13.1 %collective-permute-start.18 = (bf16[256,128]{1,0:T(8,128)(2,1)S(1)}, bf16[256,128]{1,0:T(8,128)(2,1)S(1)}, u32[]{:S(2)}, u32[]{:S(2)}) collective-permute-start(bf16[256,128]{1,0:T(8,128)(2,1)S(1)} %get-tuple-element.80), channel_id=1, source_target_pairs={{64,0},{65,1},{66,2},{67,3},{68,4},{69,5},{70,6},{71,7},{72,8},{73... | collective-permute-start | bytes 196616 | tf_op jit(solution)/shard_map/ppermute | solution.py:558
  90.5 0.7 collective-permute-start.17
  110.5 10.2 %collective-permute-start.19 = (bf16[192,128]{1,0:T(8,128)(2,1)S(1)}, bf16[192,128]{1,0:T(8,128)(2,1)S(1)}, u32[]{:S(2)}, u32[]{:S(2)}) collective-permute-start(bf16[192,128]{1,0:T(8,128)(2,1)S(1)} %get-tuple-element.86), channel_id=1, source_target_pairs={{64,0},{65,1},{66,2},{67,3},{68,4},{69,5},{70,6},{71,7},{72,8},{73... | collective-permute-start | bytes 147464 | tf_op jit(solution)/shard_map/ppermute | solution.py:558
  111.8 18.1 %all-to-all-start.2 = ((bf16[16,256,128]{2,1,0:T(8,128)(2,1)}), bf16[16,256,128]{2,1,0:T(8,128)(2,1)S(1)}, u32[]{:S(2)}, u32[]{:S(2)}) async-start(bf16[16,256,128]{2,1,0:T(8,128)(2,1)} %get-tuple-element.83), calls=%async_computation.2 | async-start | bytes 2097152 | tf_op jit(solution)/shard_map/all_to_all | solution.py:542
  129.9 17.0 %all-to-all-start.3 = ((bf16[16,192,128]{2,1,0:T(8,128)(2,1)}), bf16[16,192,128]{2,1,0:T(8,128)(2,1)S(1)}, u32[]{:S(2)}, u32[]{:S(2)}) async-start(bf16[16,192,128]{2,1,0:T(8,128)(2,1)} %get-tuple-element.92), calls=%async_computation.3 | async-start | bytes 1572864 | tf_op jit(solution)/shard_map/all_to_all | solution.py:542

commit v6 on v5

--- a/solution.py
+++ b/solution.py
@@ -244,8 +244,9 @@
     )(lens, k_from, v_from, q, *k, *v)
 
 
-GROUPS = ((15, 16), (14, 15), (12, 14), (8, 12), (4, 8), (0, 4))
-AHEAD = 3
+GROUPS = ((15, 16), (14, 15), (12, 14), (10, 12), (8, 10), (6, 8), (4, 6), (2, 4), (0, 2))
+AHEAD = 4
+SAVES = 4
 
 
 def chain_kernel(prompt, active, g_in, stash_in, probs_in, keys_in, values_in, g_out, stash, probs, keys, values, grads, sems, save_sems):
@@ -276,8 +277,8 @@
         return (wide + change * SCALE).astype(bf16)
 
     def save(j):
-        half = pl.ds(j * n // 2, n // 2)
-        return pltpu.make_async_copy(grads.at[half], stash.at[half], save_sems.at[j])
+        some = pl.ds(j * (n // SAVES), n // SAVES)
+        return pltpu.make_async_copy(grads.at[some], stash.at[some], save_sems.at[j])
 
     @pl.when(active[0] == 1)
     def _():
@@ -300,12 +301,12 @@
                 body(0, 0)
             else:
                 lax.fori_loop(0, high - max(low, 1), body, 0)
-            if low == n // 2:
-                save(1).start()
+            if low and low % (n // SAVES) == 0:
+                save(low // (n // SAVES)).start()
         save(0).start()
         g_out[...] = step(0)
-        save(1).wait()
-        save(0).wait()
+        for j in range(SAVES):
+            save(j).wait()
 
 
 def chain(prompt, active, g, stash, probs, k, v):
@@ -323,7 +324,7 @@
             pltpu.VMEM(v.shape, bf16),
             pltpu.VMEM((n, rows, HD), bf16),
             pltpu.SemaphoreType.DMA((len(GROUPS), 3)),
-            pltpu.SemaphoreType.DMA((2,)),
+            pltpu.SemaphoreType.DMA((SAVES,)),
         ],
         out_shape=[shape((rows, HD), bf16), shape((n, rows, HD), bf16)],
         input_output_aliases={2: 1},

time: 190 us -> 189 us (level)
  no operation moved by 1% of the time
where the time goes in v6:
time: 189 us; the launch traced here: 188 us
  Pallas kernels  63.4 us (34%)
  starting transfers between devices  47.7 us (25%)
  waiting for transfers between devices  37.4 us (20%)
  blocking collectives  33.8 us (18%)
  local copies, waits for them, and re-layouts  2.89 us (2%)
    all_to_all x2, blocking collectives, on_device(): lax.all_to_all(spread, axes, 0, 0, tiled=True)  33.8 us
    all_to_all x4, starting transfers between devices, on_device(): swap = lambda a: lax.all_to_all(a, plane, 0, 0, tiled=True)  23 us
    pallas_call x8, Pallas kernels, chain(): pl.pallas_call(functools.partial(chain_kernel, prompt), name='prompt_chai...  18 us
    pallas_call x2, Pallas kernels, prob(): pl.pallas_call(functools.partial(prob_kernel, prompt), name='prompt_prob'...  16.8 us
    ppermute x4, waiting for transfers between devices, gathered_halves(): low, high = (lax.ppermute(block, axis, ring(step)) for step in (1, -1))  16.3 us
    ppermute x6, waiting for transfers between devices, on_device(): lower = lambda a: lax.ppermute(a, 'zl', [(now, now - 1)])  13.5 us
    pallas_call x4, Pallas kernels, own_prob(): pl.pallas_call(functools.partial(own_prob_kernel, prompt), name='own_prom...  11.6 us
    ppermute x6, starting transfers between devices, gathered(): lax.ppermute(block, axis, ring(step))  9.42 us
  transfers between devices with their start and end apart: 24, of which 7 were waited for; matrix products, arithmetic and copies ran while one was open for 2% of the time, Pallas kernels for 25%

profile of v6, /device:TPU:1, one launch (start us, length us, event | category | flops | bytes accessed | tf_op | source)
XLA Modules:
  0.0 187.8 jit_solution(6288239991456972714)
XLA Ops:
  0.0 3.7 %collective-permute-start.2 = (bf16[512,128]{1,0:T(8,128)(2,1)}, bf16[512,128]{1,0:T(8,128)(2,1)S(1)}, u32[]{:S(2)}, u32[]{:S(2)}) collective-permute-start(bf16[512,128]{1,0:T(8,128)(2,1)} %bitcast.19), channel_id=1, source_target_pairs={{0,8},{4,12},{8,0},{12,4},{1,9},{5,13},{9,1},{13,5},{2,10},{6,14},... | collective-permute-start | bytes 393224 | tf_op jit(solution)/shard_map/ppermute | solution.py:516
  3.7 0.8 collective-permute-start.1
  4.5 0.7 collective-permute-start
  5.2 2.7 %collective-permute-start.5 = (bf16[512,128]{1,0:T(8,128)(2,1)}, bf16[512,128]{1,0:T(8,128)(2,1)S(1)}, u32[]{:S(2)}, u32[]{:S(2)}) collective-permute-start(bf16[512,128]{1,0:T(8,128)(2,1)} %bitcast.23), channel_id=1, source_target_pairs={{0,32},{16,48},{32,0},{48,16},{1,33},{17,49},{33,1},{49,17},{2,34}... | collective-permute-start | bytes 393224 | tf_op jit(solution)/shard_map/ppermute | solution.py:516
  8.0 0.9 collective-permute-start.4
  8.8 0.6 collective-permute-start.3
  9.4 3.8 %pack.1 = (bf16[16,256,128]{2,1,0:T(8,128)(2,1)}, bf16[16,192,128]{2,1,0:T(8,128)(2,1)}, bf16[256,128]{1,0:T(8,128)(2,1)}, bf16[192,128]{1,0:T(8,128)(2,1)}) custom-call(s32[4]{0:T(128)} %lens.17, s32[1]{0:T(128)} %bitcast.1.place, bf16[512,2048]{1,0:T(8,128)(2,1)} %bitcast.29, bf16[512,2048]{1,0:T(8,128)(2,1)} %top_ref.1), custom_call_target="tpu_custom_call" | custom-call | flops 4000000000 | tf_op jit(solution)/shard_map/pack/pallas_call | solution.py:115
  13.3 1.3 collective-permute-done.3.refs_5_
  14.6 0.9 stack_live.1
  15.6 5.0 %all-to-all-start = ((bf16[16,256,128]{2,1,0:T(8,128)(2,1)}), bf16[16,256,128]{2,1,0:T(8,128)(2,1)}, u32[]{:S(2)}, u32[]{:S(2)}) async-start(bf16[16,256,128]{2,1,0:T(8,128)(2,1)} %get-tuple-element.89.q_ref), calls=%async_computation | async-start | bytes 2097152 | tf_op jit(solution)/shard_map/all_to_all | solution.py:543
  20.6 2.5 %collective-permute-start.7 = (bf16[4,448,128]{2,1,0:T(8,128)(2,1)S(1)}, bf16[4,448,128]{2,1,0:T(8,128)(2,1)S(1)}, u32[]{:S(2)}, u32[]{:S(2)}) collective-permute-start(bf16[4,448,128]{2,1,0:T(8,128)(2,1)S(1)} %get-tuple-element.57.refs_0_), channel_id=1, source_target_pairs={{0,48},{16,0},{32,16},{48,32},{1,49},{17,1},{33,17},{49,33},{2,50}... | collective-permute-start | bytes 1376264 | tf_op jit(solution)/shard_map/ppermute | solution.py:520
  23.1 2.4 %collective-permute-start.11 = (bf16[4,448,128]{2,1,0:T(8,128)(2,1)S(1)}, bf16[4,448,128]{2,1,0:T(8,128)(2,1)S(1)}, u32[]{:S(2)}, u32[]{:S(2)}) collective-permute-start(bf16[4,448,128]{2,1,0:T(8,128)(2,1)S(1)} %get-tuple-element.58.refs_5_), channel_id=1, source_target_pairs={{0,12},{4,0},{8,4},{12,8},{1,13},{5,1},{9,5},{13,9},{2,14},{6,2},{... | collective-permute-start | bytes 1376264 | tf_op jit(solution)/shard_map/ppermute | solution.py:520
  25.5 16.3 %collective-permute-done.7.refs_2_ = bf16[4,448,128]{2,1,0:T(8,128)(2,1)S(1)} collective-permute-done((bf16[4,448,128]{2,1,0:T(8,128)(2,1)S(1)}, bf16[4,448,128]{2,1,0:T(8,128)(2,1)S(1)}, u32[]{:S(2)}, u32[]{:S(2)}) %collective-permute-start.7) | collective-permute-done | bytes 458784 | tf_op jit(solution)/shard_map/ppermute | solution.py:520
  41.8 0.7 slice.25
  42.5 2.5 %collective-permute-start.9 = (bf16[2,448,128]{2,1,0:T(8,128)(2,1)}, bf16[2,448,128]{2,1,0:T(8,128)(2,1)S(1)}, u32[]{:S(2)}, u32[]{:S(2)}) collective-permute-start(bf16[2,448,128]{2,1,0:T(8,128)(2,1)} %slice.25), channel_id=1, source_target_pairs={{0,48},{16,0},{32,16},{48,32},{1,49},{17,1},{33,17},{49,33},{2,50}... | collective-permute-start | bytes 688136 | tf_op jit(solution)/shard_map/ppermute | solution.py:527
  45.0 0.7 slice.24
  45.8 0.7 slice.27
  46.5 2.6 %collective-permute-start.13 = (bf16[2,448,128]{2,1,0:T(8,128)(2,1)}, bf16[2,448,128]{2,1,0:T(8,128)(2,1)}, u32[]{:S(2)}, u32[]{:S(2)}) collective-permute-start(bf16[2,448,128]{2,1,0:T(8,128)(2,1)} %slice.27), channel_id=1, source_target_pairs={{0,12},{4,0},{8,4},{12,8},{1,13},{5,1},{9,5},{13,9},{2,14},{6,2},{... | collective-permute-start | bytes 688136 | tf_op jit(solution)/shard_map/ppermute | solution.py:527
  49.1 0.7 slice.26
  49.8 6.5 %all-to-all-start.1 = ((bf16[16,192,128]{2,1,0:T(8,128)(2,1)}), bf16[16,192,128]{2,1,0:T(8,128)(2,1)}, u32[]{:S(2)}, u32[]{:S(2)}) async-start(bf16[16,192,128]{2,1,0:T(8,128)(2,1)} %get-tuple-element.91.q_ref), calls=%async_computation.1 | async-start | bytes 1572864 | tf_op jit(solution)/shard_map/all_to_all | solution.py:543
  56.4 7.3 %prompt_prob.1 = (f32[16,256,384]{2,1,0:T(8,128)}, bf16[16,256,128]{2,1,0:T(8,128)(2,1)}, bf16[16,256,128]{2,1,0:T(8,128)(2,1)}) custom-call(s32[4]{0:T(128)S(1)} %copy-done.2, s32[16]{0:T(128)S(1)} %get-tuple-element.95.k_from, s32[16]{0:T(128)S(1)} %get-tuple-element.96.v_from, bf16[16,256,128]{2,1,0:T(8,128)(2,1)} %all-to-all-done.q_ref.stash_in, ...), custom_call_target="tpu_custom_call" | custom-call | flops 7000000000 | tf_op jit(solution)/shard_map/prompt_prob/pallas_call | solution.py:230
  64.0 0.7 collective-permute-start.15
  64.7 2.4 %all-to-all-done.1.q_ref.stash_in = bf16[16,192,128]{2,1,0:T(8,128)(2,1)} async-done(((bf16[16,192,128]{2,1,0:T(8,128)(2,1)}), bf16[16,192,128]{2,1,0:T(8,128)(2,1)}, u32[]{:S(2)}, u32[]{:S(2)}) %all-to-all-start.1) | async-done | bytes 786464 | tf_op jit(solution)/shard_map/all_to_all | solution.py:543
  67.1 9.5 %response_prob.1 = (f32[16,192,640]{2,1,0:T(8,128)}, bf16[16,448,128]{2,1,0:T(8,128)(2,1)}, bf16[16,448,128]{2,1,0:T(8,128)(2,1)}) custom-call(s32[4]{0:T(128)S(1)} %copy-done.2, s32[16]{0:T(128)S(1)} %get-tuple-element.95.k_from, s32[16]{0:T(128)S(1)} %get-tuple-element.96.v_from, bf16[16,192,128]{2,1,0:T(8,128)(2,1)} %all-to-all-done.1.q_ref.stash_in, ...), custom_call_target="tpu_custom_call" | custom-call | flops 7000000000 | tf_op jit(solution)/shard_map/response_prob/pallas_call | solution.py:230
  76.6 0.3 response_chain.4
  76.9 0.7 collective-permute-start.14
  77.9 0.7 collective-permute-start.16
  78.6 5.0 %own_prompt_prob.2.refs_0_ = f32[16,256,256]{2,1,0:T(8,128)} custom-call(s32[1]{0:T(128)S(6)} %sub.11.active, s32[4]{0:T(128)S(1)} %copy-done.2, bf16[16,256,128]{2,1,0:T(8,128)(2,1)} %get-tuple-element.89.q_ref, bf16[448,128]{1,0:T(8,128)(2,1)S(1)} %slice_bitcast_fusion.1.k_ref), custom_call_target="tpu_custom_call" | custom-call | flops 5000000000 | tf_op jit(solution)/shard_map/own_prompt_prob/pallas_call | solution.py:379
  83.5 5.4 %own_response_prob.2.refs_0_ = f32[4,448,768]{2,1,0:T(8,128)} custom-call(s32[1]{0:T(128)S(6)} %sub.11.active, s32[4]{0:T(128)S(1)} %copy-done.2, bf16[16,192,128]{2,1,0:T(8,128)(2,1)} %get-tuple-element.91.q_ref, bf16[448,128]{1,0:T(8,128)(2,1)S(1)} %slice_bitcast_fusion.1.k_ref), custom_call_target="tpu_custom_call" | custom-call | flops 5000000000 | tf_op jit(solution)/shard_map/own_response_prob/pallas_call | solution.py:379
  89.0 0.5 response_chain.5
  89.8 1.3 collective-permute-start.18
  91.1 0.7 collective-permute-start.17
  91.8 10.2 %collective-permute-done.18.g_in = bf16[256,128]{1,0:T(8,128)(2,1)S(1)} collective-permute-done((bf16[256,128]{1,0:T(8,128)(2,1)S(1)}, bf16[256,128]{1,0:T(8,128)(2,1)S(1)}, u32[]{:S(2)}, u32[]{:S(2)}) %collective-permute-start.18) | collective-permute-done | bytes 65568 | tf_op jit(solution)/shard_map/ppermute | solution.py:559
  102.0 7.8 %prompt_chain.7 = (bf16[256,128]{1,0:T(8,128)(2,1)}, bf16[16,256,128]{2,1,0:T(8,128)(2,1)}) custom-call(s32[1]{0:T(128)} %bitcast.5.active, bf16[256,128]{1,0:T(8,128)(2,1)S(1)} %collective-permute-done.18.g_in, bf16[16,256,128]{2,1,0:T(8,128)(2,1)} %get-tuple-element.82.stash_in, ...), custom_call_target="tpu_custom_call", output_to_operand_aliasing={{1}: (2, {})} | custom-call | flops 7000000000 | tf_op jit(solution)/shard_map/prompt_chain/pallas_call | solution.py:315
  110.2 1.3 collective-permute-start.19
  111.5 4.8 %all-to-all-start.2 = ((bf16[16,256,128]{2,1,0:T(8,128)(2,1)}), bf16[16,256,128]{2,1,0:T(8,128)(2,1)S(1)}, u32[]{:S(2)}, u32[]{:S(2)}) async-start(bf16[16,256,128]{2,1,0:T(8,128)(2,1)} %get-tuple-element.83), calls=%async_computation.2 | async-start | bytes 2097152 | tf_op jit(solution)/shard_map/all_to_all | solution.py:543
  116.3 3.2 %collective-permute-done.19.g_in = bf16[192,128]{1,0:T(8,128)(2,1)S(1)} collective-permute-done((bf16[192,128]{1,0:T(8,128)(2,1)S(1)}, bf16[192,128]{1,0:T(8,128)(2,1)S(1)}, u32[]{:S(2)}, u32[]{:S(2)}) %collective-permute-start.19) | collective-permute-done | bytes 49184 | tf_op jit(solution)/shard_map/ppermute | solution.py:559
  119.5 8.2 %response_chain.7 = (bf16[192,128]{1,0:T(8,128)(2,1)}, bf16[16,192,128]{2,1,0:T(8,128)(2,1)}) custom-call(s32[1]{0:T(128)} %bitcast.5.active, bf16[192,128]{1,0:T(8,128)(2,1)S(1)} %collective-permute-done.19.g_in, bf16[16,192,128]{2,1,0:T(8,128)(2,1)} %get-tuple-element.87.stash_in, ...), custom_call_target="tpu_custom_call", output_to_operand_aliasing={{1}: (2, {})} | custom-call | flops 7000000000 | tf_op jit(solution)/shard_map/response_chain/pallas_call | solution.py:315
  127.7 0.6 own_prompt_prob.3.probs
  128.3 6.6 %all-to-all-start.3 = ((bf16[16,192,128]{2,1,0:T(8,128)(2,1)}), bf16[16,192,128]{2,1,0:T(8,128)(2,1)S(1)}, u32[]{:S(2)}, u32[]{:S(2)}) async-start(bf16[16,192,128]{2,1,0:T(8,128)(2,1)} %get-tuple-element.92), calls=%async_computation.3 | async-start | bytes 1572864 | tf_op jit(solution)/shard_map/all_to_all | solution.py:543
  135.0 6.0 %prompt_grad.1.part_ref = f32[256,256]{1,0:T(8,128)S(1)} custom-call(f32[16,256,256]{2,1,0:T(8,128)} %own_prompt_prob.3.probs, bf16[16,256,128]{2,1,0:T(8,128)(2,1)} %get-tuple-element.89.q_ref, bf16[16,256,128]{2,1,0:T(8,128)(2,1)S(1)} %all-to-all-done.2.g_ref, bf16[448,128]{1,0:T(8,128)(2,1)S(1)} %slice_bitcast_fusion.v_ref), custom_call_target="tpu_custom_call" | custom-call | flops 5000000000 | tf_op jit(solution)/shard_map/prompt_grad/pallas_call | solution.py:427
  141.0 0.6 own_response_prob.3.probs
  141.6 3.8 %all-to-all-done.3.g_ref = bf16[16,192,128]{2,1,0:T(8,128)(2,1)S(1)} async-done(((bf16[16,192,128]{2,1,0:T(8,128)(2,1)}), bf16[16,192,128]{2,1,0:T(8,128)(2,1)S(1)}, u32[]{:S(2)}, u32[]{:S(2)}) %all-to-all-start.3) | async-done | bytes 786464 | tf_op jit(solution)/shard_map/all_to_all | solution.py:543
  145.3 6.5 %response_grad.1 = (f32[512,256]{1,0:T(8,128)S(1)}, f32[1,128]{1,0:T(1,128)S(1)}) custom-call(s32[4]{0:T(128)S(1)} %copy-done.2, f32[4,448,768]{2,1,0:T(8,128)} %own_response_prob.3.probs, bf16[16,192,128]{2,1,0:T(8,128)(2,1)} %get-tuple-element.91.q_ref, bf16[16,192,128]{2,1,0:T(8,128)(2,1)S(1)} %all-to-all-done.3.g_ref, ...), custom_call_target="tpu_custom_call" | custom-call | flops 8000000000 | tf_op jit(solution)/shard_map/response_grad/pallas_call | solution.py:489
  151.8 17.8 %all_to_all.32 = f32[32,1,128]{2,1,0:T(1,128)S(1)} all-to-all(f32[32,1,128]{2,1,0:T(1,128)S(1)} %broadcast_in_dim.26), channel_id=1, replica_groups=mesh['zl'=4,'x'=4,'y'=4,'zh'=2,'core'=2] {'x','y','core'}, dimensions={0} | all-to-all | bytes 32768 | tf_op jit(solution)/shard_map/all_to_all | solution.py:587
  169.6 16.0 %all_to_all.33 = f32[8,1,128]{2,1,0:T(1,128)S(1)} all-to-all(f32[8,1,128]{2,1,0:T(1,128)S(1)} %broadcast_in_dim.27), channel_id=1, replica_groups=mesh['zl'=4,'x'=4,'y'=4,'zh'=2,'core'=2] {'zl','zh'}, dimensions={0} | all-to-all | bytes 8192 | tf_op jit(solution)/shard_map/all_to_all | solution.py:587
  185.6 0.6 reduce_sum.20
  187.0 0.8 multiply_bitcast_fusion
  (42 shorter events, 1.4 us)
Async XLA Ops:
  0.0 8.8 %collective-permute-start.2 = (bf16[512,128]{1,0:T(8,128)(2,1)}, bf16[512,128]{1,0:T(8,128)(2,1)S(1)}, u32[]{:S(2)}, u32[]{:S(2)}) collective-permute-start(bf16[512,128]{1,0:T(8,128)(2,1)} %bitcast.19), channel_id=1, source_target_pairs={{0,8},{4,12},{8,0},{12,4},{1,9},{5,13},{9,1},{13,5},{2,10},{6,14},... | collective-permute-start | bytes 393224 | tf_op jit(solution)/shard_map/ppermute | solution.py:516
  3.7 9.5 %collective-permute-start.1 = (bf16[512,128]{1,0:T(8,128)(2,1)}, bf16[512,128]{1,0:T(8,128)(2,1)S(1)}, u32[]{:S(2)}, u32[]{:S(2)}) collective-permute-start(bf16[512,128]{1,0:T(8,128)(2,1)} %bitcast.20), channel_id=1, source_target_pairs={{0,12},{4,0},{8,4},{12,8},{1,13},{5,1},{9,5},{13,9},{2,14},{6,2},{... | collective-permute-start | bytes 393224 | tf_op jit(solution)/shard_map/ppermute | solution.py:516
  4.5 8.7 %collective-permute-start = (bf16[512,128]{1,0:T(8,128)(2,1)}, bf16[512,128]{1,0:T(8,128)(2,1)S(1)}, u32[]{:S(2)}, u32[]{:S(2)}) collective-permute-start(bf16[512,128]{1,0:T(8,128)(2,1)} %bitcast.21), channel_id=1, source_target_pairs={{0,4},{4,8},{8,12},{12,0},{1,5},{5,9},{9,13},{13,1},{2,6},{6,10},{... | collective-permute-start | bytes 393224 | tf_op jit(solution)/shard_map/ppermute | solution.py:516
  5.2 8.0 %collective-permute-start.5 = (bf16[512,128]{1,0:T(8,128)(2,1)}, bf16[512,128]{1,0:T(8,128)(2,1)S(1)}, u32[]{:S(2)}, u32[]{:S(2)}) collective-permute-start(bf16[512,128]{1,0:T(8,128)(2,1)} %bitcast.23), channel_id=1, source_target_pairs={{0,32},{16,48},{32,0},{48,16},{1,33},{17,49},{33,1},{49,17},{2,34}... | collective-permute-start | bytes 393224 | tf_op jit(solution)/shard_map/ppermute | solution.py:516
  8.0 5.3 %collective-permute-start.4 = (bf16[512,128]{1,0:T(8,128)(2,1)}, bf16[512,128]{1,0:T(8,128)(2,1)S(1)}, u32[]{:S(2)}, u32[]{:S(2)}) collective-permute-start(bf16[512,128]{1,0:T(8,128)(2,1)} %bitcast.24), channel_id=1, source_target_pairs={{0,48},{16,0},{32,16},{48,32},{1,49},{17,1},{33,17},{49,33},{2,50}... | collective-permute-start | bytes 393224 | tf_op jit(solution)/shard_map/ppermute | solution.py:516
  8.8 5.8 %collective-permute-start.3 = (bf16[512,128]{1,0:T(8,128)(2,1)}, bf16[512,128]{1,0:T(8,128)(2,1)S(1)}, u32[]{:S(2)}, u32[]{:S(2)}) collective-permute-start(bf16[512,128]{1,0:T(8,128)(2,1)} %bitcast.25), channel_id=1, source_target_pairs={{0,16},{16,32},{32,48},{48,0},{1,17},{17,33},{33,49},{49,1},{2,18}... | collective-permute-start | bytes 393224 | tf_op jit(solution)/shard_map/ppermute | solution.py:516
  9.4 5.2 %copy-start = (bf16[1,512,128]{2,1,0:T(8,128)(2,1)S(1)}, bf16[1,512,128]{2,1,0:T(8,128)(2,1)}, u32[]{:S(2)}) copy-start(bf16[1,512,128]{2,1,0:T(8,128)(2,1)} %param.6) | copy-start | bytes 393220
  9.4 5.2 %copy-start.1 = (bf16[1,512,128]{2,1,0:T(8,128)(2,1)S(1)}, bf16[1,512,128]{2,1,0:T(8,128)(2,1)}, u32[]{:S(2)}) copy-start(bf16[1,512,128]{2,1,0:T(8,128)(2,1)} %param.7) | copy-start | bytes 393220
  9.4 5.2 %copy-start.2 = (s32[4]{0:T(128)S(1)}, s32[4]{0:T(128)}, u32[]{:S(2)}) copy-start(s32[4]{0:T(128)} %lens.17) | copy-start | bytes 52
  15.6 34.3 %all-to-all-start = ((bf16[16,256,128]{2,1,0:T(8,128)(2,1)}), bf16[16,256,128]{2,1,0:T(8,128)(2,1)}, u32[]{:S(2)}, u32[]{:S(2)}) async-start(bf16[16,256,128]{2,1,0:T(8,128)(2,1)} %get-tuple-element.89.q_ref), calls=%async_computation | async-start | bytes 2097152 | tf_op jit(solution)/shard_map/all_to_all | solution.py:543
  20.6 21.2 %collective-permute-start.7 = (bf16[4,448,128]{2,1,0:T(8,128)(2,1)S(1)}, bf16[4,448,128]{2,1,0:T(8,128)(2,1)S(1)}, u32[]{:S(2)}, u32[]{:S(2)}) collective-permute-start(bf16[4,448,128]{2,1,0:T(8,128)(2,1)S(1)} %get-tuple-element.57.refs_0_), channel_id=1, source_target_pairs={{0,48},{16,0},{32,16},{48,32},{1,49},{17,1},{33,17},{49,33},{2,50}... | collective-permute-start | bytes 1376264 | tf_op jit(solution)/shard_map/ppermute | solution.py:520
  23.1 21.9 %collective-permute-start.6 = (bf16[4,448,128]{2,1,0:T(8,128)(2,1)S(1)}, bf16[4,448,128]{2,1,0:T(8,128)(2,1)S(1)}, u32[]{:S(2)}, u32[]{:S(2)}) collective-permute-start(bf16[4,448,128]{2,1,0:T(8,128)(2,1)S(1)} %get-tuple-element.57.refs_0_), channel_id=1, source_target_pairs={{0,16},{16,32},{32,48},{48,0},{1,17},{17,33},{33,49},{49,1},{2,18}... | collective-permute-start | bytes 1376264 | tf_op jit(solution)/shard_map/ppermute | solution.py:520
  23.1 22.6 %collective-permute-start.11 = (bf16[4,448,128]{2,1,0:T(8,128)(2,1)S(1)}, bf16[4,448,128]{2,1,0:T(8,128)(2,1)S(1)}, u32[]{:S(2)}, u32[]{:S(2)}) collective-permute-start(bf16[4,448,128]{2,1,0:T(8,128)(2,1)S(1)} %get-tuple-element.58.refs_5_), channel_id=1, source_target_pairs={{0,12},{4,0},{8,4},{12,8},{1,13},{5,1},{9,5},{13,9},{2,14},{6,2},{... | collective-permute-start | bytes 1376264 | tf_op jit(solution)/shard_map/ppermute | solution.py:520
  25.5 23.6 %collective-permute-start.10 = (bf16[4,448,128]{2,1,0:T(8,128)(2,1)S(1)}, bf16[4,448,128]{2,1,0:T(8,128)(2,1)S(1)}, u32[]{:S(2)}, u32[]{:S(2)}) collective-permute-start(bf16[4,448,128]{2,1,0:T(8,128)(2,1)S(1)} %get-tuple-element.58.refs_5_), channel_id=1, source_target_pairs={{0,4},{4,8},{8,12},{12,0},{1,5},{5,9},{9,13},{13,1},{2,6},{6,10},{... | collective-permute-start | bytes 1376264 | tf_op jit(solution)/shard_map/ppermute | solution.py:520
  42.5 13.9 %collective-permute-start.9 = (bf16[2,448,128]{2,1,0:T(8,128)(2,1)}, bf16[2,448,128]{2,1,0:T(8,128)(2,1)S(1)}, u32[]{:S(2)}, u32[]{:S(2)}) collective-permute-start(bf16[2,448,128]{2,1,0:T(8,128)(2,1)} %slice.25), channel_id=1, source_target_pairs={{0,48},{16,0},{32,16},{48,32},{1,49},{17,1},{33,17},{49,33},{2,50}... | collective-permute-start | bytes 688136 | tf_op jit(solution)/shard_map/ppermute | solution.py:527
  45.7 10.6 %collective-permute-start.8 = (bf16[2,448,128]{2,1,0:T(8,128)(2,1)}, bf16[2,448,128]{2,1,0:T(8,128)(2,1)S(1)}, u32[]{:S(2)}, u32[]{:S(2)}) collective-permute-start(bf16[2,448,128]{2,1,0:T(8,128)(2,1)} %slice.24), channel_id=1, source_target_pairs={{0,16},{16,32},{32,48},{48,0},{1,17},{17,33},{33,49},{49,1},{2,18}... | collective-permute-start | bytes 688136 | tf_op jit(solution)/shard_map/ppermute | solution.py:526
  46.5 9.9 %collective-permute-start.13 = (bf16[2,448,128]{2,1,0:T(8,128)(2,1)}, bf16[2,448,128]{2,1,0:T(8,128)(2,1)}, u32[]{:S(2)}, u32[]{:S(2)}) collective-permute-start(bf16[2,448,128]{2,1,0:T(8,128)(2,1)} %slice.27), channel_id=1, source_target_pairs={{0,12},{4,0},{8,4},{12,8},{1,13},{5,1},{9,5},{13,9},{2,14},{6,2},{... | collective-permute-start | bytes 688136 | tf_op jit(solution)/shard_map/ppermute | solution.py:527
  49.8 6.6 %collective-permute-start.12 = (bf16[2,448,128]{2,1,0:T(8,128)(2,1)}, bf16[2,448,128]{2,1,0:T(8,128)(2,1)}, u32[]{:S(2)}, u32[]{:S(2)}) collective-permute-start(bf16[2,448,128]{2,1,0:T(8,128)(2,1)} %slice.26), channel_id=1, source_target_pairs={{0,4},{4,8},{8,12},{12,0},{1,5},{5,9},{9,13},{13,1},{2,6},{6,10},{... | collective-permute-start | bytes 688136 | tf_op jit(solution)/shard_map/ppermute | solution.py:526
  49.8 17.3 %all-to-all-start.1 = ((bf16[16,192,128]{2,1,0:T(8,128)(2,1)}), bf16[16,192,128]{2,1,0:T(8,128)(2,1)}, u32[]{:S(2)}, u32[]{:S(2)}) async-start(bf16[16,192,128]{2,1,0:T(8,128)(2,1)} %get-tuple-element.91.q_ref), calls=%async_computation.1 | async-start | bytes 1572864 | tf_op jit(solution)/shard_map/all_to_all | solution.py:543
  56.4 7.3 %copy-start.3 = (bf16[256,128]{1,0:T(8,128)(2,1)S(1)}, bf16[256,128]{1,0:T(8,128)(2,1)}, u32[]{:S(2)}) copy-start(bf16[256,128]{1,0:T(8,128)(2,1)} %get-tuple-element.56.g_in) | copy-start | bytes 196612
  64.0 13.6 %collective-permute-start.15 = (bf16[256,128]{1,0:T(8,128)(2,1)S(1)}, bf16[256,128]{1,0:T(8,128)(2,1)S(1)}, u32[]{:S(2)}, u32[]{:S(2)}) collective-permute-start(bf16[256,128]{1,0:T(8,128)(2,1)S(1)} %get-tuple-element.62), channel_id=1, source_target_pairs={{192,128},{193,129},{194,130},{195,131},{196,132},{197,133},{198,1... | collective-permute-start | bytes 196616 | tf_op jit(solution)/shard_map/ppermute | solution.py:559
  67.1 9.5 %copy-start.4 = (bf16[192,128]{1,0:T(8,128)(2,1)S(1)}, bf16[192,128]{1,0:T(8,128)(2,1)}, u32[]{:S(2)}) copy-start(bf16[192,128]{1,0:T(8,128)(2,1)} %get-tuple-element.63.g_in) | copy-start | bytes 147460
  76.9 12.1 %collective-permute-start.14 = (bf16[192,128]{1,0:T(8,128)(2,1)S(1)}, bf16[192,128]{1,0:T(8,128)(2,1)S(1)}, u32[]{:S(2)}, u32[]{:S(2)}) collective-permute-start(bf16[192,128]{1,0:T(8,128)(2,1)S(1)} %get-tuple-element.68), channel_id=1, source_target_pairs={{192,128},{193,129},{194,130},{195,131},{196,132},{197,133},{198,1... | collective-permute-start | bytes 147464 | tf_op jit(solution)/shard_map/ppermute | solution.py:559
  77.9 11.1 %collective-permute-start.16 = (bf16[256,128]{1,0:T(8,128)(2,1)S(1)}, bf16[256,128]{1,0:T(8,128)(2,1)S(1)}, u32[]{:S(2)}, u32[]{:S(2)}) collective-permute-start(bf16[256,128]{1,0:T(8,128)(2,1)S(1)} %get-tuple-element.71), channel_id=1, source_target_pairs={{128,64},{129,65},{130,66},{131,67},{132,68},{133,69},{134,70},{13... | collective-permute-start | bytes 196616 | tf_op jit(solution)/shard_map/ppermute | solution.py:559
  89.8 12.2 %collective-permute-start.18 = (bf16[256,128]{1,0:T(8,128)(2,1)S(1)}, bf16[256,128]{1,0:T(8,128)(2,1)S(1)}, u32[]{:S(2)}, u32[]{:S(2)}) collective-permute-start(bf16[256,128]{1,0:T(8,128)(2,1)S(1)} %get-tuple-element.80), channel_id=1, source_target_pairs={{64,0},{65,1},{66,2},{67,3},{68,4},{69,5},{70,6},{71,7},{72,8},{73... | collective-permute-start | bytes 196616 | tf_op jit(solution)/shard_map/ppermute | solution.py:559
  91.1 0.7 collective-permute-start.17
  110.2 9.4 %collective-permute-start.19 = (bf16[192,128]{1,0:T(8,128)(2,1)S(1)}, bf16[192,128]{1,0:T(8,128)(2,1)S(1)}, u32[]{:S(2)}, u32[]{:S(2)}) collective-permute-start(bf16[192,128]{1,0:T(8,128)(2,1)S(1)} %get-tuple-element.86), channel_id=1, source_target_pairs={{64,0},{65,1},{66,2},{67,3},{68,4},{69,5},{70,6},{71,7},{72,8},{73... | collective-permute-start | bytes 147464 | tf_op jit(solution)/shard_map/ppermute | solution.py:559
  111.5 16.9 %all-to-all-start.2 = ((bf16[16,256,128]{2,1,0:T(8,128)(2,1)}), bf16[16,256,128]{2,1,0:T(8,128)(2,1)S(1)}, u32[]{:S(2)}, u32[]{:S(2)}) async-start(bf16[16,256,128]{2,1,0:T(8,128)(2,1)} %get-tuple-element.83), calls=%async_computation.2 | async-start | bytes 2097152 | tf_op jit(solution)/shard_map/all_to_all | solution.py:543
  128.3 17.0 %all-to-all-start.3 = ((bf16[16,192,128]{2,1,0:T(8,128)(2,1)}), bf16[16,192,128]{2,1,0:T(8,128)(2,1)S(1)}, u32[]{:S(2)}, u32[]{:S(2)}) async-start(bf16[16,192,128]{2,1,0:T(8,128)(2,1)} %get-tuple-element.92), calls=%async_computation.3 | async-start | bytes 1572864 | tf_op jit(solution)/shard_map/all_to_all | solution.py:543

commit v7 on v6

--- a/solution.py
+++ b/solution.py
@@ -171,6 +171,7 @@
 
 
 AT_ONCE = 4
+SENT = 2
 PROMPT_ROW = PROMPT + HD
 RESP_ROW = 2 * PROMPT + HD
 def in_hbm(x):
@@ -197,7 +198,7 @@
         copy.start()
 
     def done(i):
-        some = pl.ds(i * AT_ONCE, AT_ONCE)
+        some = pl.ds(i * SENT, SENT)
         return pltpu.make_async_copy(probs.at[some], probs_out.at[some], sems.at[i])
 
     def body(i, carry):
@@ -215,11 +216,12 @@
                 probs[layer, :, 2 * PROMPT :] = dot(p1.astype(bf16), v[:PROMPT]) + dot(
                     p2.astype(bf16), v[PROMPT:]
                 )
-        done(i).start()
+            if u % SENT == SENT - 1:
+                done(i * (AT_ONCE // SENT) + u // SENT).start()
         return carry
 
     lax.fori_loop(0, n // AT_ONCE, body, 0)
-    for copy in ordered + [done(i) for i in range(n // AT_ONCE)]:
+    for copy in ordered + [done(i) for i in range(n // SENT)]:
         copy.wait()
 
 
@@ -236,7 +238,7 @@
         scratch_shapes=[pltpu.VMEM(*r) for r in results]
         + [
             pltpu.VMEM((rows, rows), f32),
-            pltpu.SemaphoreType.DMA((n // AT_ONCE,)),
+            pltpu.SemaphoreType.DMA((n // SENT,)),
             pltpu.SemaphoreType.DMA((2,)),
         ],
         out_shape=[pltpu.HBM(*r) for r in results],

time: 189 us -> 188 us (level)
  no operation moved by 1% of the time
where the time goes in v7:
time: 188 us; the launch traced here: 187 us
  Pallas kernels  63 us (34%)
  starting transfers between devices  47.6 us (25%)
  waiting for transfers between devices  37.5 us (20%)
  blocking collectives  33.8 us (18%)
  local copies, waits for them, and re-layouts  2.89 us (2%)
    all_to_all x2, blocking collectives, on_device(): lax.all_to_all(spread, axes, 0, 0, tiled=True)  33.8 us
    all_to_all x4, starting transfers between devices, on_device(): swap = lambda a: lax.all_to_all(a, plane, 0, 0, tiled=True)  22.8 us
    pallas_call x8, Pallas kernels, chain(): pl.pallas_call(functools.partial(chain_kernel, prompt), name='prompt_chai...  18 us
    pallas_call x2, Pallas kernels, prob(): pl.pallas_call(functools.partial(prob_kernel, prompt), name='prompt_prob'...  16.3 us
    ppermute x4, waiting for transfers between devices, gathered_halves(): low, high = (lax.ppermute(block, axis, ring(step)) for step in (1, -1))  16.3 us
    ppermute x6, waiting for transfers between devices, on_device(): lower = lambda a: lax.ppermute(a, 'zl', [(now, now - 1)])  13.5 us
    pallas_call x4, Pallas kernels, own_prob(): pl.pallas_call(functools.partial(own_prob_kernel, prompt), name='own_prom...  11.6 us
    ppermute x6, starting transfers between devices, gathered(): lax.ppermute(block, axis, ring(step))  9.42 us
  transfers between devices with their start and end apart: 24, of which 7 were waited for; matrix products, arithmetic and copies ran while one was open for 2% of the time, Pallas kernels for 25%

profile of v7, /device:TPU:1, one launch (start us, length us, event | category | flops | bytes accessed | tf_op | source)
XLA Modules:
  0.0 187.4 jit_solution(14285961712095892156)
XLA Ops:
  0.0 3.7 %collective-permute-start.2 = (bf16[512,128]{1,0:T(8,128)(2,1)}, bf16[512,128]{1,0:T(8,128)(2,1)S(1)}, u32[]{:S(2)}, u32[]{:S(2)}) collective-permute-start(bf16[512,128]{1,0:T(8,128)(2,1)} %bitcast.19), channel_id=1, source_target_pairs={{0,8},{4,12},{8,0},{12,4},{1,9},{5,13},{9,1},{13,5},{2,10},{6,14},... | collective-permute-start | bytes 393224 | tf_op jit(solution)/shard_map/ppermute | solution.py:518
  3.7 0.8 collective-permute-start.1
  4.5 0.7 collective-permute-start
  5.2 2.7 %collective-permute-start.5 = (bf16[512,128]{1,0:T(8,128)(2,1)}, bf16[512,128]{1,0:T(8,128)(2,1)S(1)}, u32[]{:S(2)}, u32[]{:S(2)}) collective-permute-start(bf16[512,128]{1,0:T(8,128)(2,1)} %bitcast.23), channel_id=1, source_target_pairs={{0,32},{16,48},{32,0},{48,16},{1,33},{17,49},{33,1},{49,17},{2,34}... | collective-permute-start | bytes 393224 | tf_op jit(solution)/shard_map/ppermute | solution.py:518
  8.0 0.9 collective-permute-start.4
  8.8 0.6 collective-permute-start.3
  9.4 3.8 %pack.1 = (bf16[16,256,128]{2,1,0:T(8,128)(2,1)}, bf16[16,192,128]{2,1,0:T(8,128)(2,1)}, bf16[256,128]{1,0:T(8,128)(2,1)}, bf16[192,128]{1,0:T(8,128)(2,1)}) custom-call(s32[4]{0:T(128)} %lens.17, s32[1]{0:T(128)} %bitcast.1.place, bf16[512,2048]{1,0:T(8,128)(2,1)} %bitcast.29, bf16[512,2048]{1,0:T(8,128)(2,1)} %top_ref.1), custom_call_target="tpu_custom_call" | custom-call | flops 4000000000 | tf_op jit(solution)/shard_map/pack/pallas_call | solution.py:115
  13.3 1.3 collective-permute-done.3.refs_5_
  14.6 0.9 stack_live.1
  15.6 5.0 %all-to-all-start = ((bf16[16,256,128]{2,1,0:T(8,128)(2,1)}), bf16[16,256,128]{2,1,0:T(8,128)(2,1)}, u32[]{:S(2)}, u32[]{:S(2)}) async-start(bf16[16,256,128]{2,1,0:T(8,128)(2,1)} %get-tuple-element.89.q_ref), calls=%async_computation | async-start | bytes 2097152 | tf_op jit(solution)/shard_map/all_to_all | solution.py:545
  20.6 2.5 %collective-permute-start.7 = (bf16[4,448,128]{2,1,0:T(8,128)(2,1)S(1)}, bf16[4,448,128]{2,1,0:T(8,128)(2,1)S(1)}, u32[]{:S(2)}, u32[]{:S(2)}) collective-permute-start(bf16[4,448,128]{2,1,0:T(8,128)(2,1)S(1)} %get-tuple-element.57.refs_0_), channel_id=1, source_target_pairs={{0,48},{16,0},{32,16},{48,32},{1,49},{17,1},{33,17},{49,33},{2,50}... | collective-permute-start | bytes 1376264 | tf_op jit(solution)/shard_map/ppermute | solution.py:522
  23.1 2.4 %collective-permute-start.11 = (bf16[4,448,128]{2,1,0:T(8,128)(2,1)S(1)}, bf16[4,448,128]{2,1,0:T(8,128)(2,1)S(1)}, u32[]{:S(2)}, u32[]{:S(2)}) collective-permute-start(bf16[4,448,128]{2,1,0:T(8,128)(2,1)S(1)} %get-tuple-element.58.refs_5_), channel_id=1, source_target_pairs={{0,12},{4,0},{8,4},{12,8},{1,13},{5,1},{9,5},{13,9},{2,14},{6,2},{... | collective-permute-start | bytes 1376264 | tf_op jit(solution)/shard_map/ppermute | solution.py:522
  25.5 16.3 %collective-permute-done.7.refs_2_ = bf16[4,448,128]{2,1,0:T(8,128)(2,1)S(1)} collective-permute-done((bf16[4,448,128]{2,1,0:T(8,128)(2,1)S(1)}, bf16[4,448,128]{2,1,0:T(8,128)(2,1)S(1)}, u32[]{:S(2)}, u32[]{:S(2)}) %collective-permute-start.7) | collective-permute-done | bytes 458784 | tf_op jit(solution)/shard_map/ppermute | solution.py:522
  41.8 0.7 slice.25
  42.5 2.5 %collective-permute-start.9 = (bf16[2,448,128]{2,1,0:T(8,128)(2,1)}, bf16[2,448,128]{2,1,0:T(8,128)(2,1)S(1)}, u32[]{:S(2)}, u32[]{:S(2)}) collective-permute-start(bf16[2,448,128]{2,1,0:T(8,128)(2,1)} %slice.25), channel_id=1, source_target_pairs={{0,48},{16,0},{32,16},{48,32},{1,49},{17,1},{33,17},{49,33},{2,50}... | collective-permute-start | bytes 688136 | tf_op jit(solution)/shard_map/ppermute | solution.py:529
  45.0 0.7 slice.24
  45.8 0.7 slice.27
  46.5 2.6 %collective-permute-start.13 = (bf16[2,448,128]{2,1,0:T(8,128)(2,1)}, bf16[2,448,128]{2,1,0:T(8,128)(2,1)}, u32[]{:S(2)}, u32[]{:S(2)}) collective-permute-start(bf16[2,448,128]{2,1,0:T(8,128)(2,1)} %slice.27), channel_id=1, source_target_pairs={{0,12},{4,0},{8,4},{12,8},{1,13},{5,1},{9,5},{13,9},{2,14},{6,2},{... | collective-permute-start | bytes 688136 | tf_op jit(solution)/shard_map/ppermute | solution.py:529
  49.1 0.7 slice.26
  49.8 6.5 %all-to-all-start.1 = ((bf16[16,192,128]{2,1,0:T(8,128)(2,1)}), bf16[16,192,128]{2,1,0:T(8,128)(2,1)}, u32[]{:S(2)}, u32[]{:S(2)}) async-start(bf16[16,192,128]{2,1,0:T(8,128)(2,1)} %get-tuple-element.91.q_ref), calls=%async_computation.1 | async-start | bytes 1572864 | tf_op jit(solution)/shard_map/all_to_all | solution.py:545
  56.4 7.1 %prompt_prob.1 = (f32[16,256,384]{2,1,0:T(8,128)}, bf16[16,256,128]{2,1,0:T(8,128)(2,1)}, bf16[16,256,128]{2,1,0:T(8,128)(2,1)}) custom-call(s32[4]{0:T(128)S(1)} %copy-done.2, s32[16]{0:T(128)S(1)} %get-tuple-element.95.k_from, s32[16]{0:T(128)S(1)} %get-tuple-element.96.v_from, bf16[16,256,128]{2,1,0:T(8,128)(2,1)} %all-to-all-done.q_ref.stash_in, ...), custom_call_target="tpu_custom_call" | custom-call | flops 7000000000 | tf_op jit(solution)/shard_map/prompt_prob/pallas_call | solution.py:232
  63.5 0.3 prompt_chain.4
  63.8 0.7 collective-permute-start.15
  64.5 2.6 %all-to-all-done.1.q_ref.stash_in = bf16[16,192,128]{2,1,0:T(8,128)(2,1)} async-done(((bf16[16,192,128]{2,1,0:T(8,128)(2,1)}), bf16[16,192,128]{2,1,0:T(8,128)(2,1)}, u32[]{:S(2)}, u32[]{:S(2)}) %all-to-all-start.1) | async-done | bytes 786464 | tf_op jit(solution)/shard_map/all_to_all | solution.py:545
  67.1 9.2 %response_prob.1 = (f32[16,192,640]{2,1,0:T(8,128)}, bf16[16,448,128]{2,1,0:T(8,128)(2,1)}, bf16[16,448,128]{2,1,0:T(8,128)(2,1)}) custom-call(s32[4]{0:T(128)S(1)} %copy-done.2, s32[16]{0:T(128)S(1)} %get-tuple-element.95.k_from, s32[16]{0:T(128)S(1)} %get-tuple-element.96.v_from, bf16[16,192,128]{2,1,0:T(8,128)(2,1)} %all-to-all-done.1.q_ref.stash_in, ...), custom_call_target="tpu_custom_call" | custom-call | flops 7000000000 | tf_op jit(solution)/shard_map/response_prob/pallas_call | solution.py:232
  76.6 0.7 collective-permute-start.14
  77.6 0.7 collective-permute-start.16
  78.3 5.0 %own_prompt_prob.2.refs_0_ = f32[16,256,256]{2,1,0:T(8,128)} custom-call(s32[1]{0:T(128)S(6)} %sub.11.active, s32[4]{0:T(128)S(1)} %copy-done.2, bf16[16,256,128]{2,1,0:T(8,128)(2,1)} %get-tuple-element.89.q_ref, bf16[448,128]{1,0:T(8,128)(2,1)S(1)} %slice_bitcast_fusion.1.k_ref), custom_call_target="tpu_custom_call" | custom-call | flops 5000000000 | tf_op jit(solution)/shard_map/own_prompt_prob/pallas_call | solution.py:381
  83.3 5.4 %own_response_prob.2.refs_0_ = f32[4,448,768]{2,1,0:T(8,128)} custom-call(s32[1]{0:T(128)S(6)} %sub.11.active, s32[4]{0:T(128)S(1)} %copy-done.2, bf16[16,192,128]{2,1,0:T(8,128)(2,1)} %get-tuple-element.91.q_ref, bf16[448,128]{1,0:T(8,128)(2,1)S(1)} %slice_bitcast_fusion.1.k_ref), custom_call_target="tpu_custom_call" | custom-call | flops 5000000000 | tf_op jit(solution)/shard_map/own_response_prob/pallas_call | solution.py:381
  88.7 0.5 response_chain.5
  89.5 1.3 collective-permute-start.18
  90.8 0.7 collective-permute-start.17
  91.5 10.2 %collective-permute-done.18.g_in = bf16[256,128]{1,0:T(8,128)(2,1)S(1)} collective-permute-done((bf16[256,128]{1,0:T(8,128)(2,1)S(1)}, bf16[256,128]{1,0:T(8,128)(2,1)S(1)}, u32[]{:S(2)}, u32[]{:S(2)}) %collective-permute-start.18) | collective-permute-done | bytes 65568 | tf_op jit(solution)/shard_map/ppermute | solution.py:561
  101.8 7.8 %prompt_chain.7 = (bf16[256,128]{1,0:T(8,128)(2,1)}, bf16[16,256,128]{2,1,0:T(8,128)(2,1)}) custom-call(s32[1]{0:T(128)} %bitcast.5.active, bf16[256,128]{1,0:T(8,128)(2,1)S(1)} %collective-permute-done.18.g_in, bf16[16,256,128]{2,1,0:T(8,128)(2,1)} %get-tuple-element.82.stash_in, ...), custom_call_target="tpu_custom_call", output_to_operand_aliasing={{1}: (2, {})} | custom-call | flops 7000000000 | tf_op jit(solution)/shard_map/prompt_chain/pallas_call | solution.py:317
  109.9 1.3 collective-permute-start.19
  111.2 4.7 %all-to-all-start.2 = ((bf16[16,256,128]{2,1,0:T(8,128)(2,1)}), bf16[16,256,128]{2,1,0:T(8,128)(2,1)S(1)}, u32[]{:S(2)}, u32[]{:S(2)}) async-start(bf16[16,256,128]{2,1,0:T(8,128)(2,1)} %get-tuple-element.83), calls=%async_computation.2 | async-start | bytes 2097152 | tf_op jit(solution)/shard_map/all_to_all | solution.py:545
  115.9 3.2 %collective-permute-done.19.g_in = bf16[192,128]{1,0:T(8,128)(2,1)S(1)} collective-permute-done((bf16[192,128]{1,0:T(8,128)(2,1)S(1)}, bf16[192,128]{1,0:T(8,128)(2,1)S(1)}, u32[]{:S(2)}, u32[]{:S(2)}) %collective-permute-start.19) | collective-permute-done | bytes 49184 | tf_op jit(solution)/shard_map/ppermute | solution.py:561
  119.1 8.2 %response_chain.7 = (bf16[192,128]{1,0:T(8,128)(2,1)}, bf16[16,192,128]{2,1,0:T(8,128)(2,1)}) custom-call(s32[1]{0:T(128)} %bitcast.5.active, bf16[192,128]{1,0:T(8,128)(2,1)S(1)} %collective-permute-done.19.g_in, bf16[16,192,128]{2,1,0:T(8,128)(2,1)} %get-tuple-element.87.stash_in, ...), custom_call_target="tpu_custom_call", output_to_operand_aliasing={{1}: (2, {})} | custom-call | flops 7000000000 | tf_op jit(solution)/shard_map/response_chain/pallas_call | solution.py:317
  127.3 0.6 own_prompt_prob.3.probs
  127.9 6.6 %all-to-all-start.3 = ((bf16[16,192,128]{2,1,0:T(8,128)(2,1)}), bf16[16,192,128]{2,1,0:T(8,128)(2,1)S(1)}, u32[]{:S(2)}, u32[]{:S(2)}) async-start(bf16[16,192,128]{2,1,0:T(8,128)(2,1)} %get-tuple-element.92), calls=%async_computation.3 | async-start | bytes 1572864 | tf_op jit(solution)/shard_map/all_to_all | solution.py:545
  134.5 6.0 %prompt_grad.1.part_ref = f32[256,256]{1,0:T(8,128)S(1)} custom-call(f32[16,256,256]{2,1,0:T(8,128)} %own_prompt_prob.3.probs, bf16[16,256,128]{2,1,0:T(8,128)(2,1)} %get-tuple-element.89.q_ref, bf16[16,256,128]{2,1,0:T(8,128)(2,1)S(1)} %all-to-all-done.2.g_ref, bf16[448,128]{1,0:T(8,128)(2,1)S(1)} %slice_bitcast_fusion.v_ref), custom_call_target="tpu_custom_call" | custom-call | flops 5000000000 | tf_op jit(solution)/shard_map/prompt_grad/pallas_call | solution.py:429
  140.5 0.6 own_response_prob.3.probs
  141.1 3.8 %all-to-all-done.3.g_ref = bf16[16,192,128]{2,1,0:T(8,128)(2,1)S(1)} async-done(((bf16[16,192,128]{2,1,0:T(8,128)(2,1)}), bf16[16,192,128]{2,1,0:T(8,128)(2,1)S(1)}, u32[]{:S(2)}, u32[]{:S(2)}) %all-to-all-start.3) | async-done | bytes 786464 | tf_op jit(solution)/shard_map/all_to_all | solution.py:545
  144.9 6.5 %response_grad.1 = (f32[512,256]{1,0:T(8,128)S(1)}, f32[1,128]{1,0:T(1,128)S(1)}) custom-call(s32[4]{0:T(128)S(1)} %copy-done.2, f32[4,448,768]{2,1,0:T(8,128)} %own_response_prob.3.probs, bf16[16,192,128]{2,1,0:T(8,128)(2,1)} %get-tuple-element.91.q_ref, bf16[16,192,128]{2,1,0:T(8,128)(2,1)S(1)} %all-to-all-done.3.g_ref, ...), custom_call_target="tpu_custom_call" | custom-call | flops 8000000000 | tf_op jit(solution)/shard_map/response_grad/pallas_call | solution.py:491
  151.4 17.8 %all_to_all.32 = f32[32,1,128]{2,1,0:T(1,128)S(1)} all-to-all(f32[32,1,128]{2,1,0:T(1,128)S(1)} %broadcast_in_dim.26), channel_id=1, replica_groups=mesh['zl'=4,'x'=4,'y'=4,'zh'=2,'core'=2] {'x','y','core'}, dimensions={0} | all-to-all | bytes 32768 | tf_op jit(solution)/shard_map/all_to_all | solution.py:589
  169.2 16.0 %all_to_all.33 = f32[8,1,128]{2,1,0:T(1,128)S(1)} all-to-all(f32[8,1,128]{2,1,0:T(1,128)S(1)} %broadcast_in_dim.27), channel_id=1, replica_groups=mesh['zl'=4,'x'=4,'y'=4,'zh'=2,'core'=2] {'zl','zh'}, dimensions={0} | all-to-all | bytes 8192 | tf_op jit(solution)/shard_map/all_to_all | solution.py:589
  185.2 0.6 reduce_sum.20
  186.5 0.8 multiply_bitcast_fusion
  (42 shorter events, 1.4 us)
Async XLA Ops:
  0.0 8.8 %collective-permute-start.2 = (bf16[512,128]{1,0:T(8,128)(2,1)}, bf16[512,128]{1,0:T(8,128)(2,1)S(1)}, u32[]{:S(2)}, u32[]{:S(2)}) collective-permute-start(bf16[512,128]{1,0:T(8,128)(2,1)} %bitcast.19), channel_id=1, source_target_pairs={{0,8},{4,12},{8,0},{12,4},{1,9},{5,13},{9,1},{13,5},{2,10},{6,14},... | collective-permute-start | bytes 393224 | tf_op jit(solution)/shard_map/ppermute | solution.py:518
  3.7 9.5 %collective-permute-start.1 = (bf16[512,128]{1,0:T(8,128)(2,1)}, bf16[512,128]{1,0:T(8,128)(2,1)S(1)}, u32[]{:S(2)}, u32[]{:S(2)}) collective-permute-start(bf16[512,128]{1,0:T(8,128)(2,1)} %bitcast.20), channel_id=1, source_target_pairs={{0,12},{4,0},{8,4},{12,8},{1,13},{5,1},{9,5},{13,9},{2,14},{6,2},{... | collective-permute-start | bytes 393224 | tf_op jit(solution)/shard_map/ppermute | solution.py:518
  4.5 8.7 %collective-permute-start = (bf16[512,128]{1,0:T(8,128)(2,1)}, bf16[512,128]{1,0:T(8,128)(2,1)S(1)}, u32[]{:S(2)}, u32[]{:S(2)}) collective-permute-start(bf16[512,128]{1,0:T(8,128)(2,1)} %bitcast.21), channel_id=1, source_target_pairs={{0,4},{4,8},{8,12},{12,0},{1,5},{5,9},{9,13},{13,1},{2,6},{6,10},{... | collective-permute-start | bytes 393224 | tf_op jit(solution)/shard_map/ppermute | solution.py:518
  5.2 8.0 %collective-permute-start.5 = (bf16[512,128]{1,0:T(8,128)(2,1)}, bf16[512,128]{1,0:T(8,128)(2,1)S(1)}, u32[]{:S(2)}, u32[]{:S(2)}) collective-permute-start(bf16[512,128]{1,0:T(8,128)(2,1)} %bitcast.23), channel_id=1, source_target_pairs={{0,32},{16,48},{32,0},{48,16},{1,33},{17,49},{33,1},{49,17},{2,34}... | collective-permute-start | bytes 393224 | tf_op jit(solution)/shard_map/ppermute | solution.py:518
  8.0 5.3 %collective-permute-start.4 = (bf16[512,128]{1,0:T(8,128)(2,1)}, bf16[512,128]{1,0:T(8,128)(2,1)S(1)}, u32[]{:S(2)}, u32[]{:S(2)}) collective-permute-start(bf16[512,128]{1,0:T(8,128)(2,1)} %bitcast.24), channel_id=1, source_target_pairs={{0,48},{16,0},{32,16},{48,32},{1,49},{17,1},{33,17},{49,33},{2,50}... | collective-permute-start | bytes 393224 | tf_op jit(solution)/shard_map/ppermute | solution.py:518
  8.8 5.8 %collective-permute-start.3 = (bf16[512,128]{1,0:T(8,128)(2,1)}, bf16[512,128]{1,0:T(8,128)(2,1)S(1)}, u32[]{:S(2)}, u32[]{:S(2)}) collective-permute-start(bf16[512,128]{1,0:T(8,128)(2,1)} %bitcast.25), channel_id=1, source_target_pairs={{0,16},{16,32},{32,48},{48,0},{1,17},{17,33},{33,49},{49,1},{2,18}... | collective-permute-start | bytes 393224 | tf_op jit(solution)/shard_map/ppermute | solution.py:518
  9.4 5.2 %copy-start = (bf16[1,512,128]{2,1,0:T(8,128)(2,1)S(1)}, bf16[1,512,128]{2,1,0:T(8,128)(2,1)}, u32[]{:S(2)}) copy-start(bf16[1,512,128]{2,1,0:T(8,128)(2,1)} %param.6) | copy-start | bytes 393220
  9.4 5.2 %copy-start.1 = (bf16[1,512,128]{2,1,0:T(8,128)(2,1)S(1)}, bf16[1,512,128]{2,1,0:T(8,128)(2,1)}, u32[]{:S(2)}) copy-start(bf16[1,512,128]{2,1,0:T(8,128)(2,1)} %param.7) | copy-start | bytes 393220
  9.4 5.2 %copy-start.2 = (s32[4]{0:T(128)S(1)}, s32[4]{0:T(128)}, u32[]{:S(2)}) copy-start(s32[4]{0:T(128)} %lens.17) | copy-start | bytes 52
  15.6 34.3 %all-to-all-start = ((bf16[16,256,128]{2,1,0:T(8,128)(2,1)}), bf16[16,256,128]{2,1,0:T(8,128)(2,1)}, u32[]{:S(2)}, u32[]{:S(2)}) async-start(bf16[16,256,128]{2,1,0:T(8,128)(2,1)} %get-tuple-element.89.q_ref), calls=%async_computation | async-start | bytes 2097152 | tf_op jit(solution)/shard_map/all_to_all | solution.py:545
  20.6 21.2 %collective-permute-start.7 = (bf16[4,448,128]{2,1,0:T(8,128)(2,1)S(1)}, bf16[4,448,128]{2,1,0:T(8,128)(2,1)S(1)}, u32[]{:S(2)}, u32[]{:S(2)}) collective-permute-start(bf16[4,448,128]{2,1,0:T(8,128)(2,1)S(1)} %get-tuple-element.57.refs_0_), channel_id=1, source_target_pairs={{0,48},{16,0},{32,16},{48,32},{1,49},{17,1},{33,17},{49,33},{2,50}... | collective-permute-start | bytes 1376264 | tf_op jit(solution)/shard_map/ppermute | solution.py:522
  23.1 21.9 %collective-permute-start.6 = (bf16[4,448,128]{2,1,0:T(8,128)(2,1)S(1)}, bf16[4,448,128]{2,1,0:T(8,128)(2,1)S(1)}, u32[]{:S(2)}, u32[]{:S(2)}) collective-permute-start(bf16[4,448,128]{2,1,0:T(8,128)(2,1)S(1)} %get-tuple-element.57.refs_0_), channel_id=1, source_target_pairs={{0,16},{16,32},{32,48},{48,0},{1,17},{17,33},{33,49},{49,1},{2,18}... | collective-permute-start | bytes 1376264 | tf_op jit(solution)/shard_map/ppermute | solution.py:522
  23.1 22.6 %collective-permute-start.11 = (bf16[4,448,128]{2,1,0:T(8,128)(2,1)S(1)}, bf16[4,448,128]{2,1,0:T(8,128)(2,1)S(1)}, u32[]{:S(2)}, u32[]{:S(2)}) collective-permute-start(bf16[4,448,128]{2,1,0:T(8,128)(2,1)S(1)} %get-tuple-element.58.refs_5_), channel_id=1, source_target_pairs={{0,12},{4,0},{8,4},{12,8},{1,13},{5,1},{9,5},{13,9},{2,14},{6,2},{... | collective-permute-start | bytes 1376264 | tf_op jit(solution)/shard_map/ppermute | solution.py:522
  25.5 23.6 %collective-permute-start.10 = (bf16[4,448,128]{2,1,0:T(8,128)(2,1)S(1)}, bf16[4,448,128]{2,1,0:T(8,128)(2,1)S(1)}, u32[]{:S(2)}, u32[]{:S(2)}) collective-permute-start(bf16[4,448,128]{2,1,0:T(8,128)(2,1)S(1)} %get-tuple-element.58.refs_5_), channel_id=1, source_target_pairs={{0,4},{4,8},{8,12},{12,0},{1,5},{5,9},{9,13},{13,1},{2,6},{6,10},{... | collective-permute-start | bytes 1376264 | tf_op jit(solution)/shard_map/ppermute | solution.py:522
  42.5 13.9 %collective-permute-start.9 = (bf16[2,448,128]{2,1,0:T(8,128)(2,1)}, bf16[2,448,128]{2,1,0:T(8,128)(2,1)S(1)}, u32[]{:S(2)}, u32[]{:S(2)}) collective-permute-start(bf16[2,448,128]{2,1,0:T(8,128)(2,1)} %slice.25), channel_id=1, source_target_pairs={{0,48},{16,0},{32,16},{48,32},{1,49},{17,1},{33,17},{49,33},{2,50}... | collective-permute-start | bytes 688136 | tf_op jit(solution)/shard_map/ppermute | solution.py:529
  45.7 10.6 %collective-permute-start.8 = (bf16[2,448,128]{2,1,0:T(8,128)(2,1)}, bf16[2,448,128]{2,1,0:T(8,128)(2,1)S(1)}, u32[]{:S(2)}, u32[]{:S(2)}) collective-permute-start(bf16[2,448,128]{2,1,0:T(8,128)(2,1)} %slice.24), channel_id=1, source_target_pairs={{0,16},{16,32},{32,48},{48,0},{1,17},{17,33},{33,49},{49,1},{2,18}... | collective-permute-start | bytes 688136 | tf_op jit(solution)/shard_map/ppermute | solution.py:528
  46.5 9.9 %collective-permute-start.13 = (bf16[2,448,128]{2,1,0:T(8,128)(2,1)}, bf16[2,448,128]{2,1,0:T(8,128)(2,1)}, u32[]{:S(2)}, u32[]{:S(2)}) collective-permute-start(bf16[2,448,128]{2,1,0:T(8,128)(2,1)} %slice.27), channel_id=1, source_target_pairs={{0,12},{4,0},{8,4},{12,8},{1,13},{5,1},{9,5},{13,9},{2,14},{6,2},{... | collective-permute-start | bytes 688136 | tf_op jit(solution)/shard_map/ppermute | solution.py:529
  49.8 6.6 %collective-permute-start.12 = (bf16[2,448,128]{2,1,0:T(8,128)(2,1)}, bf16[2,448,128]{2,1,0:T(8,128)(2,1)}, u32[]{:S(2)}, u32[]{:S(2)}) collective-permute-start(bf16[2,448,128]{2,1,0:T(8,128)(2,1)} %slice.26), channel_id=1, source_target_pairs={{0,4},{4,8},{8,12},{12,0},{1,5},{5,9},{9,13},{13,1},{2,6},{6,10},{... | collective-permute-start | bytes 688136 | tf_op jit(solution)/shard_map/ppermute | solution.py:528
  49.8 17.3 %all-to-all-start.1 = ((bf16[16,192,128]{2,1,0:T(8,128)(2,1)}), bf16[16,192,128]{2,1,0:T(8,128)(2,1)}, u32[]{:S(2)}, u32[]{:S(2)}) async-start(bf16[16,192,128]{2,1,0:T(8,128)(2,1)} %get-tuple-element.91.q_ref), calls=%async_computation.1 | async-start | bytes 1572864 | tf_op jit(solution)/shard_map/all_to_all | solution.py:545
  56.4 7.1 %copy-start.3 = (bf16[256,128]{1,0:T(8,128)(2,1)S(1)}, bf16[256,128]{1,0:T(8,128)(2,1)}, u32[]{:S(2)}) copy-start(bf16[256,128]{1,0:T(8,128)(2,1)} %get-tuple-element.56.g_in) | copy-start | bytes 196612
  63.8 13.5 %collective-permute-start.15 = (bf16[256,128]{1,0:T(8,128)(2,1)S(1)}, bf16[256,128]{1,0:T(8,128)(2,1)S(1)}, u32[]{:S(2)}, u32[]{:S(2)}) collective-permute-start(bf16[256,128]{1,0:T(8,128)(2,1)S(1)} %get-tuple-element.62), channel_id=1, source_target_pairs={{192,128},{193,129},{194,130},{195,131},{196,132},{197,133},{198,1... | collective-permute-start | bytes 196616 | tf_op jit(solution)/shard_map/ppermute | solution.py:561
  67.1 9.2 %copy-start.4 = (bf16[192,128]{1,0:T(8,128)(2,1)S(1)}, bf16[192,128]{1,0:T(8,128)(2,1)}, u32[]{:S(2)}) copy-start(bf16[192,128]{1,0:T(8,128)(2,1)} %get-tuple-element.63.g_in) | copy-start | bytes 147460
  76.6 12.1 %collective-permute-start.14 = (bf16[192,128]{1,0:T(8,128)(2,1)S(1)}, bf16[192,128]{1,0:T(8,128)(2,1)S(1)}, u32[]{:S(2)}, u32[]{:S(2)}) collective-permute-start(bf16[192,128]{1,0:T(8,128)(2,1)S(1)} %get-tuple-element.68), channel_id=1, source_target_pairs={{192,128},{193,129},{194,130},{195,131},{196,132},{197,133},{198,1... | collective-permute-start | bytes 147464 | tf_op jit(solution)/shard_map/ppermute | solution.py:561
  77.6 11.1 %collective-permute-start.16 = (bf16[256,128]{1,0:T(8,128)(2,1)S(1)}, bf16[256,128]{1,0:T(8,128)(2,1)S(1)}, u32[]{:S(2)}, u32[]{:S(2)}) collective-permute-start(bf16[256,128]{1,0:T(8,128)(2,1)S(1)} %get-tuple-element.71), channel_id=1, source_target_pairs={{128,64},{129,65},{130,66},{131,67},{132,68},{133,69},{134,70},{13... | collective-permute-start | bytes 196616 | tf_op jit(solution)/shard_map/ppermute | solution.py:561
  89.5 12.2 %collective-permute-start.18 = (bf16[256,128]{1,0:T(8,128)(2,1)S(1)}, bf16[256,128]{1,0:T(8,128)(2,1)S(1)}, u32[]{:S(2)}, u32[]{:S(2)}) collective-permute-start(bf16[256,128]{1,0:T(8,128)(2,1)S(1)} %get-tuple-element.80), channel_id=1, source_target_pairs={{64,0},{65,1},{66,2},{67,3},{68,4},{69,5},{70,6},{71,7},{72,8},{73... | collective-permute-start | bytes 196616 | tf_op jit(solution)/shard_map/ppermute | solution.py:561
  90.8 0.7 collective-permute-start.17
  109.9 9.2 %collective-permute-start.19 = (bf16[192,128]{1,0:T(8,128)(2,1)S(1)}, bf16[192,128]{1,0:T(8,128)(2,1)S(1)}, u32[]{:S(2)}, u32[]{:S(2)}) collective-permute-start(bf16[192,128]{1,0:T(8,128)(2,1)S(1)} %get-tuple-element.86), channel_id=1, source_target_pairs={{64,0},{65,1},{66,2},{67,3},{68,4},{69,5},{70,6},{71,7},{72,8},{73... | collective-permute-start | bytes 147464 | tf_op jit(solution)/shard_map/ppermute | solution.py:561
  111.2 16.7 %all-to-all-start.2 = ((bf16[16,256,128]{2,1,0:T(8,128)(2,1)}), bf16[16,256,128]{2,1,0:T(8,128)(2,1)S(1)}, u32[]{:S(2)}, u32[]{:S(2)}) async-start(bf16[16,256,128]{2,1,0:T(8,128)(2,1)} %get-tuple-element.83), calls=%async_computation.2 | async-start | bytes 2097152 | tf_op jit(solution)/shard_map/all_to_all | solution.py:545
  127.9 17.0 %all-to-all-start.3 = ((bf16[16,192,128]{2,1,0:T(8,128)(2,1)}), bf16[16,192,128]{2,1,0:T(8,128)(2,1)S(1)}, u32[]{:S(2)}, u32[]{:S(2)}) async-start(bf16[16,192,128]{2,1,0:T(8,128)(2,1)} %get-tuple-element.92), calls=%async_computation.3 | async-start | bytes 1572864 | tf_op jit(solution)/shard_map/all_to_all | solution.py:545
